TPU v7x, 32 devices: a whole 2x2x4 slice. The times are simulated.
32 devices in a mesh: seq: 8 (over y, x, core), head: 4 (over z).
Axes of the slice: x: 2, y: 2, z: 4, core: 2. Of those that a mesh axis runs over, the one named last changes fastest.
Arguments:
- residual_in: bfloat16 [4, 4096, 1536], P(None, 'seq'), may hold values from -6 to 6
- lengths: int32 [4], replicated, may hold values from 1024 to 4096, as said below
- norm_gain: float32 [1536], replicated, may hold values from 0.5 to 1.5
- gate_projection_weight: bfloat16 [1536, 3072], P(None, 'head'), may hold values from -0.15625 to 0.15625
- head_channels_weight: bfloat16 [1536, 3072], P(None, 'head'), may hold values from -0.15625 to 0.15625
- input_state_pair_weight: bfloat16 [1536, 256], P(None, 'head'), may hold values from -0.15625 to 0.15625
- step_size_weight: bfloat16 [1536, 48], P(None, 'head'), may hold values from -0.15625 to 0.15625
- x_taps: float32 [4, 3072], P(None, 'head'), may hold values from -2.5 to 2.5
- bc_taps: float32 [4, 256], P(None, 'head'), may hold values from -2.5 to 2.5
- x_bias: float32 [3072], P('head'), may hold values from -1.5 to 1.5
- bc_bias: float32 [256], P('head'), may hold values from -1.5 to 1.5
- step_bias: float32 [48], P('head'), may hold values from -4 to -2
- decay_log: float32 [48], P('head'), may hold values from -6 to -1
- skip_gain: float32 [48], P('head'), may hold values from 0.5 to 1.5
- out_gain: float32 [3072], P('head'), may hold values from 0.5 to 1.5
- output_projection_weight: bfloat16 [3072, 1536], P('head'), may hold values from -0.109375 to 0.109375
- cotangent: bfloat16 [4, 4096, 1536], P(None, 'seq'), may hold values from -6 to 6
Outputs:
- result: bfloat16 [4, 4096, 1536], P(None, 'seq')
- grad_input: float32 [4, 4096, 1536], P(None, 'seq')
- grad_norm_gain: float32 [1536], replicated
- grad_z_weight: float32 [1536, 3072], P(None, 'head')
- grad_x_weight: float32 [1536, 3072], P(None, 'head')
- grad_bc_weight: float32 [1536, 256], P(None, 'head')
- grad_step_weight: float32 [1536, 48], P(None, 'head')
- grad_x_taps: float32 [4, 3072], P(None, 'head')
- grad_bc_taps: float32 [4, 256], P(None, 'head')
- grad_x_bias: float32 [3072], P('head')
- grad_bc_bias: float32 [256], P('head')
- grad_step_bias: float32 [48], P('head')
- grad_decay_log: float32 [48], P('head')
- grad_skip_gain: float32 [48], P('head')
- grad_out_gain: float32 [3072], P('head')
- grad_out_weight: float32 [3072, 1536], P('head')
Inputs may be any that keep to these rules, and one draw needn't show every extreme that they name: `lengths`: one sequence, drawn from the seed, has all 4096 slots valid and another has 1024; the valid slots of a sequence are its first ones.
All inputs are finite; a program needn't handle non-finite values.
Results may differ from a plain program's by a relative error of at most 0.00145.
The roundings to bfloat16 on the way count: a program that leaves them out, or rounds other values in their place, can miss the bound.
Values may be sent and summed in bfloat16 or wider, within the bound.
No kernel may reach another device: no remote copies, remote signals or barrier semaphores. Data moves between devices by JAX's collectives and lax.ppermute only.
A program may use at most 448 MiB of HBM per device.

v0:
```python
import jax
import jax.numpy as jnp
from jax import lax
from jax.sharding import PartitionSpec as P

HEAD_DIM = 64
STATE = 128
CONV = 4
GROUP = 256
INNER = 3072


EPSILON = 1e-05
MATMUL_ACCURACY = lax.Precision.HIGHEST


def shifted(block, axis, distance):
    devices = range(lax.axis_size(axis))
    route = [(i - distance, i) for i in devices if i - distance in devices]
    return lax.ppermute(block, axis, route)


def carried_in(value, axis, join, neutral, backward):
    count, mine = (lax.axis_size(axis), lax.axis_index(axis))
    pieces = jax.tree.map(lambda part: lax.all_gather(part, axis), value)
    if backward:
        pieces = jax.tree.map(lambda part: part[::-1], pieces)
        mine = count - 1 - mine
    subtotal = jax.tree.map(
        lambda part, zero: jnp.full_like(part, 0) + jnp.asarray(zero, part.dtype), value, neutral
    )

    def hop(position, subtotal):
        longer = join(subtotal, jax.tree.map(lambda part: part[position], pieces))
        return jax.tree.map(lambda new, old: jnp.where(position < mine, new, old), longer, subtotal)

    return lax.fori_loop(0, count - 1, hop, subtotal)


def convolve(extended, taps, offset_bias, length):
    summed = offset_bias + taps[0] * extended[:, 0:length]
    for tap_index in range(1, taps.shape[0]):
        summed = summed + taps[tap_index] * extended[:, tap_index : tap_index + length]
    return summed


def block_math(block_x, block_b, block_c, block_step, block_rate, state_in):
    cumulative = jnp.cumsum(block_rate, axis=-1)
    length = block_rate.shape[-1]
    lower_mask = lax.iota(jnp.int32, length)[:, None] >= lax.iota(jnp.int32, length)[None, :]
    gap_matrix = cumulative[..., :, None] - cumulative[..., None, :]
    kernel = jnp.where(lower_mask, jnp.exp(jnp.where(lower_mask, gap_matrix, 0.0)), 0.0)
    intersection_scores = jnp.einsum("sln,smn->slm", block_c, block_b, precision=MATMUL_ACCURACY)
    mixing = kernel * intersection_scores[:, None] * block_step[..., None, :]
    carried = jnp.einsum("sln,shpn->shlp", block_c, state_in, precision=MATMUL_ACCURACY)
    output = (
        jnp.einsum("shlm,shmp->shlp", mixing, block_x, precision=MATMUL_ACCURACY)
        + jnp.exp(cumulative)[..., None] * carried
    )
    ending = cumulative[..., -1:]
    weighted = (jnp.exp(ending - cumulative) * block_step)[..., None] * block_x
    updated = jnp.exp(ending)[..., None] * state_in + jnp.einsum(
        "shlp,sln->shpn", weighted, block_b, precision=MATMUL_ACCURACY
    )
    return (output, updated, cumulative)


def ssd_piece(x_ext, x_taps, x_bias, step_size_raw, step_bias, decay_log, skip_gain, bc_full):
    seq_count, extended_len, inner_dev = x_ext.shape
    slot_dev = extended_len - (CONV - 1)
    heads_dev = step_size_raw.shape[-1]
    blocks = slot_dev // GROUP
    xs = jax.nn.silu(convolve(x_ext, x_taps, x_bias, slot_dev))
    step = jax.nn.softplus(step_size_raw + step_bias)
    rate = -step * jnp.exp(decay_log)
    heads_view = xs.reshape(seq_count, slot_dev, heads_dev, HEAD_DIM)
    xs_blocks = heads_view.reshape(seq_count, blocks, GROUP, heads_dev, HEAD_DIM).transpose(
        1, 0, 3, 2, 4
    )
    b_blocks = bc_full[..., :STATE].reshape(seq_count, blocks, GROUP, STATE).transpose(1, 0, 2, 3)
    c_blocks = bc_full[..., STATE:].reshape(seq_count, blocks, GROUP, STATE).transpose(1, 0, 2, 3)
    step_blocks = step.reshape(seq_count, blocks, GROUP, heads_dev).transpose(1, 0, 3, 2)
    rate_blocks = rate.reshape(seq_count, blocks, GROUP, heads_dev).transpose(1, 0, 3, 2)

    def advance(carry, pieces):
        state_in, offset = carry
        output, updated, cumulative = block_math(
            pieces[0], pieces[1], pieces[2], pieces[3], pieces[4], state_in
        )
        return ((updated, offset + cumulative[..., -1]), (output, offset[..., None] + cumulative))

    start_state = (
        jnp.zeros((seq_count, heads_dev, HEAD_DIM, STATE), jnp.float32),
        jnp.zeros((seq_count, heads_dev), jnp.float32),
    )
    carry_out, stacked = lax.scan(
        advance, start_state, (xs_blocks, b_blocks, c_blocks, step_blocks, rate_blocks)
    )
    mixed = stacked[0].transpose(1, 0, 3, 2, 4).reshape(seq_count, slot_dev, inner_dev)
    mixed = mixed + (heads_view * skip_gain[:, None]).reshape(seq_count, slot_dev, inner_dev)
    cumulated = stacked[1].transpose(1, 2, 0, 3).reshape(seq_count, heads_dev, slot_dev)
    return (mixed, carry_out[0], cumulated)


def combine_states(earlier, later_part):
    return (earlier[0] * later_part[0], later_part[0][..., None, None] * earlier[1] + later_part[1])


def per_device(
    residual_in,
    lengths,
    norm_gain,
    gate_projection_weight,
    head_channels_weight,
    input_state_pair_weight,
    step_size_weight,
    x_taps,
    bc_taps,
    x_bias,
    bc_bias,
    step_bias,
    decay_log,
    skip_gain,
    out_gain,
    output_projection_weight,
    cotangent,
):
    seq_count, slot_dev, width = residual_in.shape
    inner_dev = head_channels_weight.shape[1]
    bc_dev = input_state_pair_weight.shape[1]
    heads_dev = step_size_weight.shape[1]
    margin = CONV - 1
    cut_x = 2 * inner_dev
    cut_bc = cut_x + bc_dev
    positions = lax.axis_index("seq") * slot_dev + lax.iota(jnp.int32, slot_dev)
    valid_mask = (positions[None, :] < lengths[:, None]).astype(jnp.float32)
    inputs = residual_in.astype(jnp.float32)
    scale_in = lax.rsqrt(jnp.mean(inputs * inputs, axis=-1, keepdims=True) + EPSILON)
    normalized_rows = (inputs * scale_in * norm_gain).astype(jnp.bfloat16)
    input_projection_weight = jnp.concatenate(
        [gate_projection_weight, head_channels_weight, input_state_pair_weight, step_size_weight],
        axis=1,
    )
    projected_rows = jnp.einsum(
        "aym,mq->ayq", normalized_rows, input_projection_weight, preferred_element_type=jnp.float32
    )
    gate_before_activation = projected_rows[..., :inner_dev]
    head_channels_raw = projected_rows[..., inner_dev:cut_x]
    input_state_pair_raw = projected_rows[..., cut_x:cut_bc]
    step_size_raw = projected_rows[..., cut_bc:]
    tail_rows = jnp.concatenate(
        [head_channels_raw[:, slot_dev - margin :], input_state_pair_raw[:, slot_dev - margin :]],
        axis=-1,
    )
    received = shifted(tail_rows, "seq", 1)
    x_ext = jnp.concatenate([received[..., :inner_dev], head_channels_raw], axis=1)
    bc_ext = jnp.concatenate([received[..., inner_dev:], input_state_pair_raw], axis=1)

    def bc_piece(extended, taps, offset_bias):
        return jax.nn.silu(convolve(extended, taps, offset_bias, slot_dev))

    bc_own, bc_back = jax.vjp(bc_piece, bc_ext, bc_taps, bc_bias)
    bc_full = lax.all_gather(bc_own, "head", axis=2, tiled=True)
    c_full = bc_full[..., STATE:]
    pieces, ssd_back = jax.vjp(
        ssd_piece, x_ext, x_taps, x_bias, step_size_raw, step_bias, decay_log, skip_gain, bc_full
    )
    local_mixed, end_state, cumulated = pieces
    totals = jnp.exp(cumulated[..., -1])
    identity = (jnp.ones_like(totals), jnp.zeros_like(end_state))
    before_scan = carried_in((totals, end_state), "seq", combine_states, identity, False)
    state_in = before_scan[1]
    exp_cumul = jnp.exp(cumulated).transpose(0, 2, 1)
    inter_part = (
        jnp.einsum("sln,shpn->slhp", c_full, state_in, precision=MATMUL_ACCURACY)
        * exp_cumul[..., None]
    )
    mixed = local_mixed + inter_part.reshape(seq_count, slot_dev, inner_dev)
    sig_gate = jax.nn.sigmoid(gate_before_activation)
    gated = mixed * jax.nn.silu(gate_before_activation)
    squares = lax.psum(jnp.sum(gated * gated, axis=-1), "head")
    gate_scale = lax.rsqrt(squares / INNER + EPSILON)[..., None]
    hidden_rows = (gated * gate_scale * out_gain).astype(jnp.bfloat16)
    residual_branch = lax.psum(
        jnp.einsum(
            "kmq,qh->kmh", hidden_rows, output_projection_weight, preferred_element_type=jnp.float32
        ),
        "head",
    )
    result = ((inputs + residual_branch) * valid_mask[..., None]).astype(jnp.bfloat16)
    grad_branch = cotangent.astype(jnp.float32) * valid_mask[..., None]
    branch_reduced_precision = grad_branch.astype(jnp.bfloat16)
    grad_out_weight = jnp.einsum(
        "yfx,yfw->xw", hidden_rows, branch_reduced_precision, preferred_element_type=jnp.float32
    )
    grad_hidden = jnp.einsum(
        "tge,ve->tgv",
        branch_reduced_precision,
        output_projection_weight,
        preferred_element_type=jnp.float32,
    )
    grad_out_gain = jnp.sum(grad_hidden * gated * gate_scale, axis=(0, 1))
    weighted = grad_hidden * out_gain
    gate_dots = lax.psum(jnp.sum(gated * weighted, axis=-1), "head")
    grad_gated = gate_scale * weighted - gated * (gate_scale**3 * gate_dots[..., None] / INNER)
    grad_mixed = grad_gated * jax.nn.silu(gate_before_activation)
    grad_gate_pre = (
        grad_gated * mixed * sig_gate * (1.0 + gate_before_activation * (1.0 - sig_gate))
    )
    grad_heads = grad_mixed.reshape(seq_count, slot_dev, heads_dev, HEAD_DIM)
    weighted_grad = grad_heads * exp_cumul[..., None]
    grad_state_in = jnp.einsum("slhp,sln->shpn", weighted_grad, c_full, precision=MATMUL_ACCURACY)
    grad_c_inter = jnp.einsum("slhp,shpn->sln", weighted_grad, state_in, precision=MATMUL_ACCURACY)
    grad_cumul = jnp.sum(grad_heads * inter_part, axis=-1).transpose(0, 2, 1)
    after_scan = carried_in((totals, grad_state_in), "seq", combine_states, identity, True)
    later_grad = after_scan[1]
    through_end = totals * jnp.sum(later_grad * state_in, axis=(-2, -1))
    grad_cumul = grad_cumul + jnp.pad(through_end[..., None], ((0, 0), (0, 0), (slot_dev - 1, 0)))
    grads_ssd = ssd_back((grad_mixed, later_grad, grad_cumul))
    grad_bc_full = grads_ssd[7] + jnp.concatenate(
        [jnp.zeros_like(grad_c_inter), grad_c_inter], axis=-1
    )
    grad_bc_own = lax.psum_scatter(grad_bc_full, "head", scatter_dimension=2, tiled=True)
    grad_bc_ext, grad_bc_taps, grad_bc_bias = bc_back(grad_bc_own)
    grad_x_ext = grads_ssd[0]
    edge_grad = jnp.concatenate([grad_x_ext[:, :margin], grad_bc_ext[:, :margin]], axis=-1)
    returned = shifted(edge_grad, "seq", -1)
    returned = jnp.pad(returned, ((0, 0), (slot_dev - margin, 0), (0, 0)))
    projection_gradient = jnp.concatenate(
        [
            grad_gate_pre,
            grad_x_ext[:, margin:] + returned[..., :inner_dev],
            grad_bc_ext[:, margin:] + returned[..., inner_dev:],
            grads_ssd[3],
        ],
        axis=-1,
    ).astype(jnp.bfloat16)
    grad_in_weight = jnp.einsum(
        "wji,wjr->ir", normalized_rows, projection_gradient, preferred_element_type=jnp.float32
    )
    grad_normed = lax.psum(
        jnp.einsum(
            "sgl,ol->sgo",
            projection_gradient,
            input_projection_weight,
            preferred_element_type=jnp.float32,
        ),
        "head",
    )
    grad_norm_gain = jnp.sum(grad_normed * inputs * scale_in, axis=(0, 1))
    weighted_in = grad_normed * norm_gain
    grad_input = (
        scale_in * weighted_in
        - inputs * scale_in**3 * jnp.mean(weighted_in * inputs, axis=-1, keepdims=True)
        + grad_branch
    )
    summed = lax.psum(
        (
            grad_norm_gain,
            grad_in_weight[:, :inner_dev],
            grad_in_weight[:, inner_dev:cut_x],
            grad_in_weight[:, cut_x:cut_bc],
            grad_in_weight[:, cut_bc:],
            grads_ssd[1],
            grad_bc_taps,
            grads_ssd[2],
            grad_bc_bias,
            grads_ssd[4],
            grads_ssd[5],
            grads_ssd[6],
            grad_out_gain,
            grad_out_weight,
        ),
        "seq",
    )
    return (
        result,
        grad_input,
        summed[0],
        summed[1],
        summed[2],
        summed[3],
        summed[4],
        summed[5],
        summed[6],
        summed[7],
        summed[8],
        summed[9],
        summed[10],
        summed[11],
        summed[12],
        summed[13],
    )


def solution(mesh):
    return jax.shard_map(
        per_device,
        mesh=mesh,
        in_specs=(
            P(None, "seq", None),
            P(),
            P(),
            P(None, "head"),
            P(None, "head"),
            P(None, "head"),
            P(None, "head"),
            P(None, "head"),
            P(None, "head"),
            P("head"),
            P("head"),
            P("head"),
            P("head"),
            P("head"),
            P("head"),
            P("head", None),
            P(None, "seq", None),
        ),
        out_specs=(
            P(None, "seq", None),
            P(None, "seq", None),
            P(),
            P(None, "head"),
            P(None, "head"),
            P(None, "head"),
            P(None, "head"),
            P(None, "head"),
            P(None, "head"),
            P("head"),
            P("head"),
            P("head"),
            P("head"),
            P("head"),
            P("head"),
            P("head", None),
        ),
        check_vma=False,
    )
```

profile of v0, /device:TPU:0, one launch (start us, length us, event | category | flops | bytes accessed | tf_op | source)
XLA Modules:
  0.0 2083.6 jit_solution(18031763541794819482)
XLA Ops:
  20.7 21.0 %fusion.166 = f32[4,512,1612]{1,2,0:T(8,128)} fusion(bf16[4,512,1536]{2,1,0:T(8,128)(2,1)} %param.25, f32[1536]{0:T(1024)S(1)} %copy-done.62, f32[4,512]{1,0:T(4,128)S(1)} %get-tuple-element.2187, bf16[1536,12]{0,1:T(8,128)(2,1)S(1)} %copy-done.101, bf16[1536,64]{0,1:T(8,128)(2,1)S(1)} %copy-done.99, bf16[1536,768]{0,1:T(8,128)(2,1)} %copy.425, ...), kind=kOutput, calls=%fused_computation.246 | convolution fusion | flops 10174218240 | bytes 24463360 | tf_op jit(solution)/shard_map/aym,mq->ayq/dot_general | solution.py:144
  63.8 17.6 fusion.156
  126.1 150.2 %while.109 = (s32[]{:T(128)}, f32[4,12,64,128]{3,2,1,0:T(8,128)}, f32[4,12]{1,0:T(4,128)}, f32[2,4,12,256,64]{3,4,2,1,0:T(8,128)}, f32[2,4,12,256]{3,1,2,0:T(4,1...) while((s32[]{:T(128)}, f32[4,12,64,128]{3,2,1,0:T(8,128)}, ...), condition=%wide.region_4.5_spmd.clone.clone, body=%wide.region_1.4_spmd.clone.clone.sunk | while | flops 5272707072 | bytes 202985168 | solution.py:96
  137.4 18.4 multiply_dynamic-update-slice_fusion.4
  166.8 18.1 bitcast_dynamic-update-slice_fusion.14
  211.9 18.4 multiply_dynamic-update-slice_fusion.4
  241.9 18.1 bitcast_dynamic-update-slice_fusion.14
  279.7 11.5 copy.439
  309.9 37.4 %all-gather.9.cloned.1.call-done = f32[32,12,64,128]{3,2,1,0:T(8,128)} async-done(((f32[4,12,64,128]{3,2,1,0:T(8,128)}), f32[32,12,64,128]{3,2,1,0:T(8,128)}) %all-gather.9.cloned.1.call-update) | async-done | bytes 12582928 | tf_op jit(solution)/shard_map/all_gather | solution.py:25
  347.3 27.2 %while.107 = (s32[]{:T(128)}, f32[4,12,64,128]{3,2,1,0:T(8,128)}, s32[]{:T(128)}, f32[8,4,12]{2,1,0:T(4,128)}, f32[8,4,12,64,128]{4,3,2,1,0:T(8,128)}, /*index=5*/s32[]{:T(128)}, s32[]{:T(128)}) while((s32[]{:T(128)}, f32[4,12,64,128]{3,2,1,0:T(8,128)}, s32[]{:T(128)}, f32[8,4,12]{2,1,0:T(4,128)}, ...), condition=%wide.region_6.7_spmd.clone, body=%wide.region_5.6_spmd.clone.sunk | while | flops 1572868 | bytes 4719273 | solution.py:37
  381.7 12.4 multiply_reduce_fusion.8
  394.1 11.9 psum.126
  406.1 11.1 multiply_reduce_fusion
  425.9 15.1 multiply_reduce_fusion.1
  483.9 37.5 %all-gather.11.cloned.1.call-done = f32[32,12,64,128]{3,2,1,0:T(8,128)} async-done(((f32[4,12,64,128]{3,2,1,0:T(8,128)}), f32[32,12,64,128]{3,2,1,0:T(8,128)}) %all-gather.11.cloned.1.call-update) | async-done | bytes 12582928 | tf_op jit(solution)/shard_map/all_gather | solution.py:25
  521.4 12.1 rev.7
  533.5 27.3 %while.108 = (s32[]{:T(128)}, f32[4,12,64,128]{3,2,1,0:T(8,128)}, s32[]{:T(128)}, f32[8,4,12]{2,1,0:T(4,128)}, f32[8,4,12,64,128]{4,3,2,1,0:T(8,128)}, /*index=5*/s32[]{:T(128)}, s32[]{:T(128)}) while((s32[]{:T(128)}, f32[4,12,64,128]{3,2,1,0:T(8,128)}, s32[]{:T(128)}, f32[8,4,12]{2,1,0:T(4,128)}, ...), condition=%wide.region_13.14_spmd.clone, body=%wide.region_12.13_spmd.clone.sunk | while | flops 1572868 | bytes 4719273 | solution.py:37
  574.5 252.0 %while.110 = (s32[]{:T(128)}, f32[4,12,64,128]{3,2,1,0:T(8,128)}, f32[4,12]{1,0:T(4,128)S(1)}, f32[2,4,12,256,64]{3,4,2,1,0:T(8,128)}, f32[2,4,256,128]{3,2,1,0:...) while((s32[]{:T(128)}, f32[4,12,64,128]{3,2,1,0:T(8,128)}, ...), condition=%wide.region_28.29_spmd.clone.clone, body=%wide.region_16.28_spmd.clone.clone.sunk | while | flops 10513170432 | bytes 131728640 | solution.py:96
  595.1 27.3 %fusion.282 = (f32[4,12,256]{2,1,0:T(8,128)}, f32[4,12,256]{2,1,0:T(8,128)}, f32[4,256,256]{2,1,0:T(8,128)}, f32[4,12,256]{2,1,0:T(8,128)}) fusion(f32[2,4,12,256,256]{4,3,2,1,0:T(8,128)} %get-tuple-element.2885, s32[]{:T(128)S(6)} %sub.273, f32[4,256,256]{2,1,0:T(8,128)} %dynamic-slice_bitcast_fusion.8, f32[4,12,256]{2,1,0:T(8,128)} %bitcast.551, ...), kind=kOutput, calls=%fused_computation.129.clone.1 | convolution fusion | flops 2450223104 | bytes 46417408 | tf_op jit(solution)/shard_map/transpose(jvp())/while/body/eval_jaxpr/shlm,shmp->shlp/dot_general | solution.py:57
  676.1 16.5 bitcast_dynamic-update-slice_fusion.17
  719.6 27.6 %fusion.282 = (f32[4,12,256]{2,1,0:T(8,128)}, f32[4,12,256]{2,1,0:T(8,128)}, f32[4,256,256]{2,1,0:T(8,128)}, f32[4,12,256]{2,1,0:T(8,128)}) fusion(f32[2,4,12,256,256]{4,3,2,1,0:T(8,128)} %get-tuple-element.2885, s32[]{:T(128)S(6)} %sub.273, f32[4,256,256]{2,1,0:T(8,128)} %dynamic-slice_bitcast_fusion.8, f32[4,12,256]{2,1,0:T(8,128)} %bitcast.551, ...), kind=kOutput, calls=%fused_computation.129.clone.1 | convolution fusion | flops 2450223104 | bytes 46417408 | tf_op jit(solution)/shard_map/transpose(jvp())/while/body/eval_jaxpr/shlm,shmp->shlp/dot_general | solution.py:57
  800.7 16.5 bitcast_dynamic-update-slice_fusion.17
  851.4 11.1 copy.459
  871.5 21.2 %multiply_reduce_fusion.4 = (f32[768]{0:T(1024)}, f32[768]{0:T(1024)}, f32[768]{0:T(1024)}, f32[768]{0:T(1024)}, f32[768]{0:T(1024)}, /*index=5*/f32[4,512,768]{1,2,0:T(8,128)}) fusion(f32[4,512,768]{1,2,0:T(8,128)} %slice.190, f32[4,3,768]{1,2,0:T(8,128)} %copy.429, f32[4,512,1612]{1,2,0:T(8,128)} %fusion.166, f32[4,512,768]{1,2,0:T(8,128)} %get-tuple-element.2142, ...), kind=kLoop, calls=%fused_computation.226 | loop fusion | flops 36172032 | bytes 37804032 | tf_op jit(solution)/shard_map/transpose(jvp())/reduce_sum | solution.py:43
  912.4 13.3 pad_add_fusion
  949.4 22.4 %convolution_bitcast_fusion = f32[1536,1612]{0,1:T(8,128)} fusion(bf16[4,512,1536]{2,1,0:T(8,128)(2,1)} %param.25, f32[1536]{0:T(1024)S(1)} %copy-done.63, f32[4,512]{1,0:T(4,128)S(1)} %copy-done.47, bf16[4,512,12]{1,2,0:T(8,128)(2,1)S(1)} %copy-done.48, bf16[4,512,64]{1,2,0:T(8,128)(2,1)S(1)} %copy-done.43, bf16[4,512,768]{1,2,0:T(8,128)(2,1)} %fusion.152, ...), kind=kOutput, calls=%fused_computation.207 | convolution fusion | flops 10180820992 | bytes 22812672 | tf_op jit(solution)/shard_map/wji,wjr->ir/dot_general | solution.py:238
  984.2 11.3 fusion.174
  995.5 20.5 fusion.176
  1017.1 165.5 %all-reduce.29.cloned.1.call-done = (f32[1536,768]{0,1:T(8,128)}, f32[1536,768]{0,1:T(8,128)}, f32[1536,64]{0,1:T(8,128)}, f32[1536,12]{0,1:T(8,128)}, f32[768,1536]{1,0:T(8,128)}) async-done(((f32[1536,768]{0,1:T(8,128)}, f32[1536,768]{0,1:T(8,128)}, f32[1536,64]{0,1:T(8,128)}, f32[1536,12]{0,1:T(8,128)}, f32[768,1536]{1,0:T(8,128)}), (f32[1536,768]{0,1:T(8,128)}, f32[1536,768]{0,1:T(8,128)}, ...) | async-done | bytes 14622736 | tf_op jit(solution)/shard_map/psum | solution.py:257
  1194.8 825.0 %all-reduce.31.cloned.1.call-done = (f32[4,512,1536]{2,1,0:T(8,128)}, f32[4,512,1536]{2,1,0:T(8,128)}) async-done(((f32[4,512,1536]{2,1,0:T(8,128)}, f32[4,512,1536]{2,1,0:T(8,128)}), (f32[4,512,1536]{2,1,0:T(8,128)}, f32[4,512,1536]{2,1,0:T(8,128)})) %all-reduce.31.cloned.1.call-update) | async-done | bytes 25165840 | tf_op jit(solution)/shard_map/psum | solution.py:184
  2030.0 15.7 fusion.144
  2045.7 24.6 %all-reduce.23 = (f32[1536]{0:T(1024)}, f32[4,768]{1,0:T(4,128)}, f32[4,64]{1,0:T(4,128)}, f32[768]{0:T(1024)}, f32[64]{0:T(128)}, /*index=5*/f32[12]{0:T(128)}, f32[12]{0:T(128)}, f32[12]{0:T(128)}, f32[768]{0:T(1024)}) all-reduce(f32[1536]{0:T(1024)S(1)} %get-tuple-element.1960, ...), channel_id=1, replica_groups=mesh['seq'=8,'head'=4] {'seq'}, use_global_device_ids=true, to_apply=%region_33.34 | all-reduce | flops 6500 | bytes 52000 | tf_op jit(solution)/shard_map/psum | solution.py:257
  (599 shorter events, 584.1 us)
Async XLA Ops:
  7.2 398.9 %copy-start = (bf16[768,1536]{1,0:T(8,128)(2,1)S(1)}, bf16[768,1536]{1,0:T(8,128)(2,1)}, u32[]{:S(2)}) copy-start(bf16[768,1536]{1,0:T(8,128)(2,1)} %param.40) | copy-start | bytes 7077892
  7.2 95.6 %all-gather.7.cloned.1.call-start = ((), (), s32[]{:S(2)}) async-start(), calls=%async_computation.1 | async-start | bytes 2621440 | tf_op jit(solution)/shard_map/all_gather | solution.py:163
  12.1 29.6 %copy-start.46 = (f32[4,512]{1,0:T(4,128)}, f32[4,512]{1,0:T(4,128)S(1)}, u32[]{:S(2)}) copy-start(f32[4,512]{1,0:T(4,128)S(1)} %get-tuple-element.2187) | copy-start | bytes 24580
  20.7 28.6 %copy-start.91 = (f32[4,64]{1,0:T(4,128)S(1)}, f32[4,64]{1,0:T(4,128)}, u32[]{:S(2)}) copy-start(f32[4,64]{1,0:T(4,128)} %param.33) | copy-start | bytes 3076
  46.9 3.5 collective-permute-start
  52.3 295.0 %all-gather.9.cloned.1.call-start = ((), (), s32[]{:S(2)}) async-start(), calls=%async_computation.3 | async-start | bytes 14155776 | tf_op jit(solution)/shard_map/all_gather | solution.py:25
  58.9 22.5 %copy-start.89 = (f32[12]{0:T(128)}, f32[12]{0:T(128)S(1)}, u32[]{:S(2)}) copy-start(f32[12]{0:T(128)S(1)} %exp.148) | copy-start | bytes 148
  60.0 21.4 %copy-start.36 = (f32[4,512,12]{1,2,0:T(8,128)}, f32[4,512,12]{1,2,0:T(8,128)S(1)}, u32[]{:S(2)}) copy-start(f32[4,512,12]{1,2,0:T(8,128)S(1)} %get-tuple-element.2144) | copy-start | bytes 294916
  134.3 21.5 %copy-start.18 = (f32[4,12,256]{2,1,0:T(8,128)}, f32[4,12,256]{2,1,0:T(8,128)S(1)}, u32[]{:S(2)}) copy-start(f32[4,12,256]{2,1,0:T(8,128)S(1)} %copy.625) | copy-start | bytes 147460 | tf_op jit(solution)/shard_map/jvp()/while
  134.4 21.4 %copy-start.22 = (f32[4,12,256]{2,1,0:T(8,128)}, f32[4,12,256]{2,1,0:T(8,128)S(1)}, u32[]{:S(2)}) copy-start(f32[4,12,256]{2,1,0:T(8,128)S(1)} %copy.624) | copy-start | bytes 147460 | tf_op jit(solution)/shard_map/jvp()/while
  161.2 23.8 %slice-start = ((s8[6291456]{0:T(1024)(128)(4,1)}), s8[4194304]{0:T(1024)(128)(4,1)S(1)}, s32[]{:S(2)}) async-start(s8[6291456]{0:T(1024)(128)(4,1)} %bitcast.527), calls=%async_computation.7 | async-start | bytes 8388608 | tf_op jit(solution)/shard_map/jvp()/while
  161.2 23.8 %slice-start.2 = ((s8[6291456]{0:T(1024)(128)(4,1)}), s8[4194304]{0:T(1024)(128)(4,1)S(1)}, s32[]{:S(2)}) async-start(s8[6291456]{0:T(1024)(128)(4,1)} %bitcast.534), calls=%async_computation.9 | async-start | bytes 8388608 | tf_op jit(solution)/shard_map/jvp()/while
  208.8 21.5 %copy-start.18 = (f32[4,12,256]{2,1,0:T(8,128)}, f32[4,12,256]{2,1,0:T(8,128)S(1)}, u32[]{:S(2)}) copy-start(f32[4,12,256]{2,1,0:T(8,128)S(1)} %copy.625) | copy-start | bytes 147460 | tf_op jit(solution)/shard_map/jvp()/while
  208.9 21.4 %copy-start.22 = (f32[4,12,256]{2,1,0:T(8,128)}, f32[4,12,256]{2,1,0:T(8,128)S(1)}, u32[]{:S(2)}) copy-start(f32[4,12,256]{2,1,0:T(8,128)S(1)} %copy.624) | copy-start | bytes 147460 | tf_op jit(solution)/shard_map/jvp()/while
  235.7 24.4 %slice-start = ((s8[6291456]{0:T(1024)(128)(4,1)}), s8[4194304]{0:T(1024)(128)(4,1)S(1)}, s32[]{:S(2)}) async-start(s8[6291456]{0:T(1024)(128)(4,1)} %bitcast.527), calls=%async_computation.7 | async-start | bytes 8388608 | tf_op jit(solution)/shard_map/jvp()/while
  235.7 24.4 %slice-start.2 = ((s8[6291456]{0:T(1024)(128)(4,1)}), s8[4194304]{0:T(1024)(128)(4,1)S(1)}, s32[]{:S(2)}) async-start(s8[6291456]{0:T(1024)(128)(4,1)} %bitcast.534), calls=%async_computation.9 | async-start | bytes 8388608 | tf_op jit(solution)/shard_map/jvp()/while
  276.3 245.1 %all-gather.11.cloned.1.call-start = ((), (), s32[]{:S(2)}) async-start(), calls=%async_computation.4 | async-start | bytes 14155776 | tf_op jit(solution)/shard_map/all_gather | solution.py:25
  277.2 104.6 %copy-start.60 = (f32[768]{0:T(1024)}, f32[768]{0:T(1024)S(1)}, u32[]{:S(2)}) copy-start(f32[768]{0:T(1024)S(1)} %mul.929) | copy-start | bytes 9220
  277.9 128.2 %copy-start.65 = (f32[4,512]{1,0:T(4,128)}, f32[4,512]{1,0:T(4,128)S(1)}, u32[]{:S(2)}) copy-start(f32[4,512]{1,0:T(4,128)S(1)} %compare_convert_fusion) | copy-start | bytes 24580
  450.4 475.4 %reduce-scatter.2.cloned.1.call-start = ((), (), s32[]{:S(2)}) async-start(), calls=%async_computation.2 | async-start | bytes 2621440 | tf_op jit(solution)/shard_map/reduce_scatter | solution.py:223
  533.5 29.5 %copy-start.72 = (f32[4,12,1]{1,0,2:T(4,128)S(1)}, f32[4,12,1]{1,0,2:T(4,128)}, u32[]{:S(2)}) copy-start(f32[4,12,1]{1,0,2:T(4,128)} %copy-done.71) | copy-start | bytes 580
  583.9 38.5 %copy-start.20 = (f32[1,4,12,256]{3,1,2,0:T(4,128)}, f32[1,4,12,256]{3,1,2,0:T(4,128)S(1)}, u32[]{:S(2)}) copy-start(f32[1,4,12,256]{3,1,2,0:T(4,128)S(1)} %get-tuple-element.2654) | copy-start | bytes 147460 | tf_op jit(solution)/shard_map/transpose(jvp())/while
  708.4 38.8 %copy-start.20 = (f32[1,4,12,256]{3,1,2,0:T(4,128)}, f32[1,4,12,256]{3,1,2,0:T(4,128)S(1)}, u32[]{:S(2)}) copy-start(f32[1,4,12,256]{3,1,2,0:T(4,128)S(1)} %get-tuple-element.2654) | copy-start | bytes 147460 | tf_op jit(solution)/shard_map/transpose(jvp())/while
  840.5 342.2 %all-reduce.29.cloned.1.call-start = ((), (), s32[]{:S(2)}) async-start(), calls=%async_computation.5 | async-start | bytes 29294592 | tf_op jit(solution)/shard_map/psum | solution.py:257
  871.5 21.2 %copy-start.53 = (f32[768]{0:T(1024)S(1)}, f32[768]{0:T(1024)}, u32[]{:S(2)}) copy-start(f32[768]{0:T(1024)} %copy-done.52) | copy-start | bytes 9220
  871.5 21.2 %copy-start.55 = (f32[768]{0:T(1024)S(1)}, f32[768]{0:T(1024)}, u32[]{:S(2)}) copy-start(f32[768]{0:T(1024)} %copy-done.54) | copy-start | bytes 9220
  871.5 21.2 %copy-start.57 = (f32[768]{0:T(1024)S(1)}, f32[768]{0:T(1024)}, u32[]{:S(2)}) copy-start(f32[768]{0:T(1024)} %copy-done.56) | copy-start | bytes 9220
  871.5 21.2 %copy-start.59 = (f32[768]{0:T(1024)S(1)}, f32[768]{0:T(1024)}, u32[]{:S(2)}) copy-start(f32[768]{0:T(1024)} %copy-done.58) | copy-start | bytes 9220
  933.6 3.7 collective-permute-start.1
  983.5 1036.3 %all-reduce.31.cloned.1.call-start = ((), (), s32[]{:S(2)}) async-start(), calls=%async_computation.6 | async-start | bytes 50331648 | tf_op jit(solution)/shard_map/psum | solution.py:184
  2030.0 40.3 %copy-start.41 = (f32[1536,64]{0,1:T(8,128)S(1)}, f32[1536,64]{0,1:T(8,128)}, u32[]{:S(2)}) copy-start(f32[1536,64]{0,1:T(8,128)} %get-tuple-element.2895) | copy-start | bytes 1179652
  2030.0 41.1 %copy-start.45 = (f32[1536,12]{0,1:T(8,128)S(1)}, f32[1536,12]{0,1:T(8,128)}, u32[]{:S(2)}) copy-start(f32[1536,12]{0,1:T(8,128)} %get-tuple-element.2896) | copy-start | bytes 221188
  (112 other events, 920.9 us)
Sparse Core Ops, SparseCore 0:
  52.4 50.4 all-gather.6
  276.4 70.8 all-gather.8
  450.5 70.8 all-gather.10
  840.6 43.7 reduce-scatter.1
  983.6 198.9 all-reduce.28
  1185.7 834.1 all-reduce.30
where the time goes:
time: 2100 us; the launch traced here: 2080 us
  waiting for transfers between devices  1070 us (51%)
  matrix products  332 us (16%)
  other arithmetic  305 us (15%)
  local copies, waits for them, and re-layouts  295 us (14%)
  blocking collectives  55 us (3%)
    psum x1, waiting for transfers between devices, per_device(): lax.psum(jnp.einsum('kmq,qh->kmh', hidden_rows, output_projection_weight,...  825 us
    psum x1, waiting for transfers between devices, per_device(): lax.psum((grad_norm_gain, grad_in_weight[:, :inner_dev], grad_in_weight[:...  166 us
    dot_general x6, matrix products, block_math(): jnp.einsum('shlm,shmp->shlp', mixing, block_x, precision=MATMUL_ACCURACY)  124 us
    all_gather x2, waiting for transfers between devices, carried_in(): pieces = jax.tree.map(lambda part: lax.all_gather(part, axis), value)  74.9 us
    dynamic_update_slice x12, other arithmetic, ssd_piece(): lax.scan(advance, start_state, (xs_blocks, b_blocks, c_blocks, step_block...  46.9 us
    select_n x14, other arithmetic, hop(): jnp.where(position < mine, new, old)  45.2 us
  transfers between devices with their start and end apart: 8, of which 5 were waited for; matrix products, arithmetic and copies ran while one was open for 11% of the time, Pallas kernels for 0%

commit v1 on v0

v1 whole, which is shorter than its diff:
```python
import functools

import jax
import jax.numpy as jnp
from jax import lax
from jax.experimental import pallas as pl
from jax.experimental.pallas import tpu as pltpu
from jax.sharding import PartitionSpec as P

HEAD_DIM = 64
STATE = 128
CONV = 4
INNER = 3072
CHUNK = 128
ROWS = 256
HALF = 64
LANES = 128
EPSILON = 1e-05
GROUPS = 2
F32 = jnp.float32
BF16 = jnp.bfloat16
F16 = jnp.float16
I32 = jnp.int32
VMEM_LIMIT = 60 * 1024 * 1024


def halves(value):
    high = value.astype(BF16)
    return high, (value - high.astype(F32)).astype(BF16)


def thirds(value):
    high = value.astype(BF16)
    rest = value - high.astype(F32)
    middle = rest.astype(BF16)
    return high, middle, (rest - middle.astype(F32)).astype(BF16)


def mm(a, b, ca=1, cb=0):
    return lax.dot_general(a, b, (((ca,), (cb,)), ((), ())), preferred_element_type=F32)


def dot3(a, b):
    return mm(jnp.concatenate([a[0], a[1]], axis=1), jnp.concatenate([b[0], b[0]], axis=0)) + mm(a[0], b[1])


def dot3_t(a, b):
    n = b[0].shape[0]
    wide = mm(a[0], jnp.concatenate([b[0], b[1]], axis=0), 1, 1)
    return wide[:, :n] + wide[:, n:] + mm(a[1], b[0], 1, 1)


def per_head(value, expand):
    high, low = halves(value)
    return mm(high, expand, 1, 1) + mm(low, expand, 1, 1)


def summed_by(matrix, value):
    out = None
    for part in thirds(value):
        term = mm(matrix, part)
        out = term if out is None else out + term
    return out


def rows8(row):
    return jnp.broadcast_to(row, (8, row.shape[-1]))


def fold8(value):
    return jnp.sum(value.reshape(value.shape[0] // 8, 8, value.shape[1]), axis=0)


def peak8(value):
    return jnp.max(jnp.abs(value).reshape(value.shape[0] // 8, 8, value.shape[1]), axis=0)


def left_half(rows):
    return lax.broadcasted_iota(jnp.int32, (rows, LANES), 1) < HEAD_DIM


def spread_pair(value, pair, left):
    h = 2 * pair
    return jnp.where(left, value[:, h : h + 1], value[:, h + 1 : h + 2])


def spread(value, channels):
    left = left_half(value.shape[0])
    return jnp.concatenate([spread_pair(value, j, left) for j in range(channels // LANES)], axis=1)


def softplus(value):
    small = jnp.exp(-jnp.abs(value))
    one = 1.0 + small
    log = jnp.where(one == 1.0, small, jnp.log(one) * (small / jnp.where(one == 1.0, 1.0, one - 1.0)))
    return jnp.maximum(value, 0.0) + log


def sigmoid(value):
    return 1.0 / (1.0 + jnp.exp(-value))


def conv(ext_ref, taps_ref, bias_ref, start, length, lanes):
    summed = bias_ref[0:1, lanes] + taps_ref[0:1, lanes] * ext_ref[start + 5 : start + 5 + length, lanes]
    for k in range(1, CONV):
        summed = summed + taps_ref[k : k + 1, lanes] * ext_ref[start + 5 + k : start + 5 + k + length, lanes]
    return summed


def conv_back(grad_ref, taps_ref, start, length, lanes):
    raw = taps_ref[CONV - 1 : CONV, lanes] * grad_ref[start : start + length, lanes]
    for j in range(1, CONV):
        raw = raw + taps_ref[CONV - 1 - j : CONV - j, lanes] * grad_ref[start + j : start + j + length, lanes]
    return raw


def as_column(row):
    return jnp.broadcast_to(row, (LANES, LANES)).T


def row_sums(value):
    ones = jnp.ones((8, LANES), BF16)
    parts = thirds(value)
    return mm(ones, parts[0], 1, 1) + (mm(ones, parts[1], 1, 1) + mm(ones, parts[2], 1, 1))


def triangle(length, lower):
    row = lax.broadcasted_iota(jnp.int32, (length, length), 0)
    column = lax.broadcasted_iota(jnp.int32, (length, length), 1)
    return row >= column if lower else row <= column


ANYWHERE = pl.BlockSpec(memory_space=pl.ANY)


class Order:
    def __init__(self):
        self.now, self.pending, self.used = None, [], 0

    def before_next(self, *arrays):
        self.pending += [array for array in arrays if array.dtype != F16]

    def fence(self):
        tokens = self.pending + ([] if self.now is None else [self.now])
        self.pending = []

        def body(*refs):
            refs[-1][...] = jnp.zeros_like(refs[-1])

        self.now = pl.pallas_call(
            body,
            in_specs=[ANYWHERE] * len(tokens),
            out_shape=SHAPE((8, LANES), F32),
            compiler_params=pltpu.CompilerParams(vmem_limit_bytes=VMEM_LIMIT),
            name="fence",
        )(*tokens)

    def tie(self, value):
        if self.now is None:
            return value
        self.used += 1
        at = (self.used // LANES % 8, self.used % LANES)
        return value + lax.slice(self.now, at, (at[0] + 1, at[1] + 1)).reshape(()).astype(value.dtype)

    def call(self, kernel, operands, *, meta, grid, in_specs, out_specs, out_shape, scratch=(), flops, moved, name, aliases=None):
        tokens = self.pending + ([] if self.now is None else [self.now])
        inputs, outputs = len(operands), len(out_shape)
        self.pending = []

        def body(meta_ref, *refs):
            last = inputs + len(tokens) + outputs
            refs[last][...] = jnp.zeros_like(refs[last])
            kernel(meta_ref, *refs[:inputs], *refs[inputs + len(tokens) : last], *refs[last + 1 :])

        result = pl.pallas_call(
            body,
            grid_spec=pltpu.PrefetchScalarGridSpec(
                num_scalar_prefetch=1,
                grid=grid,
                in_specs=list(in_specs) + [ANYWHERE] * len(tokens),
                out_specs=list(out_specs) + [whole((8, LANES))],
                scratch_shapes=list(scratch),
            ),
            out_shape=list(out_shape) + [SHAPE((8, LANES), F32)],
            input_output_aliases=aliases or {},
            compiler_params=pltpu.CompilerParams(
                vmem_limit_bytes=VMEM_LIMIT, dimension_semantics=("arbitrary",) * len(grid)
            ),
            cost_estimate=pl.CostEstimate(flops=int(flops), bytes_accessed=int(moved), transcendentals=0),
            name=name,
        )(meta, *operands, *tokens)
        self.now = result[-1]
        return result[:-1]


def constants_kernel(lengths_ref, step_bias_ref, decay_ref, skip_ref, out_gain_ref, meta_ref, head_ref, chan_ref, expand_ref, *, slots):
    seqs, heads = lengths_ref.shape[0], step_bias_ref.shape[1]
    channels = out_gain_ref.shape[1]
    place, least = jnp.int32(0), lengths_ref[0]
    for s in range(1, seqs):
        shorter = lengths_ref[s] < least
        place, least = jnp.where(shorter, s, place), jnp.where(shorter, lengths_ref[s], least)
    first = lax.axis_index("seq") * slots
    for s in range(seqs):
        source = jnp.where(place == s, seqs - 1, s) if s < seqs - 1 else place
        meta_ref[s] = source
        meta_ref[seqs + s] = lengths_ref[source] - first
    mine, count = lax.axis_index("head"), lax.axis_size("head")
    meta_ref[2 * seqs] = jnp.where((mine == 0) | (mine == count - 1), 1, 0)
    lane = lax.broadcasted_iota(jnp.int32, (8, LANES), 1)
    row = lax.broadcasted_iota(jnp.int32, (8, LANES), 0)
    pad = lambda ref: jnp.concatenate([ref[...], jnp.zeros((1, LANES - heads), F32)], axis=1)
    head_ref[...] = jnp.zeros((8, LANES), F32)
    head_ref[0:1, :] = pad(step_bias_ref)
    head_ref[1:2, :] = pad(decay_ref)
    chan_ref[...] = jnp.zeros_like(chan_ref)
    chan_ref[0:1, :] = spread(rows8(pad(skip_ref)), channels)[0:1, :]
    chan_ref[1:2, :] = out_gain_ref[...]
    head_of = lax.broadcasted_iota(jnp.int32, (LANES, channels), 1) // HEAD_DIM
    expand_ref[...] = jnp.where(head_of == lax.broadcasted_iota(jnp.int32, (LANES, channels), 0), 1.0, 0.0).astype(BF16)


def normalized(rows, gain):
    u = rows.astype(F32)
    scale = lax.rsqrt(jnp.mean(u * u, axis=-1, keepdims=True) + EPSILON)
    return (u * scale * gain).astype(BF16)


def project_kernel(
    meta_ref, u_ref, cot_ref, gain_ref, gate_ref, x_ref, step_ref, out_ref, normed_ref, branch_ref, proj_ref, gh_ref, *, first
):
    rows, channels = u_ref.shape[0], gate_ref.shape[1]
    normed = normalized(u_ref[...], gain_ref[...])
    normed_ref[...] = normed
    at = pl.program_id(1) * rows + lax.broadcasted_iota(jnp.int32, cot_ref.shape, 0)
    live = at < meta_ref[4 + first + pl.program_id(0)]
    branch = jnp.where(live, cot_ref[...].astype(F32), 0.0).astype(BF16)
    branch_ref[...] = branch
    proj_ref[:, :channels] = mm(normed, gate_ref[...])
    proj_ref[:, channels : 2 * channels] = mm(normed, x_ref[...])
    proj_ref[:, 2 * channels :] = mm(normed, step_ref[...])
    gh_ref[...] = mm(branch, out_ref[...])


def edge_kernel(meta_ref, before_ref, gain_ref, x_ref, pair_ref, xhalo_ref, bchalo_ref):
    seqs, rows, width = before_ref.shape
    normed = normalized(before_ref[...].reshape(seqs * rows, width), gain_ref[...])
    xhalo_ref[...] = mm(normed, x_ref[...]).reshape(xhalo_ref.shape)
    bchalo_ref[...] = mm(normed, pair_ref[...]).reshape(bchalo_ref.shape)


def local_state_kernel(
    meta_ref, x_ref, xhalo_ref, normed_ref, pair_ref, bchalo_ref, step_ref, taps_ref, bias_ref, btaps_ref, bbias_ref,
    head_ref, xs_ref, raw_ref, bcs_ref, sc_ref, end_ref, xe, be, state, total,
):
    c, rows = pl.program_id(1), x_ref.shape[0]
    channels = x_ref.shape[1]

    @pl.when(c == 0)
    def _():
        xe[0:8, :] = xhalo_ref[...]
        be[0:8, :] = bchalo_ref[...]
        state[...] = jnp.zeros_like(state)
        total[...] = jnp.zeros_like(total)

    xe[8 : 8 + rows, :] = x_ref[...]
    raw = mm(normed_ref[...], pair_ref[...])
    raw_ref[...] = raw
    be[8 : 8 + rows, :] = raw
    lower = triangle(CHUNK, True).astype(BF16)
    left = left_half(CHUNK)
    lane = lax.broadcasted_iota(I32, (CHUNK, LANES), 1)
    for at in range(0, rows, CHUNK):
        here = slice(at, at + CHUNK)
        for lanes in (slice(0, STATE), slice(STATE, 2 * STATE)):
            pb = conv(be, btaps_ref, bbias_ref, at, CHUNK, lanes)
            bcs_ref[here, lanes] = pb * sigmoid(pb)
        step = softplus(step_ref[here, :] + head_ref[0:1, :])
        cum = summed_by(lower, -step * jnp.exp(head_ref[1:2, :]))
        sc_ref[here, :] = jnp.where(lane < HALF, step, pltpu.roll(cum, HALF, 1))
        end = cum[CHUNK - 1 : CHUNK, :]
        fading = step * jnp.exp(end - cum)
        keep = spread(rows8(jnp.exp(end)), channels)
        bt2 = halves(bcs_ref[here, :STATE].T)
        for pair in range(channels // LANES):
            lanes = slice(pair * LANES, (pair + 1) * LANES)
            p = conv(xe, taps_ref, bias_ref, at, CHUNK, lanes)
            xs = p * sigmoid(p)
            xs_ref[here, lanes] = xs
            weighted = halves(xs * spread_pair(fading, pair, left))
            state[:, lanes] = keep[0:1, lanes] * state[:, lanes] + dot3(bt2, weighted)
        total[...] += rows8(end)
    xe[0:8, :] = xe[rows : rows + 8, :]
    be[0:8, :] = be[rows : rows + 8, :]

    @pl.when(c == pl.num_programs(1) - 1)
    def _():
        end_ref[0:STATE, :] = state[...]
        end_ref[STATE : STATE + 8, :] = spread(jnp.exp(total[...]), channels)


def mix_kernel(
    meta_ref, xs_ref, bcs_ref, sc_ref, start_ref, gate_ref, gh_ref, chan_ref,
    mixed_ref, red_ref, states_ref, final_ref, state,
):
    c, rows = pl.program_id(1), xs_ref.shape[0]
    channels = xs_ref.shape[1]

    @pl.when(c == 0)
    def _():
        state[...] = start_ref[...]

    lower = triangle(CHUNK, True)
    left = left_half(CHUNK)
    zero = jnp.zeros((CHUNK, LANES), BF16)
    for at in range(0, rows, CHUNK):
        here = slice(at, at + CHUNK)
        entering = state[...]
        states_ref[at // CHUNK] = entering
        sc = sc_ref[here, :]
        sc_t = sc.T
        b2, c2 = halves(bcs_ref[here, :STATE]), halves(bcs_ref[here, STATE:])
        bt2 = halves(bcs_ref[here, :STATE].T)
        scores = dot3_t(c2, b2)
        carried = dot3(c2, halves(entering))
        end_full = spread(rows8(pltpu.roll(sc, HALF, 1)[CHUNK - 1 : CHUNK, :]), channels)
        sq = jnp.zeros((CHUNK, LANES), F32)
        dt = jnp.zeros((CHUNK, LANES), F32)
        for pair in range(channels // LANES):
            lanes = slice(pair * LANES, (pair + 1) * LANES)
            xs = xs_ref[here, lanes]
            weighted = xs * spread_pair(sc, pair, left)
            high, low = halves(weighted)
            stacked, columns = [], []
            for h in (HALF + 2 * pair, HALF + 2 * pair + 1):
                column = jnp.broadcast_to(sc[:, h : h + 1], (CHUNK, LANES))
                columns.append(column)
                mixing = jnp.where(lower, jnp.exp(column - sc_t[h : h + 1, :]), 0.0) * scores
                stacked.append(jnp.concatenate(halves(mixing), axis=1))
            right = jnp.concatenate(
                [jnp.concatenate([high, low], axis=1), jnp.concatenate([high, zero], axis=1)], axis=0
            )
            out = mm(jnp.concatenate(stacked, axis=0), right)
            out = out[:, :LANES] + out[:, LANES:]
            cum_full = jnp.where(left, columns[0], columns[1])
            mixed = (
                jnp.where(left, out[:CHUNK], out[CHUNK:])
                + carried[:, lanes] * jnp.exp(cum_full)
                + chan_ref[0:1, lanes] * xs
            )
            mixed_ref[here, lanes] = mixed
            gate = gate_ref[here, lanes]
            gated = mixed * (gate * sigmoid(gate))
            sq = sq + gated * gated
            dt = dt + gated * (gh_ref[here, lanes] * chan_ref[1:2, lanes])
            tail = end_full[0:1, lanes]
            later = halves(weighted * jnp.exp(tail - cum_full))
            state[:, lanes] = jnp.exp(tail) * state[:, lanes] + dot3(bt2, later)
        row = lax.broadcasted_iota(I32, (8, CHUNK), 0)
        red_ref[:, here] = jnp.where(row == 0, row_sums(sq), row_sums(dt))

    @pl.when(c == pl.num_programs(1) - 1)
    def _():
        final_ref[...] = state[...]


def gate_back_kernel(
    meta_ref, mixed_ref, gate_ref, gh_ref, row_ref, bcs_ref, sc_ref, chan_ref,
    hidden_ref, ggate_ref, dy_ref, gend_ref, acc_ref, peak_ref, grad, total,
):
    c, rows = pl.program_id(1), mixed_ref.shape[0]
    channels = mixed_ref.shape[1]

    @pl.when(c == 0)
    def _():
        grad[...] = jnp.zeros_like(grad)
        total[...] = jnp.zeros_like(total)

    @pl.when((c == 0) & (pl.program_id(0) == 0))
    def _():
        acc_ref[...] = jnp.zeros_like(acc_ref)
        peak_ref[...] = jnp.zeros_like(peak_ref)

    left = left_half(CHUNK)
    for at in reversed(range(0, rows, CHUNK)):
        here = slice(at, at + CHUNK)
        cum = pltpu.roll(sc_ref[here, :], HALF, 1)
        ct2 = halves(bcs_ref[here, STATE:].T)
        keep = spread(rows8(jnp.exp(cum[CHUNK - 1 : CHUNK, :])), channels)
        grown = jnp.exp(cum)
        squares, dots = as_column(row_ref[0:1, here]), as_column(row_ref[1:2, here])
        r = lax.rsqrt(squares * (1.0 / INNER) + EPSILON)
        pull = r * r * r * dots * (1.0 / INNER)
        for pair in range(channels // LANES):
            lanes = slice(pair * LANES, (pair + 1) * LANES)
            mixed, gate, gh = mixed_ref[here, lanes], gate_ref[here, lanes], gh_ref[here, lanes]
            out_gain = chan_ref[1:2, lanes]
            sig = sigmoid(gate)
            silu = gate * sig
            gated = mixed * silu
            normal = gated * r
            hidden_ref[here, lanes] = (normal * out_gain).astype(BF16)
            acc_ref[:, lanes] += fold8(gh * normal)
            grad_gated = r * (gh * out_gain) - gated * pull
            dy = grad_gated * silu
            dy_ref[here, lanes] = dy
            ggate = grad_gated * mixed * (sig * (1.0 + gate * (1.0 - sig)))
            ggate_ref[here, lanes] = ggate.astype(BF16)
            peak_ref[:, lanes] = jnp.maximum(peak_ref[:, lanes], jnp.maximum(peak8(ggate), peak8(dy)))
            grad[:, lanes] = keep[0:1, lanes] * grad[:, lanes] + dot3(
                ct2, halves(dy * spread_pair(grown, pair, left))
            )
        total[...] += rows8(cum[CHUNK - 1 : CHUNK, :])

    @pl.when(c == pl.num_programs(1) - 1)
    def _():
        gend_ref[0:STATE, :] = grad[...]
        gend_ref[STATE : STATE + 8, :] = spread(jnp.exp(total[...]), channels)


def state_back_kernel(
    meta_ref, x_ref, xprev_ref, xhalo_ref, bcs_ref, sc_ref, step_ref, dy_ref, mixed_ref, states_ref, final_ref,
    gin_ref, ggate_ref, taps_ref, bias_ref, head_ref, chan_ref, expand_ref,
    gp_ref, dbc_ref, tail_ref, first_ref, acc_ref, hacc_ref,
    xe, ge, grad, flux, wide, wlow, dhigh, dlow, sums,
):
    c, rows = pl.program_id(1), x_ref.shape[0]
    blocks = pl.num_programs(1)
    channels = x_ref.shape[1]
    expand = expand_ref[...]

    @pl.when((c == 0) & (pl.program_id(0) == 0))
    def _():
        acc_ref[...] = jnp.zeros_like(acc_ref)
        hacc_ref[...] = jnp.zeros_like(hacc_ref)

    @pl.when(c == 0)
    def _():
        grad[...] = gin_ref[...]
        ending = per_head(fold8(grad[...] * final_ref[...]), expand)
        flux[...] = rows8(jnp.sum(ending, axis=0, keepdims=True))
        ge[rows : rows + 8, :] = jnp.zeros((8, channels), F32)

    @pl.when(c != 0)
    def _():
        ge[rows : rows + 8, :] = ge[0:8, :]

    @pl.when(c == blocks - 1)
    def _():
        xe[0:8, :] = xhalo_ref[...]

    @pl.when(c != blocks - 1)
    def _():
        xe[0:8, :] = xprev_ref[...]

    xe[8 : 8 + rows, :] = x_ref[...]
    gp_ref[:, :channels] = ggate_ref[...]
    upper = triangle(CHUNK, False)
    left = left_half(CHUNK)
    zero = jnp.zeros((CHUNK, LANES), BF16)
    turn = lambda value: pltpu.roll(value.astype(F32), HEAD_DIM, 1).astype(BF16)
    for at in reversed(range(0, rows, CHUNK)):
        here = slice(at, at + CHUNK)
        sc = sc_ref[here, :]
        sc_t = sc.T
        cum = pltpu.roll(sc, HALF, 1)
        end_full = spread(rows8(cum[CHUNK - 1 : CHUNK, :]), channels)
        b2, c2 = halves(bcs_ref[here, :STATE]), halves(bcs_ref[here, STATE:])
        ct2 = halves(bcs_ref[here, STATE:].T)
        scores_t = dot3_t(b2, c2)
        leaving2 = halves(grad[...])
        pulled = dot3(b2, leaving2)
        dscores_t = jnp.zeros((CHUNK, CHUNK), F32)
        for pair in range(channels // LANES):
            lanes = slice(pair * LANES, (pair + 1) * LANES)
            p = conv(xe, taps_ref, bias_ref, at, CHUNK, lanes)
            sig = sigmoid(p)
            xs = p * sig
            slope = sig * (1.0 + p * (1.0 - sig))
            step_full = spread_pair(sc, pair, left)
            weighted = xs * step_full
            wh, wl = halves(weighted)
            dy = dy_ref[here, lanes]
            dh, dl = halves(dy)
            turned_wh, turned_wl, turned_dh = turn(wh), turn(wl), turn(dh)
            w_rows = (
                jnp.concatenate([jnp.where(left, wh, turned_wl), jnp.where(left, wh, zero)], axis=1),
                jnp.concatenate([jnp.where(left, turned_wh, wl), jnp.where(left, zero, wh)], axis=1),
            )
            d_rows = (
                jnp.concatenate([jnp.where(left, dh, turned_dh), dl], axis=1),
                jnp.concatenate([jnp.where(left, turned_dh, dh), dl], axis=1),
            )
            stacked, columns = [], []
            for side, h in enumerate((HALF + 2 * pair, HALF + 2 * pair + 1)):
                column = jnp.broadcast_to(sc[:, h : h + 1], (CHUNK, LANES))
                columns.append(column)
                kern = jnp.where(upper, jnp.exp(sc_t[h : h + 1, :] - column), 0.0)
                dscores_t = dscores_t + kern * mm(w_rows[side], d_rows[side], 1, 1)
                stacked.append(jnp.concatenate(halves(kern * scores_t), axis=1))
            right = jnp.concatenate(
                [jnp.concatenate([dh, dl], axis=1), jnp.concatenate([dh, zero], axis=1)], axis=0
            )
            out = mm(jnp.concatenate(stacked, axis=0), right)
            out = out[:, :LANES] + out[:, LANES:]
            cum_full = jnp.where(left, columns[0], columns[1])
            fade = jnp.exp(end_full[0:1, lanes] - cum_full)
            dxw = jnp.where(left, out[:CHUNK], out[CHUNK:]) + pulled[:, lanes] * fade
            grad_xs = step_full * dxw + chan_ref[0:1, lanes] * dy
            wide[:, lanes], wlow[:, lanes] = halves(weighted * fade)
            gh, gl = halves(dy * jnp.exp(cum_full))
            dhigh[:, lanes], dlow[:, lanes] = gh, gl
            keep = jnp.exp(end_full[0:1, lanes])
            grad[:, lanes] = keep * grad[:, lanes] + dot3(ct2, (gh, gl))
            sums[0:CHUNK, lanes] = xs * dxw
            sums[CHUNK:, lanes] = dy * mixed_ref[here, lanes] - xs * grad_xs
            grad_p = grad_xs * slope
            ge[here, lanes] = grad_p
            for k in range(CONV):
                acc_ref[8 * k : 8 * k + 8, lanes] += fold8(grad_p * xe[at + 5 + k : at + 5 + k + CHUNK, lanes])
            acc_ref[32:40, lanes] += fold8(grad_p)
            acc_ref[40:48, lanes] += fold8(dy * xs)
            raw = conv_back(ge, taps_ref, at, CHUNK, lanes)
            gp_ref[here, channels + pair * LANES : channels + (pair + 1) * LANES] = raw.astype(BF16)
            if at == rows - CHUNK:
                tail_ref[:, lanes] = raw[CHUNK - 8 :, :]
        entering2 = halves(states_ref[at // CHUNK])
        dscores2 = halves(dscores_t)
        dscores_back = halves(dscores_t.T)
        dbc_ref[here, :STATE] = dot3(dscores2, c2) + dot3_t((wide[...], wlow[...]), leaving2)
        dbc_ref[here, STATE:] = dot3(dscores_back, b2) + dot3_t((dhigh[...], dlow[...]), entering2)
        both = per_head(sums[...], expand)
        grad_rate = summed_by(upper.astype(BF16), both[CHUNK:]) + flux[0:1, :]
        flux[...] = rows8(grad_rate[0:1, :])
        rate_of = jnp.exp(head_ref[1:2, :])
        grad_step = both[:CHUNK] - rate_of * grad_rate
        grad_raw = grad_step * sigmoid(step_ref[here, :] + head_ref[0:1, :])
        hacc_ref[0:8, :] += fold8(grad_raw)
        hacc_ref[8:16, :] += fold8(-rate_of * jnp.where(lax.broadcasted_iota(I32, sc.shape, 1) < HALF, sc, 0.0) * grad_rate)
        gp_ref[here, 2 * channels :] = grad_raw.astype(BF16)

    @pl.when(c == blocks - 1)
    def _():
        first_ref[...] = ge[0:8, :]


def pair_back_kernel(
    meta_ref, raw_ref, halo_ref, g_ref, taps_ref, bias_ref, out_ref, tail_ref, first_ref, acc_ref, xe, ge
):
    length, channels = raw_ref.shape

    @pl.when(pl.program_id(0) == 0)
    def _():
        acc_ref[...] = jnp.zeros_like(acc_ref)

    xe[0:8, :] = halo_ref[...]
    xe[8 : 8 + length, :] = raw_ref[...]
    ge[length : length + 8, :] = jnp.zeros((8, channels), F32)
    for at in range(0, length, CHUNK):
        here = slice(at, at + CHUNK)
        for half in range(2):
            lanes = slice(half * STATE, (half + 1) * STATE)
            p = conv(xe, taps_ref, bias_ref, at, CHUNK, lanes)
            sig = sigmoid(p)
            grad_p = g_ref[here, lanes] * (sig * (1.0 + p * (1.0 - sig)))
            ge[here, lanes] = grad_p
            for k in range(CONV):
                acc_ref[8 * k : 8 * k + 8, lanes] += fold8(grad_p * xe[at + 5 + k : at + 5 + k + CHUNK, lanes])
            acc_ref[32:40, lanes] += fold8(grad_p)
    for at in range(0, length, CHUNK):
        for lanes in (slice(0, STATE), slice(STATE, 2 * STATE)):
            raw = conv_back(ge, taps_ref, at, CHUNK, lanes)
            out_ref[at : at + CHUNK, lanes] = raw.astype(BF16)
            if at == length - CHUNK:
                tail_ref[:, lanes] = raw[CHUNK - 8 :, :]
    first_ref[...] = ge[0:8, :]


def finish_kernel(meta_ref, gn_ref, u_ref, branch_ref, gbc_ref, weight_ref, gain_ref, *refs):
    out_ref, acc_ref = refs[-2:]

    @pl.when((pl.program_id(1) == 0) & (pl.program_id(0) == 0))
    def _():
        acc_ref[...] = jnp.zeros_like(acc_ref)

    u = u_ref[...].astype(F32)
    scale = lax.rsqrt(jnp.mean(u * u, axis=-1, keepdims=True) + EPSILON)
    grad = gn_ref[...] + mm(gbc_ref[...], weight_ref[...], 1, 1)
    normal = u * scale
    acc_ref[...] += fold8(grad * normal)
    w = grad * gain_ref[...]
    pull = scale * jnp.mean(w * normal, axis=-1, keepdims=True)
    out_ref[...] = scale * w - normal * pull + branch_ref[...].astype(F32)


def place_kernel(meta_ref, own_ref, got_ref, *refs, takes_at):
    out_ref = refs[-1]
    takes = meta_ref[takes_at] == 1

    @pl.when(takes)
    def _():
        out_ref[...] = got_ref[...]

    @pl.when(jnp.logical_not(takes))
    def _():
        out_ref[...] = own_ref[...]


SHAPE = jax.ShapeDtypeStruct


def whole(shape):
    return pl.BlockSpec(shape, lambda s, c, meta: (0,) * len(shape))


def per_seq(rows, width):
    return pl.BlockSpec((None, rows, width), lambda s, c, meta: (s, 0, 0))


def forward_rows(width, column):
    return pl.BlockSpec((None, ROWS, width), lambda s, c, meta: (s, c, column))


def constants(lengths, step_bias, decay_log, skip_gain, out_gain, slots):
    seqs, channels = lengths.shape[0], out_gain.shape[0]
    row = lambda value: value[None]
    smem = pl.BlockSpec(memory_space=pltpu.SMEM)
    vmem = pl.BlockSpec(memory_space=pltpu.VMEM)
    return pl.pallas_call(
        functools.partial(constants_kernel, slots=slots),
        in_specs=[smem] + [vmem] * 4,
        out_specs=[smem, vmem, vmem, vmem],
        out_shape=[
            SHAPE((2 * seqs + 1,), jnp.int32), SHAPE((8, LANES), F32), SHAPE((8, channels), F32),
            SHAPE((LANES, channels), BF16),
        ],
        name="constants",
    )(lengths, row(step_bias), row(decay_log), row(skip_gain), row(out_gain))


def project(order, meta, residual_in, cotangent, gain, gate, x, step, out, first, count):
    seqs, slots, width = residual_in.shape
    channels = gate.shape[1]
    rows = 256
    placed = pl.BlockSpec((None, rows, width), lambda s, c, meta: (meta[s + first], c, 0))
    plain = lambda wide: pl.BlockSpec((None, rows, wide), lambda s, c, meta: (s, c, 0))
    wide = 2 * channels + LANES
    return order.call(
        functools.partial(project_kernel, first=first),
        (residual_in, cotangent, gain, gate, x, step, out),
        meta=meta,
        grid=(count, slots // rows),
        in_specs=[placed, placed] + [whole(a.shape) for a in (gain, gate, x, step, out)],
        out_specs=[plain(width), plain(width), plain(wide), plain(channels)],
        out_shape=[
            SHAPE((count, slots, width), BF16), SHAPE((count, slots, width), BF16),
            SHAPE((count, slots, wide), F32), SHAPE((count, slots, channels), F32),
        ],
        flops=2 * count * slots * width * (wide + channels),
        moved=count * slots * (width * 8 + wide * 4),
        name="project",
    )


def edge_halos(order, meta, before, gain, x, pair):
    seqs = before.shape[0]
    operands = (before, gain, x, pair)
    shapes = [(seqs, 8, x.shape[1]), (seqs, 8, pair.shape[1])]
    return order.call(
        edge_kernel,
        operands,
        meta=meta,
        grid=(1, 1),
        in_specs=[whole(a.shape) for a in operands],
        out_specs=[whole(a) for a in shapes],
        out_shape=[SHAPE(a, F32) for a in shapes],
        flops=1e8,
        moved=4e6,
        name="edge_halos",
    )


def local_states(order, meta, proj, normed, pair, halo_x, halo_bc, taps, bias, btaps, bbias, head, first, channels):
    count, slots, _ = proj.shape
    placed = lambda width: pl.BlockSpec((None, 8, width), lambda s, c, meta: (meta[first + s], 0, 0))
    return order.call(
        local_state_kernel,
        (proj, halo_x, normed, pair, halo_bc, proj, taps, bias, btaps, bbias, head),
        meta=meta,
        grid=(count, slots // ROWS),
        in_specs=[
            forward_rows(channels, 1), placed(channels), forward_rows(normed.shape[2], 0), whole(pair.shape),
            placed(2 * STATE),
            forward_rows(LANES, 2 * channels // LANES), whole(taps.shape), whole(bias.shape), whole(btaps.shape),
            whole(bbias.shape), whole(head.shape),
        ],
        out_specs=[
            forward_rows(channels, 0), forward_rows(2 * STATE, 0), forward_rows(2 * STATE, 0),
            forward_rows(LANES, 0), per_seq(STATE + 8, channels),
        ],
        out_shape=[
            SHAPE((count, slots, channels), F32), SHAPE((count, slots, 2 * STATE), F32),
            SHAPE((count, slots, 2 * STATE), F32),
            SHAPE((count, slots, LANES), F32), SHAPE((count, STATE + 8, channels), F32),
        ],
        scratch=[
            pltpu.VMEM((ROWS + 8, channels), F32), pltpu.VMEM((ROWS + 8, 2 * STATE), F32),
            pltpu.VMEM((STATE, channels), F32), pltpu.VMEM((8, LANES), F32),
        ],
        flops=count * 4e9,
        moved=count * slots * channels * 8,
        name="local_states",
    )


def mix(order, meta, xs, bcs, sc, start, proj, grad_hidden, chan):
    count, slots, channels = xs.shape
    chunks = slots // CHUNK
    return order.call(
        mix_kernel,
        (xs, bcs, sc, start, proj, grad_hidden, chan),
        meta=meta,
        grid=(count, slots // ROWS),
        in_specs=[
            forward_rows(channels, 0), forward_rows(2 * STATE, 0), forward_rows(LANES, 0),
            per_seq(STATE, channels),
            forward_rows(channels, 0), forward_rows(channels, 0), whole(chan.shape),
        ],
        out_specs=[
            forward_rows(channels, 0), pl.BlockSpec((None, 8, ROWS), lambda s, c, meta: (s, 0, c)),
            pl.BlockSpec((None, ROWS // CHUNK, STATE, channels), lambda s, c, meta: (s, c, 0, 0)),
            per_seq(STATE, channels),
        ],
        out_shape=[
            SHAPE((count, slots, channels), F32), SHAPE((count, 8, slots), F32),
            SHAPE((count, chunks, STATE, channels), F32), SHAPE((count, STATE, channels), F32),
        ],
        scratch=[pltpu.VMEM((STATE, channels), F32)],
        flops=count * 6e9,
        moved=count * slots * channels * 20,
        name="mix",
    )


def gate_back(order, meta, mixed, proj, grad_hidden, rows, bcs, sc, chan):
    count, slots, channels = mixed.shape
    chunks = slots // ROWS
    row = lambda width, column: pl.BlockSpec(
        (None, ROWS, width), lambda s, c, meta: (s, chunks - 1 - c, column)
    )
    return order.call(
        gate_back_kernel,
        (mixed, proj, grad_hidden, rows, bcs, sc, chan),
        meta=meta,
        grid=(count, chunks),
        in_specs=[
            row(channels, 0), row(channels, 0), row(channels, 0),
            pl.BlockSpec((None, 8, ROWS), lambda s, c, meta: (s, 0, chunks - 1 - c)), row(2 * STATE, 0),
            row(LANES, 0), whole(chan.shape),
        ],
        out_specs=[
            row(channels, 0), row(channels, 0), row(channels, 0), per_seq(STATE + 8, channels),
            whole((8, channels)), whole((8, channels)),
        ],
        out_shape=[
            SHAPE((count, slots, channels), BF16), SHAPE((count, slots, channels), BF16),
            SHAPE((count, slots, channels), F32), SHAPE((count, STATE + 8, channels), F32),
            SHAPE((8, channels), F32), SHAPE((8, channels), F32),
        ],
        scratch=[pltpu.VMEM((STATE, channels), F32), pltpu.VMEM((8, LANES), F32)],
        flops=count * 4e9,
        moved=count * slots * channels * 20,
        name="gate_back",
    )


def state_back(
    order, meta, at, first, proj, halo_x, bcs, sc, dy, mixed, states, final, grad_in, grad_gate, taps, bias, head, chan, expand
):
    _, slots, channels = mixed.shape
    chunks = slots // ROWS
    tiles = ROWS // 8
    row = lambda width, column, s=at: pl.BlockSpec(
        (None, ROWS, width), lambda _, c, meta: (s, chunks - 1 - c, column)
    )
    only = lambda rows, width, s=at: pl.BlockSpec((None, rows, width), lambda _, c, meta: (s, 0, 0))
    before = pl.BlockSpec(
        (None, 8, channels), lambda _, c, meta: (at, jnp.maximum((chunks - 1 - c) * tiles - 1, 0), 1)
    )
    tail = pl.BlockSpec((None, None, 8, channels), lambda _, c, meta: (0, chunks - 1 - c, 0, 0))
    return order.call(
        state_back_kernel,
        (
            proj, proj, halo_x, bcs, sc, proj, dy, mixed, states, final, grad_in, grad_gate, taps, bias, head, chan,
            expand,
        ),
        meta=meta,
        grid=(1, chunks),
        in_specs=[
            row(channels, 1), before,
            pl.BlockSpec((None, 8, channels), lambda _, c, meta: (meta[first + at], 0, 0)),
            row(2 * STATE, 0), row(LANES, 0),
            row(LANES, 2 * channels // LANES), row(channels, 0), row(channels, 0),
            pl.BlockSpec((None, ROWS // CHUNK, STATE, channels), lambda _, c, meta: (at, chunks - 1 - c, 0, 0)),
            only(STATE, channels),
            only(STATE, channels),
            row(channels, 0),
            whole(taps.shape), whole(bias.shape), whole(head.shape), whole(chan.shape), whole(expand.shape),
        ],
        out_specs=[
            row(2 * channels + LANES, 0, 0), row(2 * STATE, 0, 0), tail, only(8, channels, 0),
            whole((48, channels)), whole((16, LANES)),
        ],
        out_shape=[
            SHAPE((1, slots, 2 * channels + LANES), BF16), SHAPE((1, slots, 2 * STATE), F32),
            SHAPE((1, chunks, 8, channels), F32), SHAPE((1, 8, channels), F32),
            SHAPE((48, channels), F32), SHAPE((16, LANES), F32),
        ],
        scratch=[
            pltpu.VMEM((ROWS + 8, channels), F32), pltpu.VMEM((ROWS + 8, channels), F32),
            pltpu.VMEM((STATE, channels), F32), pltpu.VMEM((8, LANES), F32),
            pltpu.VMEM((CHUNK, channels), BF16), pltpu.VMEM((CHUNK, channels), BF16),
            pltpu.VMEM((CHUNK, channels), BF16), pltpu.VMEM((CHUNK, channels), BF16),
            pltpu.VMEM((2 * CHUNK, channels), F32),
        ],
        flops=12e9,
        moved=slots * channels * 24,
        name="state_back",
    )


def pair_back(order, meta, first, raw, halo, grad, taps, bias):
    count, slots, channels = raw.shape
    placed = pl.BlockSpec((None, 8, channels), lambda s, c, meta: (meta[first + s], 0, 0))
    return order.call(
        pair_back_kernel,
        (raw, halo, grad, taps, bias),
        meta=meta,
        grid=(count, 1),
        in_specs=[
            per_seq(slots, channels), placed, per_seq(slots, channels), whole(taps.shape), whole(bias.shape),
        ],
        out_specs=[
            per_seq(slots, channels), per_seq(8, channels), per_seq(8, channels), whole((40, channels)),
        ],
        out_shape=[
            SHAPE((count, slots, channels), BF16), SHAPE((count, 8, channels), F32),
            SHAPE((count, 8, channels), F32), SHAPE((40, channels), F32),
        ],
        scratch=[pltpu.VMEM((slots + 8, channels), F32), pltpu.VMEM((slots + 8, channels), F32)],
        flops=count * 1e9,
        moved=count * slots * channels * 10,
        name="pair_back",
    )


def finish(order, meta, grad_normed, residual_in, branch, gbc, weight, gain, at, local, target):
    seqs, slots, width = residual_in.shape
    rows = 128
    placed = pl.BlockSpec((None, rows, width), lambda s, c, meta: (meta[at], c, 0))
    fixed = lambda where, wide: pl.BlockSpec((None, rows, wide), lambda s, c, meta: (where, c, 0))
    extra = () if target is None else (target,)
    return order.call(
        finish_kernel,
        (grad_normed, residual_in, branch, gbc, weight, gain) + extra,
        meta=meta,
        grid=(1, slots // rows),
        in_specs=[
            fixed(0, width), placed, fixed(local, width), fixed(local, gbc.shape[2]),
            whole(weight.shape), whole(gain.shape),
        ] + [ANYWHERE] * len(extra),
        out_specs=[placed, whole((8, width))],
        out_shape=[SHAPE((seqs, slots, width), F32), SHAPE((8, width), F32)],
        aliases={7: 0} if extra else None,
        flops=1e9,
        moved=slots * width * 14,
        name="finish",
    )


def place(order, meta, own, got, at, seqs, target):
    count, slots, width = own.shape
    rows = 256
    plain = pl.BlockSpec((None, rows, width), lambda s, c, meta: (s, c, 0))
    placed = pl.BlockSpec((None, rows, width), lambda s, c, meta: (meta[at + s], c, 0))
    extra = () if target is None else (target,)
    return order.call(
        functools.partial(place_kernel, takes_at=2 * seqs),
        (own, got) + extra,
        meta=meta,
        grid=(count, slots // rows),
        in_specs=[plain, plain] + [ANYWHERE] * len(extra),
        out_specs=[placed],
        out_shape=[SHAPE((seqs, slots, width), own.dtype)],
        aliases={3: 0} if extra else None,
        flops=1e6,
        moved=count * slots * width * 6,
        name="place",
    )[0]


class Running:
    def __init__(self, order, steps):
        self.order, self.steps, self.value, self.ended = order, steps, None, False
        self.advance()

    def advance(self, times=1):
        for _ in range(times):
            if self.ended:
                return self
            try:
                sent = next(self.steps)
                self.order.before_next(*sent)
            except StopIteration as stop:
                self.value, self.ended = stop.value, True
        return self

    def end(self):
        while not self.ended:
            self.advance()
        return self.value


def line_sum(order, part, axis, finish, choose=True):
    count, mine = lax.axis_size(axis), lax.axis_index(axis)
    if count % 2:
        done = finish(lax.psum(part.astype(F32), axis))
        return done if choose else (done, done)
    middle = count // 2
    send = lambda value, pairs: lax.ppermute(value, axis, pairs)
    plus = lambda a, b: order.tie(a.astype(F32) + b.astype(F32))
    for k in range(middle - 1):
        pairs = [(k, k + 1), (count - 1 - k, count - 2 - k)]
        got = send(part, pairs)
        yield (part,)
        part = plus(part, got).astype(part.dtype)
    got = send(part, [(middle - 1, middle), (middle, middle - 1)])
    yield (part,)
    done = finish(plus(part, got))
    for k in range(middle - 1, 0, -1):
        got = send(done, [(k, k - 1), (count - 1 - k, count - k)])
        yield (done,)
        if k == 1 and not choose:
            return done, got
        takes = (mine == k - 1) | (mine == count - k)
        done = order.tie(jnp.where(takes, got, done))
    return done if choose else (done, done)


def crossed(order, value, axis, join):
    count = lax.axis_size(axis)
    pairs = lambda distance: [(i, (i + distance) % count) for i in range(count)]
    got = [lax.ppermute(value, axis, pairs(distance)) for distance in range(1, count)]
    yield (value,)
    for other in got:
        value = join(value, other)
    return order.tie(value)


def bits_of(axis):
    size = lax.axis_size(axis)
    assert size & (size - 1) == 0
    return [1 << k for k in range(size.bit_length() - 1)]


def flipped(value, axis, bit):
    return lax.ppermute(value, axis, [(i, i ^ bit) for i in range(lax.axis_size(axis))])


def pack(state, decay):
    return jnp.concatenate([state, jnp.broadcast_to(decay, decay.shape[:-2] + (8, decay.shape[-1]))], axis=-2)


def carried(order, payload, axis, backward):
    mine, size = lax.axis_index(axis), lax.axis_size(axis)
    steps = bits_of(axis)
    odd = (mine & 1) == 1
    own = jnp.where(odd, payload[1], payload[0])
    give = jnp.where(odd, payload[0], payload[1])
    got = flipped(give, axis, 1)
    yield (give,)
    is_first = odd if backward else jnp.logical_not(odd)
    one, two = jnp.where(is_first, own, got), jnp.where(is_first, got, own)
    one_decay, two_decay = order.tie(one[STATE : STATE + 1]), order.tie(two[STATE : STATE + 1])
    state = two_decay * one[:STATE] + two[:STATE]
    decay = one_decay * two_decay
    entering, through = jnp.zeros_like(state), jnp.ones_like(decay)
    for bit in steps[1:]:
        later = ((mine & bit) == 0) if backward else ((mine & bit) != 0)
        last = bit == steps[-1]
        pairs = [(i, i ^ bit) for i in range(size) if not last or bool(i & bit) == backward]
        sent = pack(state, decay)
        got = lax.ppermute(sent, axis, pairs)
        yield (sent,)
        got_state, got_decay = got[:STATE], order.tie(got[STATE : STATE + 1])
        through = order.tie(through)
        entering = jnp.where(later, through * got_state + entering, entering)
        through = jnp.where(later, got_decay * through, through)
        if not last:
            state = jnp.where(later, decay * got_state + state, got_decay * state + got_state)
            decay = decay * got_decay
    second = one_decay * entering + one[:STATE]
    mine_now, other_now = jnp.where(is_first, entering, second), jnp.where(is_first, second, entering)
    back = flipped(other_now, axis, 1)
    yield (other_now,)
    return jnp.stack([jnp.where(odd, back, mine_now), jnp.where(odd, mine_now, back)])


def butterfly_sum(value, axis):
    for bit in bits_of(axis):
        value = value + flipped(value, axis, bit)
    return value


def gathered(order, value, axis):
    mine = lax.axis_index(axis)
    for bit in bits_of(axis):
        got = flipped(value, axis, bit)
        yield (value,)
        got = order.tie(got)
        value = jnp.where(
            (mine & bit) == 0, jnp.concatenate([value, got], axis=1), jnp.concatenate([got, value], axis=1)
        )
    return value


def shifted(block, axis, distance):
    devices = range(lax.axis_size(axis))
    route = [(i - distance, i) for i in devices if i - distance in devices]
    return lax.ppermute(block, axis, route)


BRANCH_SCALE = 64.0


def pad_lanes(value, width):
    return jnp.pad(value, [(0, 0)] * (value.ndim - 1) + [(0, width - value.shape[-1])])


def edge_terms(halo, taps):
    ext = jnp.concatenate([jnp.zeros_like(halo), halo], axis=1)
    return sum(taps[CONV - 1 - j] * ext[:, j : j + 8] for j in range(1, CONV))


def per_device(
    residual_in, lengths, norm_gain, gate_projection_weight, head_channels_weight, input_state_pair_weight,
    step_size_weight, x_taps, bc_taps, x_bias, bc_bias, step_bias, decay_log, skip_gain, out_gain,
    output_projection_weight, cotangent,
):
    seqs, slots, width = residual_in.shape
    channels = head_channels_weight.shape[1]
    own = input_state_pair_weight.shape[1]
    heads = step_size_weight.shape[1]
    head_at = lax.axis_index("head")
    count = seqs // GROUPS
    groups = range(GROUPS)
    dot = lambda spec, a, b: jnp.einsum(spec, a, b, preferred_element_type=F32)

    order = Order()
    run = lambda steps: Running(order, steps)

    meta, head, chan, expand = constants(lengths, step_bias, decay_log, skip_gain, out_gain, slots)
    places, limit = meta[:seqs], meta[seqs : 2 * seqs]
    slot = lax.iota(jnp.int32, slots)[:, None]

    before = shifted(residual_in[:, slots - 8 :], "seq", 1)
    pair_gather = run(gathered(order, input_state_pair_weight, "head"))
    taps_gather = run(
        gathered(order, jnp.pad(jnp.concatenate([bc_taps, bc_bias[None]], 0), ((0, 3), (0, 0))), "head")
    )
    step_weight = pad_lanes(step_size_weight, LANES)
    out_weight_t = output_projection_weight.T
    bias = x_bias[None]
    gain_row = norm_gain[None]

    normed, branch_grad, proj, bc_raw, xs, bcs, sc, grad_hidden = ([None] * GROUPS for _ in range(8))
    starts, partials, mixed, states, final, ends = ([None] * GROUPS for _ in range(6))
    hidden, grad_gate, dy, grad_ins, gain_acc, gate_peak = ([None] * GROUPS for _ in range(6))
    branches, sums_of = {}, {}

    def project_of(g):
        normed[g], branch_grad[g], proj[g], grad_hidden[g] = project(
            order, meta, residual_in, cotangent, gain_row, gate_projection_weight, head_channels_weight, step_weight,
            out_weight_t, g * count, count,
        )

    def states_of(g):
        xs[g], bc_raw[g], bcs[g], sc[g], ends[g] = local_states(
            order, meta, proj[g], normed[g], pair_weight, halo_x, halo_bc, x_taps, bias, bc_taps_all, bc_bias_all,
            head, g * count, channels,
        )
        starts[g] = run(carried(order, ends[g], "seq", False))

    def mix_of(g):
        mixed[g], sums, states[g], final[g] = mix(
            order, meta, xs[g], bcs[g], sc[g], starts[g].end(), proj[g], grad_hidden[g], chan
        )
        sums_of[g] = run(crossed(order, sums, "head", lambda a, b: a + b))

    def gate_of(g):
        hidden[g], grad_gate[g], dy[g], grad_end, gain_acc[g], gate_peak[g] = gate_back(
            order, meta, mixed[g], proj[g], grad_hidden[g], sums_of[g].end(), bcs[g], sc[g], chan
        )
        grad_ins[g] = run(carried(order, grad_end, "seq", True))

    def branch_of(s):
        g, i = divmod(s, count)
        branch = (dot("mq,qh->mh", hidden[g][i], output_projection_weight) * BRANCH_SCALE).astype(F16)
        u = lax.dynamic_index_in_dim(residual_in, places[s], 0, keepdims=False)
        done = lambda total: jnp.where(
            slot < limit[s], u.astype(F32) + total * (1.0 / BRANCH_SCALE), 0.0
        ).astype(BF16)
        branches[s] = run(line_sum(order, branch, "head", done, choose=False))

    def result_of(s, target):
        own_rows, got = branches[s].end()
        return place(order, meta, own_rows[None], got[None], s, seqs, target)

    gps, dbcs, tails, edges, accs, haccs = ({} for _ in range(6))
    parts, gbcs, baccs, gain_accs = {}, {}, [], []
    dbc_sums, fixes = {}, {}

    def peaks_of():
        largest = functools.reduce(jnp.maximum, [jnp.max(peak) for peak in gate_peak])
        return run(crossed(order, jnp.full((8, LANES), largest, F32), "head", jnp.maximum))

    def back_of(s):
        g, i = divmod(s, count)
        gps[s], dbcs[s], tails[s], edges[s], accs[s], haccs[s] = state_back(
            order, meta, i, g * count, proj[g], halo_x, bcs[g], sc[g], dy[g], mixed[g], states[g], final[g],
            grad_ins[g].end(), grad_gate[g], x_taps, bias, head, chan, expand,
        )

    def edges_of(g):
        mine = [g * count + i for i in range(count)]
        edge = jnp.concatenate([edges[s] for s in mine])
        fixes[g] = (shifted(edge, "seq", -1), jnp.concatenate([tails[s][:, -1] for s in mine]))
        order.before_next(edge)
        dbc_sums[g] = run(line_sum(order, jnp.concatenate([dbcs[s] for s in mine]), "head", lambda total: total))

    def fix_of(g):
        got, tail = fixes[g]
        fixed = order.tie(tail + edge_terms(got, x_taps)).astype(BF16)
        for i in range(count):
            s = g * count + i
            gps[s] = lax.dynamic_update_slice(gps[s][0], fixed[i], (slots - 8, channels))

    def part_of(s):
        part = (dot("gl,ol->go", gps[s], weight) * scale[0]).astype(F16)
        parts[s] = run(line_sum(order, part, "head", lambda total: total.astype(F16)))

    def pair_of(g):
        gbc, btail, bedge, bacc = pair_back(
            order, meta, g * count, bc_raw[g], halo_bc, dbc_sums[g].end(), bc_taps_all, bc_bias_all
        )
        baccs.append(bacc)
        gbcs[g] = (gbc, btail, shifted(bedge, "seq", -1))
        order.before_next(bedge)

    def pair_fix(g):
        gbc, btail, got = gbcs[g]
        fixed = order.tie(btail + edge_terms(got, bc_taps_all)).astype(BF16)
        gbcs[g] = lax.dynamic_update_slice(gbc, fixed, (0, slots - 8, 0))

    def finish_of(s, target):
        g, i = divmod(s, count)
        total = parts[s].end().astype(F32) * scale[1]
        target, gain = finish(
            order, meta, total[None], residual_in, branch_grad[g], gbcs[g], pair_weight, gain_row, s, i, target
        )
        gain_accs.append(gain)
        return target

    add = lambda terms: functools.reduce(lambda a, b: a + b, terms)
    tied_dots = lambda spec, pairs: order.tie(add([dot(spec, a, b) for a, b in pairs]))
    project_of(0)
    pair_gather.advance()
    taps_gather.advance()
    project_of(1)
    pair_weight = pair_gather.end()
    bc_taps_all, bc_bias_all = taps_gather.end()[:CONV], taps_gather.end()[CONV : CONV + 1]
    halo_x, halo_bc = edge_halos(order, meta, before, gain_row, head_channels_weight, pair_weight)
    states_of(0)
    order.fence()
    weight = jnp.concatenate([gate_projection_weight, head_channels_weight, order.tie(step_weight)], axis=1)
    order.before_next(weight)
    starts[0].advance()
    states_of(1)
    starts[0].advance()
    order.fence()
    starts[1].advance()
    order.fence()
    starts[0].advance()
    starts[1].advance()
    mix_of(0)
    starts[1].advance()
    mix_of(1)
    gate_of(0)
    branch_of(0)
    order.fence()
    grad_ins[0].advance()
    gate_of(1)
    grad_ins[0].advance()
    order.fence()
    branch_of(1)
    grad_ins[1].advance()
    order.fence()
    out_grad = tied_dots("yfx,yfw->xw", [(hidden[g], branch_grad[g]) for g in groups])
    order.before_next(out_grad)
    order.fence()
    grad_ins[0].advance()
    grad_ins[1].advance()
    branch_of(2)
    peak = peaks_of()
    back_of(0)
    grad_ins[1].advance()
    branches[0].advance()
    back_of(1)
    edges_of(0)
    branch_of(3)
    gate_grad = tied_dots("wji,wjr->ir", [(normed[g], grad_gate[g]) for g in groups])
    early = lax.psum((out_grad, gate_grad, order.tie(jnp.zeros((8, LANES), F32))), "seq")
    branches[1].advance()
    branches[0].advance()
    back_of(2)
    peak = jnp.maximum(peak.end()[0, 0], 1e-30)
    scale = 0.5 / peak, 2.0 * peak
    fix_of(0)
    part_of(0)
    branches[2].advance()
    branches[1].advance()
    back_of(3)
    edges_of(1)
    dbc_sums[0].advance()
    result = result_of(0, None)
    branches[3].advance()
    branches[2].advance()
    part_of(1)
    dbc_sums[0].advance()
    fix_of(1)
    part_of(2)
    result = result_of(1, result)
    branches[3].advance()
    parts[0].advance()
    pair_of(0)
    pair_fix(0)
    result = result_of(2, result)
    part_of(3)
    order.fence()
    grad_x_weight = tied_dots(
        "ji,jr->ir", [(normed[s // count][s % count], gps[s][..., channels : 2 * channels]) for s in range(seqs)]
    )
    grad_step_weight = tied_dots(
        "ji,jr->ir", [(normed[s // count][s % count], gps[s][..., 2 * channels :]) for s in range(seqs)]
    )
    order.before_next(grad_x_weight, grad_step_weight)
    order.fence()
    dbc_sums[1].advance()
    parts[1].advance()
    parts[0].advance()
    result = result_of(3, result)
    zero = order.tie(jnp.zeros((8, LANES), F32)) + jnp.clip(early[0][0, 0] + early[1][0, 0], -1.0, 1.0) * 0.0
    late = lax.psum((grad_x_weight, grad_step_weight, zero), "seq")
    parts[2].advance()
    parts[1].advance()
    dbc_sums[1].advance()
    grad_input = finish_of(0, None)
    parts[3].advance()
    parts[2].advance()
    pair_of(1)
    pair_fix(1)
    grad_pair = add(dot("wji,wjr->ir", normed[g], gbcs[g]) for g in groups)
    grad_own = lax.dynamic_slice(grad_pair, (0, head_at * own), (width, own))
    grad_input = finish_of(1, grad_input)
    parts[3].advance()
    grad_input = finish_of(2, grad_input)
    grad_input = finish_of(3, grad_input)
    acc = jnp.sum(add(accs.values()).reshape(6, 8, channels), axis=1)
    acc = jnp.concatenate([acc, jnp.sum(add(gain_acc), axis=0)[None]], axis=0)
    hacc = jnp.sum(add(haccs.values()).reshape(2, 8, LANES), axis=1)
    bacc = jnp.sum(add(baccs).reshape(5, 8, 2 * STATE), axis=1)
    flat = jnp.concatenate([acc.reshape(-1), hacc.reshape(-1), bacc.reshape(-1), grad_own.reshape(-1)])
    flat = butterfly_sum(flat.reshape(-1, LANES), "seq").reshape(-1)
    ends_at = [acc.size, acc.size + hacc.size, acc.size + hacc.size + bacc.size]
    acc, hacc, bacc, grad_own = (
        piece.reshape(like.shape) for piece, like in zip(jnp.split(flat, ends_at), (acc, hacc, bacc, grad_own))
    )
    bacc = lax.dynamic_slice(bacc, (0, head_at * own), (5, own))
    gain = butterfly_sum(jnp.sum(add(gain_accs), axis=0).reshape(-1, LANES), "seq").reshape(-1)
    return (
        result,
        grad_input,
        gain,
        early[1],
        late[0],
        grad_own,
        late[1][:, :heads],
        acc[:CONV],
        bacc[:CONV],
        acc[CONV],
        bacc[CONV],
        hacc[0, :heads],
        hacc[1, :heads],
        jnp.sum(acc[5].reshape(heads, HEAD_DIM), axis=1),
        acc[6],
        early[0],
    )


def solution(mesh):
    return jax.shard_map(
        per_device,
        mesh=mesh,
        in_specs=(
            P(None, "seq", None), P(), P(), P(None, "head"), P(None, "head"), P(None, "head"), P(None, "head"),
            P(None, "head"), P(None, "head"), P("head"), P("head"), P("head"), P("head"), P("head"), P("head"),
            P("head", None), P(None, "seq", None),
        ),
        out_specs=(
            P(None, "seq", None), P(None, "seq", None), P(), P(None, "head"), P(None, "head"), P(None, "head"),
            P(None, "head"), P(None, "head"), P(None, "head"), P("head"), P("head"), P("head"), P("head"),
            P("head"), P("head"), P("head", None),
        ),
        check_vma=False,
    )
```

time: 2100 us -> 912 us (0.43)
  waiting for transfers between devices: 1070 us -> 151 us
  matrix products: 332 us -> 86.1 us
  Pallas kernels: 0 us -> 245 us
  local copies, waits for them, and re-layouts: 295 us -> 84.2 us
  other arithmetic: 305 us -> 178 us
  starting transfers between devices: 4.12 us -> 124 us
  blocking collectives: 55 us -> 0 us
    psum x2 -> x1, waiting for transfers between devices: 991 us -> 0.01 us  [per_device(): lax.psum((out_grad, gate_grad, order.tie(jnp.zeros((8, LANES), F32))), 's...]
    dot_general x33 -> x22, matrix products: 332 us -> 86.1 us  [per_device(): dot = lambda spec, a, b: jnp.einsum(spec, a, b, preferred_element_type=F32)]
    pallas_call x0 -> x33, Pallas kernels: none -> 245 us  [the longest x23 238 us: call(): pl.pallas_call(body, grid_spec=pltpu.PrefetchScalarGridSpec(num_scalar_pr...]
    ppermute x0 -> x65, waiting for transfers between devices: none -> 151 us  [the longest x30 81.7 us: line_sum(): send = lambda value, pairs: lax.ppermute(value, axis, pairs)]
    ppermute x0 -> x65, starting transfers between devices: none -> 117 us  [the longest x30 81.1 us: line_sum(): send = lambda value, pairs: lax.ppermute(value, axis, pairs)]
    reduce_sum x18 -> x6, other arithmetic: 94.3 us -> 3.18 us  [the longest x1 0.97 us: per_device(): acc = jnp.sum(add(accs.values()).reshape(6, 8, channels), axis=1)]
    all_gather x3 -> x0, waiting for transfers between devices: 81.5 us -> none  [the longest x2 74.9 us: carried_in(): pieces = jax.tree.map(lambda part: lax.all_gather(part, axis), value)]
    convert_element_type x1 -> x17, other arithmetic: 0.73 us -> 70.8 us  [the longest x8 33.8 us: line_sum(): part = plus(part, got).astype(part.dtype)]
  transfers between devices with their start and end apart: 8 -> 71, of which waited for: 5 -> 16; matrix products, arithmetic and copies ran while one was open for 11% -> 37% of each run, Pallas kernels for 0% -> 25%
where the time goes in v1:
time: 912 us; the launch traced here: 897 us
  Pallas kernels  245 us (27%)
  other arithmetic  178 us (20%)
  waiting for transfers between devices  151 us (17%)
  starting transfers between devices  124 us (14%)
  matrix products  86.1 us (9%)
  local copies, waits for them, and re-layouts  84.2 us (9%)
  between operations  28.5 us (3%)
    pallas_call x23, Pallas kernels, call(): pl.pallas_call(body, grid_spec=pltpu.PrefetchScalarGridSpec(num_scalar_pr...  238 us
    dot_general x22, matrix products, per_device(): dot = lambda spec, a, b: jnp.einsum(spec, a, b, preferred_element_type=F32)  86.1 us
    ppermute x30, waiting for transfers between devices, line_sum(): send = lambda value, pairs: lax.ppermute(value, axis, pairs)  81.7 us
    ppermute x30, starting transfers between devices, line_sum(): send = lambda value, pairs: lax.ppermute(value, axis, pairs)  81.1 us
    ppermute x18, waiting for transfers between devices, flipped(): lax.ppermute(value, axis, [(i, i ^ bit) for i in range(lax.axis_size(axis...  52.3 us
    slice x33, local copies, waits for them, and re-layouts, tie(): lax.slice(self.now, at, (at[0] + 1, at[1] + 1)).reshape(())  38.4 us
    add x22, other arithmetic, tie(): value + lax.slice(self.now, at, (at[0] + 1, at[1] + 1)).reshape(()).astyp...  36.5 us
    convert_element_type x8, other arithmetic, line_sum(): part = plus(part, got).astype(part.dtype)  33.8 us
  transfers between devices with their start and end apart: 71, of which 16 were waited for; matrix products, arithmetic and copies ran while one was open for 37% of the time, Pallas kernels for 25%

profile of v1, /device:TPU:0, one launch (start us, length us, event | category | flops | bytes accessed | tf_op | source)
XLA Modules:
  0.0 897.1 jit_solution(4551758246257051818)
XLA Ops:
  26.6 15.4 %project.2 = (bf16[2,512,1536]{2,1,0:T(8,128)(2,1)}, bf16[2,512,1536]{2,1,0:T(8,128)(2,1)}, f32[2,512,1664]{2,1,0:T(8,128)}, f32[2,512,768]{2,1,0:T(8,128)}, f32[8,128]{1,0:T(8,128)}) custom-call(s32[9]{0:T(128)} %get-tuple-element.126.meta_ref, bf16[4,512,1536]{2,1,0:T(8,128)(2,1)} %refs_1_.11, bf16[4,512,1536]{2,1,0:T(8,128)(2,1)} %refs_1_.7, ...), custom_call_target="tpu_custom_call" | custom-call | flops 7650410496 | bytes 19398656 | tf_op jit(solution)/shard_map/project/pallas_call | solution.py:175
  53.1 15.4 %project.3 = (bf16[2,512,1536]{2,1,0:T(8,128)(2,1)}, bf16[2,512,1536]{2,1,0:T(8,128)(2,1)}, f32[2,512,1664]{2,1,0:T(8,128)}, f32[2,512,768]{2,1,0:T(8,128)}, f32[8,128]{1,0:T(8,128)}) custom-call(s32[9]{0:T(128)} %get-tuple-element.126.meta_ref, bf16[4,512,1536]{2,1,0:T(8,128)(2,1)} %refs_1_.11, bf16[4,512,1536]{2,1,0:T(8,128)(2,1)} %refs_1_.7, ...), custom_call_target="tpu_custom_call" | custom-call | flops 7650410496 | bytes 19398656 | tf_op jit(solution)/shard_map/project/pallas_call | solution.py:175
  73.8 15.1 %collective-permute-done.3 = bf16[1536,128]{1,0:T(8,128)(2,1)S(1)} collective-permute-done((bf16[1536,128]{1,0:T(8,128)(2,1)S(1)}, bf16[1536,128]{1,0:T(8,128)(2,1)S(1)}, u32[]{:S(2)}, u32[]{:S(2)}) %collective-permute-start.3) | collective-permute-done | bytes 393248 | tf_op jit(solution)/shard_map/ppermute | solution.py:967
  95.3 12.9 %local_states.2 = (f32[2,512,768]{2,1,0:T(8,128)}, f32[2,512,256]{2,1,0:T(8,128)}, f32[2,512,256]{2,1,0:T(8,128)}, f32[2,512,128]{2,1,0:T(8,128)}, f32[2,136,768]{2,1,0:T(8,128)}, /*index=5*/f32[8,128]{1,0:T(8,128)}) custom-call(s32[9]{0:T(128)} %get-tuple-element.126.meta_ref, f32[2,512,1664]{2,1,0:T(8,128)} %get-tuple-element.134.refs_0_.refs_5_.refs_4_.refs_1_, ...), custom_call_target="tpu_custom_call" | custom-call | flops 8000000000 | bytes 6291456 | tf_op jit(solution)/shard_map/local_states/pallas_call | solution.py:175
  123.2 12.9 %local_states.3 = (f32[2,512,768]{2,1,0:T(8,128)}, f32[2,512,256]{2,1,0:T(8,128)}, f32[2,512,256]{2,1,0:T(8,128)}, f32[2,512,128]{2,1,0:T(8,128)}, f32[2,136,768]{2,1,0:T(8,128)}, /*index=5*/f32[8,128]{1,0:T(8,128)}) custom-call(s32[9]{0:T(128)} %get-tuple-element.126.meta_ref, f32[2,512,1664]{2,1,0:T(8,128)} %get-tuple-element.128.refs_0_.refs_5_.refs_4_.refs_1_, ...), custom_call_target="tpu_custom_call" | custom-call | flops 8000000000 | bytes 6291456 | tf_op jit(solution)/shard_map/local_states/pallas_call | solution.py:175
  154.3 6.4 collective-permute-done.8
  164.1 13.2 %mix.2 = (f32[2,512,768]{2,1,0:T(8,128)}, f32[2,8,512]{2,1,0:T(8,128)}, f32[2,4,128,768]{3,2,1,0:T(8,128)}, f32[2,128,768]{2,1,0:T(8,128)}, f32[8,128]{1,0:T(8,128)}) custom-call(s32[9]{0:T(128)} %get-tuple-element.126.meta_ref, f32[2,512,768]{2,1,0:T(8,128)} %get-tuple-element.144.refs_0_, f32[2,512,256]{2,1,0:T(8,128)} %get-tuple-element.145.refs_1_.refs_4_.refs_3_, ...), custom_call_target="tpu_custom_call" | custom-call | flops 12000000000 | bytes 15728640 | tf_op jit(solution)/shard_map/mix/pallas_call | solution.py:175
  195.7 13.2 %mix.3 = (f32[2,512,768]{2,1,0:T(8,128)}, f32[2,8,512]{2,1,0:T(8,128)}, f32[2,4,128,768]{3,2,1,0:T(8,128)}, f32[2,128,768]{2,1,0:T(8,128)}, f32[8,128]{1,0:T(8,128)}) custom-call(s32[9]{0:T(128)} %get-tuple-element.126.meta_ref, f32[2,512,768]{2,1,0:T(8,128)} %get-tuple-element.139.refs_0_, f32[2,512,256]{2,1,0:T(8,128)} %get-tuple-element.140.refs_1_.refs_4_.refs_3_, ...), custom_call_target="tpu_custom_call" | custom-call | flops 12000000000 | bytes 15728640 | tf_op jit(solution)/shard_map/mix/pallas_call | solution.py:175
  216.5 11.7 %gate_back.2 = (bf16[2,512,768]{2,1,0:T(8,128)(2,1)}, bf16[2,512,768]{2,1,0:T(8,128)(2,1)}, f32[2,512,768]{2,1,0:T(8,128)}, f32[2,136,768]{2,1,0:T(8,128)}, f32[...) custom-call(s32[9]{0:T(128)} %get-tuple-element.126.meta_ref, ...), custom_call_target="tpu_custom_call" | custom-call | flops 8000000000 | bytes 15728640 | tf_op jit(solution)/shard_map/gate_back/pallas_call | solution.py:175
  259.2 11.8 %gate_back.3 = (bf16[2,512,768]{2,1,0:T(8,128)(2,1)}, bf16[2,512,768]{2,1,0:T(8,128)(2,1)}, f32[2,512,768]{2,1,0:T(8,128)}, f32[2,136,768]{2,1,0:T(8,128)}, f32[...) custom-call(s32[9]{0:T(128)} %get-tuple-element.126.meta_ref, ...), custom_call_target="tpu_custom_call" | custom-call | flops 8000000000 | bytes 15728640 | tf_op jit(solution)/shard_map/gate_back/pallas_call | solution.py:175
  297.9 7.1 fusion.1.refs_0_
  319.4 18.9 %state_back.4 = (bf16[1,512,1664]{2,1,0:T(8,128)(2,1)}, f32[1,512,256]{2,1,0:T(8,128)}, f32[1,2,8,768]{3,2,1,0:T(8,128)}, f32[1,8,768]{2,1,0:T(8,128)}, f32[48,7...) custom-call(s32[9]{0:T(128)} %get-tuple-element.126.meta_ref, ...), custom_call_target="tpu_custom_call" | custom-call | flops 12000000000 | bytes 9437184 | tf_op jit(solution)/shard_map/state_back/pallas_call | solution.py:175
  350.2 9.6 %collective-permute-done.28 = f32[136,768]{1,0:T(8,128)S(1)} collective-permute-done((f32[136,768]{1,0:T(8,128)S(1)}, f32[136,768]{1,0:T(8,128)S(1)}, u32[]{:S(2)}, u32[]{:S(2)}) %collective-permute-start.28) | collective-permute-done | bytes 417824 | tf_op jit(solution)/shard_map/ppermute | solution.py:993
  363.6 19.0 %state_back.5 = (bf16[1,512,1664]{2,1,0:T(8,128)(2,1)}, f32[1,512,256]{2,1,0:T(8,128)}, f32[1,2,8,768]{3,2,1,0:T(8,128)}, f32[1,8,768]{2,1,0:T(8,128)}, f32[48,7...) custom-call(s32[9]{0:T(128)} %get-tuple-element.126.meta_ref, ...), custom_call_target="tpu_custom_call" | custom-call | flops 12000000000 | bytes 9437184 | tf_op jit(solution)/shard_map/state_back/pallas_call | solution.py:175
  384.0 7.3 fusion
  409.9 18.9 %state_back.6 = (bf16[1,512,1664]{2,1,0:T(8,128)(2,1)}, f32[1,512,256]{2,1,0:T(8,128)}, f32[1,2,8,768]{3,2,1,0:T(8,128)}, f32[1,8,768]{2,1,0:T(8,128)}, f32[48,7...) custom-call(s32[9]{0:T(128)} %get-tuple-element.126.meta_ref, ...), custom_call_target="tpu_custom_call" | custom-call | flops 12000000000 | bytes 9437184 | tf_op jit(solution)/shard_map/state_back/pallas_call | solution.py:175
  454.4 18.9 %state_back.7 = (bf16[1,512,1664]{2,1,0:T(8,128)(2,1)}, f32[1,512,256]{2,1,0:T(8,128)}, f32[1,2,8,768]{3,2,1,0:T(8,128)}, f32[1,8,768]{2,1,0:T(8,128)}, f32[48,7...) custom-call(s32[9]{0:T(128)} %get-tuple-element.126.meta_ref, ...), custom_call_target="tpu_custom_call" | custom-call | flops 12000000000 | bytes 9437184 | tf_op jit(solution)/shard_map/state_back/pallas_call | solution.py:175
  479.7 11.4 %collective-permute-done.33 = f32[2,512,256]{2,1,0:T(8,128)} collective-permute-done((f32[2,512,256]{2,1,0:T(8,128)}, f32[2,512,256]{2,1,0:T(8,128)}, u32[]{:S(2)}, u32[]{:S(2)}) %collective-permute-start.33) | collective-permute-done | bytes 1048608 | tf_op jit(solution)/shard_map/ppermute | solution.py:930
  503.6 7.9 collective-permute-start.42
  544.7 6.7 collective-permute-start.49
  574.4 6.8 collective-permute-start.60
  618.2 9.9 %add_add_fusion.refs_0_ = f32[1536,768]{1,0:T(8,128)} fusion(f32[1536,768]{1,0:T(8,128)} %fusion.22, f32[1536,768]{1,0:T(8,128)} %fusion.29, f32[1536,768]{1,0:T(8,128)} %fusion.25, f32[]{:T(128)} %bitcast.104, bf16[2,512,1536]{2,1,0:T(8,128)(2,1)S(1)} %copy-done.1, bf16[512,1664]{1,0:T(8,128)(2,1)} %get-tuple-element.328), kind=kOutput, calls=%fused_computation.5 | convolution fusion | flops 1212678144 | bytes 21234176 | tf_op jit(solution)/shard_map/ji,jr->ir/dot_general | solution.py:1057
  633.8 18.9 %collective-permute-done.55 = f16[512,1536]{1,0:T(8,128)(2,1)} collective-permute-done((f16[512,1536]{1,0:T(8,128)(2,1)}, f16[512,1536]{1,0:T(8,128)(2,1)}, u32[]{:S(2)}, u32[]{:S(2)}) %collective-permute-start.55) | collective-permute-done | bytes 1572896 | tf_op jit(solution)/shard_map/ppermute | solution.py:930
  674.9 15.1 %collective-permute-done.39 = bf16[512,1536]{1,0:T(8,128)(2,1)S(1)} collective-permute-done((bf16[512,1536]{1,0:T(8,128)(2,1)}, bf16[512,1536]{1,0:T(8,128)(2,1)S(1)}, u32[]{:S(2)}, u32[]{:S(2)}) %collective-permute-start.39) | collective-permute-done | bytes 1572896 | tf_op jit(solution)/shard_map/ppermute | solution.py:930
  714.4 16.2 %collective-permute-done.51 = f16[512,1536]{1,0:T(8,128)(2,1)} collective-permute-done((f16[512,1536]{1,0:T(8,128)(2,1)}, f16[512,1536]{1,0:T(8,128)(2,1)}, u32[]{:S(2)}, u32[]{:S(2)}) %collective-permute-start.51) | collective-permute-done | bytes 1572896 | tf_op jit(solution)/shard_map/ppermute | solution.py:930
  735.0 7.1 finish.4
  743.4 9.7 %collective-permute-done.58 = f32[2,512,256]{2,1,0:T(8,128)} collective-permute-done((f32[2,512,256]{2,1,0:T(8,128)}, f32[2,512,256]{2,1,0:T(8,128)}, u32[]{:S(2)}, u32[]{:S(2)}) %collective-permute-start.58) | collective-permute-done | bytes 1048608 | tf_op jit(solution)/shard_map/ppermute | solution.py:930
  791.2 7.4 finish.5
  804.8 14.7 %collective-permute-done.68 = f32[822,128]{1,0:T(8,128)S(1)} collective-permute-done((f32[822,128]{1,0:T(8,128)S(1)}, f32[822,128]{1,0:T(8,128)S(1)}, u32[]{:S(2)}, u32[]{:S(2)}) %collective-permute-start.68) | collective-permute-done | bytes 420896 | tf_op jit(solution)/shard_map/ppermute | solution.py:967
  820.3 18.3 %collective-permute-done.69 = f32[822,128]{1,0:T(8,128)S(1)} collective-permute-done((f32[822,128]{1,0:T(8,128)S(1)}, f32[822,128]{1,0:T(8,128)S(1)}, u32[]{:S(2)}, u32[]{:S(2)}) %collective-permute-start.69) | collective-permute-done | bytes 420896 | tf_op jit(solution)/shard_map/ppermute | solution.py:967
  843.5 7.1 finish.6
  859.8 7.2 finish.7
  (560 shorter events, 476.8 us)
Async XLA Ops:
  8.3 41.7 %collective-permute-start = (bf16[1536,64]{1,0:T(8,128)(2,1)S(1)}, bf16[1536,64]{1,0:T(8,128)(2,1)S(1)}, u32[]{:S(2)}, u32[]{:S(2)}) collective-permute-start(bf16[1536,64]{1,0:T(8,128)(2,1)S(1)} %copy.56.refs_7_), channel_id=1, source_target_pairs={{0,1},{1,0},{2,3},{3,2},{4,5},{5,4},{6,7},{7,6},{8,9},{9,8},{10,11... | collective-permute-start | bytes 589832 | tf_op jit(solution)/shard_map/ppermute | solution.py:967
  13.2 77.6 %collective-permute-start.2 = (bf16[4,8,1536]{2,1,0:T(8,128)(2,1)S(1)}, bf16[4,8,1536]{2,1,0:T(8,128)(2,1)S(1)}, u32[]{:S(2)}, u32[]{:S(2)}) collective-permute-start(bf16[4,8,1536]{2,1,0:T(8,128)(2,1)S(1)} %slice.545), channel_id=1, source_target_pairs={{0,4},{4,8},{8,12},{12,16},{16,20},{20,24},{24,28},{1,5},{5,9},{9,... | collective-permute-start | bytes 294920 | tf_op jit(solution)/shard_map/ppermute | solution.py:1030
  208.9 41.9 %collective-permute-start.13 = (f32[2,8,512]{2,1,0:T(8,128)}, f32[2,8,512]{2,1,0:T(8,128)S(1)}, u32[]{:S(2)}, u32[]{:S(2)}) collective-permute-start(f32[2,8,512]{2,1,0:T(8,128)} %get-tuple-element.153.refs_7_), channel_id=1, source_target_pairs={{0,1},{1,2},{2,3},{3,0},{4,5},{5,6},{6,7},{7,4},{8,9},{9,10},{10,1... | collective-permute-start | bytes 98312 | tf_op jit(solution)/shard_map/ppermute | solution.py:953
  209.5 43.7 %collective-permute-start.14 = (f32[2,8,512]{2,1,0:T(8,128)}, f32[2,8,512]{2,1,0:T(8,128)S(1)}, u32[]{:S(2)}, u32[]{:S(2)}) collective-permute-start(f32[2,8,512]{2,1,0:T(8,128)} %get-tuple-element.153.refs_7_), channel_id=1, source_target_pairs={{0,2},{1,3},{2,0},{3,1},{4,6},{5,7},{6,4},{7,5},{8,10},{9,11},{10,... | collective-permute-start | bytes 98312 | tf_op jit(solution)/shard_map/ppermute | solution.py:953
  212.3 41.0 %collective-permute-start.15 = (f32[2,8,512]{2,1,0:T(8,128)}, f32[2,8,512]{2,1,0:T(8,128)S(1)}, u32[]{:S(2)}, u32[]{:S(2)}) collective-permute-start(f32[2,8,512]{2,1,0:T(8,128)} %get-tuple-element.153.refs_7_), channel_id=1, source_target_pairs={{0,3},{1,0},{2,1},{3,2},{4,7},{5,4},{6,5},{7,6},{8,11},{9,8},{10,9... | collective-permute-start | bytes 98312 | tf_op jit(solution)/shard_map/ppermute | solution.py:953
  238.3 153.0 %collective-permute-start.31 = (f16[512,1536]{1,0:T(8,128)(2,1)}, f16[512,1536]{1,0:T(8,128)(2,1)}, u32[]{:S(2)}, u32[]{:S(2)}) collective-permute-start(f16[512,1536]{1,0:T(8,128)(2,1)} %fusion.12), channel_id=1, source_target_pairs={{0,1},{3,2},{4,5},{7,6},{8,9},{11,10},{12,13},{15,14},{16,17},{19,... | collective-permute-start | bytes 4718600 | tf_op jit(solution)/shard_map/ppermute | solution.py:930
  250.8 94.3 %collective-permute-start.21 = (f16[512,1536]{1,0:T(8,128)(2,1)}, f16[512,1536]{1,0:T(8,128)(2,1)}, u32[]{:S(2)}, u32[]{:S(2)}) collective-permute-start(f16[512,1536]{1,0:T(8,128)(2,1)} %fusion.11), channel_id=1, source_target_pairs={{0,1},{3,2},{4,5},{7,6},{8,9},{11,10},{12,13},{15,14},{16,17},{19,... | collective-permute-start | bytes 4718600 | tf_op jit(solution)/shard_map/ppermute | solution.py:930
  280.8 149.5 %collective-permute-start.45 = (f32[8,128]{1,0:T(8,128)S(1)}, f32[8,128]{1,0:T(8,128)S(1)}, u32[]{:S(2)}, u32[]{:S(2)}) collective-permute-start(f32[8,128]{1,0:T(8,128)S(1)} %broadcast_in_dim.175.refs_19_), channel_id=1, source_target_pairs={{0,1},{1,2},{2,3},{3,0},{4,5},{5,6},{6,7},{7,4},{8,9},{9,10},{10,1... | collective-permute-start | bytes 12296 | tf_op jit(solution)/shard_map/ppermute | solution.py:953
  309.7 123.0 %collective-permute-start.46 = (f32[8,128]{1,0:T(8,128)S(1)}, f32[8,128]{1,0:T(8,128)S(1)}, u32[]{:S(2)}, u32[]{:S(2)}) collective-permute-start(f32[8,128]{1,0:T(8,128)S(1)} %broadcast_in_dim.175.refs_19_), channel_id=1, source_target_pairs={{0,2},{1,3},{2,0},{3,1},{4,6},{5,7},{6,4},{7,5},{8,10},{9,11},{10,... | collective-permute-start | bytes 12296 | tf_op jit(solution)/shard_map/ppermute | solution.py:953
  317.7 117.2 %collective-permute-start.47 = (f32[8,128]{1,0:T(8,128)S(1)}, f32[8,128]{1,0:T(8,128)S(1)}, u32[]{:S(2)}, u32[]{:S(2)}) collective-permute-start(f32[8,128]{1,0:T(8,128)S(1)} %broadcast_in_dim.175.refs_19_), channel_id=1, source_target_pairs={{0,3},{1,0},{2,1},{3,2},{4,7},{5,4},{6,5},{7,6},{8,11},{9,8},{10,9... | collective-permute-start | bytes 12296 | tf_op jit(solution)/shard_map/ppermute | solution.py:953
  359.7 43.0 %collective-permute-start.27 = (f16[512,1536]{1,0:T(8,128)(2,1)}, f16[512,1536]{1,0:T(8,128)(2,1)}, u32[]{:S(2)}, u32[]{:S(2)}) collective-permute-start(f16[512,1536]{1,0:T(8,128)(2,1)} %add_convert_fusion.11), channel_id=1, source_target_pairs={{1,2},{2,1},{5,6},{6,5},{9,10},{10,9},{13,14},{14,13},{17,18},{18,... | collective-permute-start | bytes 4718600 | tf_op jit(solution)/shard_map/ppermute | solution.py:930
  395.9 45.5 %collective-permute-start.36 = (f16[512,1536]{1,0:T(8,128)(2,1)}, f16[512,1536]{1,0:T(8,128)(2,1)}, u32[]{:S(2)}, u32[]{:S(2)}) collective-permute-start(f16[512,1536]{1,0:T(8,128)(2,1)} %fusion.13), channel_id=1, source_target_pairs={{0,1},{3,2},{4,5},{7,6},{8,9},{11,10},{12,13},{15,14},{16,17},{19,... | collective-permute-start | bytes 4718600 | tf_op jit(solution)/shard_map/ppermute | solution.py:930
  402.7 44.2 %collective-permute-start.32 = (f16[512,1536]{1,0:T(8,128)(2,1)}, f16[512,1536]{1,0:T(8,128)(2,1)}, u32[]{:S(2)}, u32[]{:S(2)}) collective-permute-start(f16[512,1536]{1,0:T(8,128)(2,1)} %add_convert_fusion.10), channel_id=1, source_target_pairs={{1,2},{2,1},{5,6},{6,5},{9,10},{10,9},{13,14},{14,13},{17,18},{18,... | collective-permute-start | bytes 4718600 | tf_op jit(solution)/shard_map/ppermute | solution.py:930
  430.2 114.5 %collective-permute-start.20 = (f16[512,1536]{1,0:T(8,128)(2,1)}, f16[512,1536]{1,0:T(8,128)(2,1)}, u32[]{:S(2)}, u32[]{:S(2)}) collective-permute-start(f16[512,1536]{1,0:T(8,128)(2,1)} %fusion.10), channel_id=1, source_target_pairs={{0,1},{3,2},{4,5},{7,6},{8,9},{11,10},{12,13},{15,14},{16,17},{19,... | collective-permute-start | bytes 4718600 | tf_op jit(solution)/shard_map/ppermute | solution.py:930
  432.6 58.5 %collective-permute-start.33 = (f32[2,512,256]{2,1,0:T(8,128)}, f32[2,512,256]{2,1,0:T(8,128)}, u32[]{:S(2)}, u32[]{:S(2)}) collective-permute-start(f32[2,512,256]{2,1,0:T(8,128)} %copy-done.24), channel_id=1, source_target_pairs={{0,1},{3,2},{4,5},{7,6},{8,9},{11,10},{12,13},{15,14},{16,17},{19,... | collective-permute-start | bytes 3145736 | tf_op jit(solution)/shard_map/ppermute | solution.py:930
  434.9 67.4 %collective-permute-start.43 = (f32[2,8,768]{2,1,0:T(8,128)S(1)}, f32[2,8,768]{2,1,0:T(8,128)S(1)}, u32[]{:S(2)}, u32[]{:S(2)}) collective-permute-start(f32[2,8,768]{2,1,0:T(8,128)S(1)} %copy-done.76), channel_id=1, source_target_pairs={{4,0},{8,4},{12,8},{16,12},{20,16},{24,20},{28,24},{5,1},{9,5},{13... | collective-permute-start | bytes 147464 | tf_op jit(solution)/shard_map/ppermute | solution.py:1030
  441.4 54.3 %collective-permute-start.29 = (bf16[512,1536]{1,0:T(8,128)(2,1)}, bf16[512,1536]{1,0:T(8,128)(2,1)}, u32[]{:S(2)}, u32[]{:S(2)}) collective-permute-start(bf16[512,1536]{1,0:T(8,128)(2,1)} %fusion.7.refs_19_), channel_id=1, source_target_pairs={{1,0},{2,3},{5,4},{6,7},{9,8},{10,11},{13,12},{14,15},{17,16},{18,... | collective-permute-start | bytes 4718600 | tf_op jit(solution)/shard_map/ppermute | solution.py:930
  447.0 114.1 %collective-permute-start.37 = (f16[512,1536]{1,0:T(8,128)(2,1)}, f16[512,1536]{1,0:T(8,128)(2,1)}, u32[]{:S(2)}, u32[]{:S(2)}) collective-permute-start(f16[512,1536]{1,0:T(8,128)(2,1)} %add_convert_fusion.8), channel_id=1, source_target_pairs={{1,2},{2,1},{5,6},{6,5},{9,10},{10,9},{13,14},{14,13},{17,18},{18,... | collective-permute-start | bytes 4718600 | tf_op jit(solution)/shard_map/ppermute | solution.py:930
  502.3 66.0 %collective-permute-start.35 = (bf16[512,1536]{1,0:T(8,128)(2,1)}, bf16[512,1536]{1,0:T(8,128)(2,1)}, u32[]{:S(2)}, u32[]{:S(2)}) collective-permute-start(bf16[512,1536]{1,0:T(8,128)(2,1)} %fusion.5.refs_17_), channel_id=1, source_target_pairs={{1,0},{2,3},{5,4},{6,7},{9,8},{10,11},{13,12},{14,15},{17,16},{18,... | collective-permute-start | bytes 4718600 | tf_op jit(solution)/shard_map/ppermute | solution.py:930
  503.6 155.3 %collective-permute-start.42 = (f32[2,512,256]{2,1,0:T(8,128)}, f32[2,512,256]{2,1,0:T(8,128)}, u32[]{:S(2)}, u32[]{:S(2)}) collective-permute-start(f32[2,512,256]{2,1,0:T(8,128)} %constant_dynamic-update-slice_fusion.6.refs_3_), channel_id=1, source_target_pairs={{0,1},{3,2},{4,5},{7,6},{8,9},{11,10},{12,13},{15,14},{16,17},{19,... | collective-permute-start | bytes 3145736 | tf_op jit(solution)/shard_map/ppermute | solution.py:930
  544.7 40.5 %collective-permute-start.49 = (f16[512,1536]{1,0:T(8,128)(2,1)}, f16[512,1536]{1,0:T(8,128)(2,1)}, u32[]{:S(2)}, u32[]{:S(2)}) collective-permute-start(f16[512,1536]{1,0:T(8,128)(2,1)} %fusion.15), channel_id=1, source_target_pairs={{0,1},{3,2},{4,5},{7,6},{8,9},{11,10},{12,13},{15,14},{16,17},{19,... | collective-permute-start | bytes 4718600 | tf_op jit(solution)/shard_map/ppermute | solution.py:930
  568.2 42.7 %collective-permute-start.40 = (bf16[512,1536]{1,0:T(8,128)(2,1)}, bf16[512,1536]{1,0:T(8,128)(2,1)}, u32[]{:S(2)}, u32[]{:S(2)}) collective-permute-start(bf16[512,1536]{1,0:T(8,128)(2,1)} %fusion.3.refs_3_), channel_id=1, source_target_pairs={{1,0},{2,3},{5,4},{6,7},{9,8},{10,11},{13,12},{14,15},{17,16},{18,... | collective-permute-start | bytes 4718600 | tf_op jit(solution)/shard_map/ppermute | solution.py:930
  574.4 127.6 %collective-permute-start.60 = (f16[512,1536]{1,0:T(8,128)(2,1)}, f16[512,1536]{1,0:T(8,128)(2,1)}, u32[]{:S(2)}, u32[]{:S(2)}) collective-permute-start(f16[512,1536]{1,0:T(8,128)(2,1)} %fusion.17), channel_id=1, source_target_pairs={{0,1},{3,2},{4,5},{7,6},{8,9},{11,10},{12,13},{15,14},{16,17},{19,... | collective-permute-start | bytes 4718600 | tf_op jit(solution)/shard_map/ppermute | solution.py:930
  585.2 67.4 %collective-permute-start.55 = (f16[512,1536]{1,0:T(8,128)(2,1)}, f16[512,1536]{1,0:T(8,128)(2,1)}, u32[]{:S(2)}, u32[]{:S(2)}) collective-permute-start(f16[512,1536]{1,0:T(8,128)(2,1)} %fusion.16), channel_id=1, source_target_pairs={{0,1},{3,2},{4,5},{7,6},{8,9},{11,10},{12,13},{15,14},{16,17},{19,... | collective-permute-start | bytes 4718600 | tf_op jit(solution)/shard_map/ppermute | solution.py:930
  595.0 172.7 %collective-permute-start.48 = (f16[512,1536]{1,0:T(8,128)(2,1)}, f16[512,1536]{1,0:T(8,128)(2,1)}, u32[]{:S(2)}, u32[]{:S(2)}) collective-permute-start(f16[512,1536]{1,0:T(8,128)(2,1)} %fusion.14), channel_id=1, source_target_pairs={{0,1},{3,2},{4,5},{7,6},{8,9},{11,10},{12,13},{15,14},{16,17},{19,... | collective-permute-start | bytes 4718600 | tf_op jit(solution)/shard_map/ppermute | solution.py:930
  615.0 54.1 %collective-permute-start.50 = (f16[512,1536]{1,0:T(8,128)(2,1)}, f16[512,1536]{1,0:T(8,128)(2,1)}, u32[]{:S(2)}, u32[]{:S(2)}) collective-permute-start(f16[512,1536]{1,0:T(8,128)(2,1)} %add_convert_fusion.7), channel_id=1, source_target_pairs={{1,2},{2,1},{5,6},{6,5},{9,10},{10,9},{13,14},{14,13},{17,18},{18,... | collective-permute-start | bytes 4718600 | tf_op jit(solution)/shard_map/ppermute | solution.py:930
  631.6 245.4 %all-reduce.9.cloned.1.call-start = ((), (), s32[]{:S(2)}) async-start(), calls=%async_computation | async-start | bytes 29884416 | tf_op jit(solution)/shard_map/psum | solution.py:1222
  700.7 52.4 %collective-permute-start.58 = (f32[2,512,256]{2,1,0:T(8,128)}, f32[2,512,256]{2,1,0:T(8,128)}, u32[]{:S(2)}, u32[]{:S(2)}) collective-permute-start(f32[2,512,256]{2,1,0:T(8,128)} %add_add_fusion.1.refs_6_), channel_id=1, source_target_pairs={{1,0},{2,3},{5,4},{6,7},{9,8},{10,11},{13,12},{14,15},{17,16},{18,... | collective-permute-start | bytes 3145736 | tf_op jit(solution)/shard_map/ppermute | solution.py:930
  706.1 56.0 %collective-permute-start.61 = (f16[512,1536]{1,0:T(8,128)(2,1)}, f16[512,1536]{1,0:T(8,128)(2,1)}, u32[]{:S(2)}, u32[]{:S(2)}) collective-permute-start(f16[512,1536]{1,0:T(8,128)(2,1)} %add_convert_fusion.1), channel_id=1, source_target_pairs={{1,2},{2,1},{5,6},{6,5},{9,10},{10,9},{13,14},{14,13},{17,18},{18,... | collective-permute-start | bytes 4718600 | tf_op jit(solution)/shard_map/ppermute | solution.py:930
  712.9 74.0 %collective-permute-start.57 = (f16[512,1536]{1,0:T(8,128)(2,1)}, f16[512,1536]{1,0:T(8,128)(2,1)}, u32[]{:S(2)}, u32[]{:S(2)}) collective-permute-start(f16[512,1536]{1,0:T(8,128)(2,1)} %add_convert_fusion.3), channel_id=1, source_target_pairs={{1,0},{2,3},{5,4},{6,7},{9,8},{10,11},{13,12},{14,15},{17,16},{18,... | collective-permute-start | bytes 4718600 | tf_op jit(solution)/shard_map/ppermute | solution.py:930
  766.3 72.9 %collective-permute-start.62 = (f16[512,1536]{1,0:T(8,128)(2,1)}, f16[512,1536]{1,0:T(8,128)(2,1)}, u32[]{:S(2)}, u32[]{:S(2)}) collective-permute-start(f16[512,1536]{1,0:T(8,128)(2,1)} %add_convert_fusion), channel_id=1, source_target_pairs={{1,0},{2,3},{5,4},{6,7},{9,8},{10,11},{13,12},{14,15},{17,16},{18,... | collective-permute-start | bytes 4718600 | tf_op jit(solution)/shard_map/ppermute | solution.py:930
  803.5 52.1 %collective-permute-start.59 = (f16[512,1536]{1,0:T(8,128)(2,1)S(1)}, f16[512,1536]{1,0:T(8,128)(2,1)}, u32[]{:S(2)}, u32[]{:S(2)}) collective-permute-start(f16[512,1536]{1,0:T(8,128)(2,1)S(1)} %add_convert_fusion.2), channel_id=1, source_target_pairs={{1,0},{2,3},{5,4},{6,7},{9,8},{10,11},{13,12},{14,15},{17,16},{18,... | collective-permute-start | bytes 4718600 | tf_op jit(solution)/shard_map/ppermute | solution.py:930
  (131 other events, 1780.6 us)
Sparse Core Ops, SparseCore 0:
  637.6 209.9 all-reduce.8

commit v2 on v1

--- a/solution.py
+++ b/solution.py
@@ -135,7 +135,7 @@
 
 class Order:
     def __init__(self):
-        self.now, self.pending, self.used = None, [], 0
+        self.now, self.pending, self.shape = None, [], (8, 2048)
 
     def before_next(self, *arrays):
         self.pending += [array for array in arrays if array.dtype != F16]
@@ -150,7 +150,7 @@
         self.now = pl.pallas_call(
             body,
             in_specs=[ANYWHERE] * len(tokens),
-            out_shape=SHAPE((8, LANES), F32),
+            out_shape=SHAPE(self.shape, F32),
             compiler_params=pltpu.CompilerParams(vmem_limit_bytes=VMEM_LIMIT),
             name="fence",
         )(*tokens)
@@ -158,9 +158,8 @@
     def tie(self, value):
         if self.now is None:
             return value
-        self.used += 1
-        at = (self.used // LANES % 8, self.used % LANES)
-        return value + lax.slice(self.now, at, (at[0] + 1, at[1] + 1)).reshape(()).astype(value.dtype)
+        zeros = lax.slice(self.now, (0, 0), (1, value.shape[-1])).astype(value.dtype)
+        return value + zeros.reshape((1,) * (value.ndim - 1) + (value.shape[-1],))
 
     def call(self, kernel, operands, *, meta, grid, in_specs, out_specs, out_shape, scratch=(), flops, moved, name, aliases=None):
         tokens = self.pending + ([] if self.now is None else [self.now])
@@ -178,10 +177,10 @@
                 num_scalar_prefetch=1,
                 grid=grid,
                 in_specs=list(in_specs) + [ANYWHERE] * len(tokens),
-                out_specs=list(out_specs) + [whole((8, LANES))],
+                out_specs=list(out_specs) + [whole(self.shape)],
                 scratch_shapes=list(scratch),
             ),
-            out_shape=list(out_shape) + [SHAPE((8, LANES), F32)],
+            out_shape=list(out_shape) + [SHAPE(self.shape, F32)],
             input_output_aliases=aliases or {},
             compiler_params=pltpu.CompilerParams(
                 vmem_limit_bytes=VMEM_LIMIT, dimension_semantics=("arbitrary",) * len(grid)
@@ -227,19 +226,26 @@
 
 
 def project_kernel(
-    meta_ref, u_ref, cot_ref, gain_ref, gate_ref, x_ref, step_ref, out_ref, normed_ref, branch_ref, proj_ref, gh_ref, *, first
+    meta_ref, u_ref, cot_ref, gain_ref, gate_ref, x_ref, step_ref, out_ref, normed_ref, branch_ref, proj_ref, gh_ref,
+    peak_ref, *, first
 ):
+    @pl.when((pl.program_id(1) == 0) & (pl.program_id(0) == 0))
+    def _():
+        peak_ref[...] = jnp.zeros_like(peak_ref)
+
     rows, channels = u_ref.shape[0], gate_ref.shape[1]
     normed = normalized(u_ref[...], gain_ref[...])
     normed_ref[...] = normed
     at = pl.program_id(1) * rows + lax.broadcasted_iota(jnp.int32, cot_ref.shape, 0)
     live = at < meta_ref[4 + first + pl.program_id(0)]
-    branch = jnp.where(live, cot_ref[...].astype(F32), 0.0).astype(BF16)
+    branch = jnp.where(live, cot_ref[...].astype(F32), 0.0)
+    peak_ref[...] = jnp.maximum(peak_ref[...], peak8(branch))
+    branch = branch.astype(BF16)
     branch_ref[...] = branch
     proj_ref[:, :channels] = mm(normed, gate_ref[...])
     proj_ref[:, channels : 2 * channels] = mm(normed, x_ref[...])
     proj_ref[:, 2 * channels :] = mm(normed, step_ref[...])
-    gh_ref[...] = mm(branch, out_ref[...])
+    gh_ref[...] = mm(branch, out_ref[...], 1, 1)
 
 
 def edge_kernel(meta_ref, before_ref, gain_ref, x_ref, pair_ref, xhalo_ref, bchalo_ref):
@@ -366,7 +372,7 @@
 
 def gate_back_kernel(
     meta_ref, mixed_ref, gate_ref, gh_ref, row_ref, bcs_ref, sc_ref, chan_ref,
-    hidden_ref, ggate_ref, dy_ref, gend_ref, acc_ref, peak_ref, grad, total,
+    hidden_ref, ggate_ref, dy_ref, gend_ref, acc_ref, grad, total,
 ):
     c, rows = pl.program_id(1), mixed_ref.shape[0]
     channels = mixed_ref.shape[1]
@@ -379,7 +385,6 @@
     @pl.when((c == 0) & (pl.program_id(0) == 0))
     def _():
         acc_ref[...] = jnp.zeros_like(acc_ref)
-        peak_ref[...] = jnp.zeros_like(peak_ref)
 
     left = left_half(CHUNK)
     for at in reversed(range(0, rows, CHUNK)):
@@ -404,9 +409,7 @@
             grad_gated = r * (gh * out_gain) - gated * pull
             dy = grad_gated * silu
             dy_ref[here, lanes] = dy
-            ggate = grad_gated * mixed * (sig * (1.0 + gate * (1.0 - sig)))
-            ggate_ref[here, lanes] = ggate.astype(BF16)
-            peak_ref[:, lanes] = jnp.maximum(peak_ref[:, lanes], jnp.maximum(peak8(ggate), peak8(dy)))
+            ggate_ref[here, lanes] = (grad_gated * mixed * (sig * (1.0 + gate * (1.0 - sig)))).astype(BF16)
             grad[:, lanes] = keep[0:1, lanes] * grad[:, lanes] + dot3(
                 ct2, halves(dy * spread_pair(grown, pair, left))
             )
@@ -420,10 +423,10 @@
 
 def state_back_kernel(
     meta_ref, x_ref, xprev_ref, xhalo_ref, bcs_ref, sc_ref, step_ref, dy_ref, mixed_ref, states_ref, final_ref,
-    gin_ref, ggate_ref, taps_ref, bias_ref, head_ref, chan_ref, expand_ref,
-    gp_ref, dbc_ref, tail_ref, first_ref, acc_ref, hacc_ref,
-    xe, ge, grad, flux, wide, wlow, dhigh, dlow, sums,
+    gin_ref, ggate_ref, taps_ref, bias_ref, head_ref, chan_ref, expand_ref, *refs
 ):
+    gp_ref, dbc_ref, tail_ref, first_ref, acc_ref, hacc_ref = refs[-15:-9]
+    xe, ge, grad, flux, wide, wlow, dhigh, dlow, sums = refs[-9:]
     c, rows = pl.program_id(1), x_ref.shape[0]
     blocks = pl.num_programs(1)
     channels = x_ref.shape[1]
@@ -651,10 +654,10 @@
         meta=meta,
         grid=(count, slots // rows),
         in_specs=[placed, placed] + [whole(a.shape) for a in (gain, gate, x, step, out)],
-        out_specs=[plain(width), plain(width), plain(wide), plain(channels)],
+        out_specs=[plain(width), plain(width), plain(wide), plain(channels), whole((8, width))],
         out_shape=[
             SHAPE((count, slots, width), BF16), SHAPE((count, slots, width), BF16),
-            SHAPE((count, slots, wide), F32), SHAPE((count, slots, channels), F32),
+            SHAPE((count, slots, wide), F32), SHAPE((count, slots, channels), F32), SHAPE((8, width), F32),
         ],
         flops=2 * count * slots * width * (wide + channels),
         moved=count * slots * (width * 8 + wide * 4),
@@ -760,12 +763,12 @@
         ],
         out_specs=[
             row(channels, 0), row(channels, 0), row(channels, 0), per_seq(STATE + 8, channels),
-            whole((8, channels)), whole((8, channels)),
+            whole((8, channels)),
         ],
         out_shape=[
             SHAPE((count, slots, channels), BF16), SHAPE((count, slots, channels), BF16),
             SHAPE((count, slots, channels), F32), SHAPE((count, STATE + 8, channels), F32),
-            SHAPE((8, channels), F32), SHAPE((8, channels), F32),
+            SHAPE((8, channels), F32),
         ],
         scratch=[pltpu.VMEM((STATE, channels), F32), pltpu.VMEM((8, LANES), F32)],
         flops=count * 4e9,
@@ -775,9 +778,10 @@
 
 
 def state_back(
-    order, meta, at, first, proj, halo_x, bcs, sc, dy, mixed, states, final, grad_in, grad_gate, taps, bias, head, chan, expand
+    order, meta, at, first, proj, halo_x, bcs, sc, dy, mixed, states, final, grad_in, grad_gate, taps, bias, head, chan, expand,
+    earlier,
 ):
-    _, slots, channels = mixed.shape
+    count, slots, channels = mixed.shape
     chunks = slots // ROWS
     tiles = ROWS // 8
     row = lambda width, column, s=at: pl.BlockSpec(
@@ -787,13 +791,14 @@
     before = pl.BlockSpec(
         (None, 8, channels), lambda _, c, meta: (at, jnp.maximum((chunks - 1 - c) * tiles - 1, 0), 1)
     )
-    tail = pl.BlockSpec((None, None, 8, channels), lambda _, c, meta: (0, chunks - 1 - c, 0, 0))
+    tail = pl.BlockSpec((None, None, 8, channels), lambda _, c, meta: (at, chunks - 1 - c, 0, 0))
+    extra = () if earlier is None else tuple(earlier)
     return order.call(
         state_back_kernel,
         (
             proj, proj, halo_x, bcs, sc, proj, dy, mixed, states, final, grad_in, grad_gate, taps, bias, head, chan,
             expand,
-        ),
+        ) + extra,
         meta=meta,
         grid=(1, chunks),
         in_specs=[
@@ -806,14 +811,14 @@
             only(STATE, channels),
             row(channels, 0),
             whole(taps.shape), whole(bias.shape), whole(head.shape), whole(chan.shape), whole(expand.shape),
-        ],
+        ] + [ANYWHERE] * len(extra),
         out_specs=[
-            row(2 * channels + LANES, 0, 0), row(2 * STATE, 0, 0), tail, only(8, channels, 0),
+            row(2 * channels + LANES, 0), row(2 * STATE, 0), tail, only(8, channels),
             whole((48, channels)), whole((16, LANES)),
         ],
         out_shape=[
-            SHAPE((1, slots, 2 * channels + LANES), BF16), SHAPE((1, slots, 2 * STATE), F32),
-            SHAPE((1, chunks, 8, channels), F32), SHAPE((1, 8, channels), F32),
+            SHAPE((count, slots, 2 * channels + LANES), BF16), SHAPE((count, slots, 2 * STATE), F32),
+            SHAPE((count, chunks, 8, channels), F32), SHAPE((count, 8, channels), F32),
             SHAPE((48, channels), F32), SHAPE((16, LANES), F32),
         ],
         scratch=[
@@ -823,6 +828,7 @@
             pltpu.VMEM((CHUNK, channels), BF16), pltpu.VMEM((CHUNK, channels), BF16),
             pltpu.VMEM((2 * CHUNK, channels), F32),
         ],
+        aliases={18 + i: i for i in range(4)} if extra else None,
         flops=12e9,
         moved=slots * channels * 24,
         name="state_back",
@@ -856,7 +862,7 @@
 
 def finish(order, meta, grad_normed, residual_in, branch, gbc, weight, gain, at, local, target):
     seqs, slots, width = residual_in.shape
-    rows = 128
+    rows = 256
     placed = pl.BlockSpec((None, rows, width), lambda s, c, meta: (meta[at], c, 0))
     fixed = lambda where, wide: pl.BlockSpec((None, rows, wide), lambda s, c, meta: (where, c, 0))
     extra = () if target is None else (target,)
@@ -909,10 +915,14 @@
             if self.ended:
                 return self
             try:
-                sent = next(self.steps)
-                self.order.before_next(*sent)
+                self.sent = next(self.steps)
+                self.order.before_next(*self.sent)
             except StopIteration as stop:
                 self.value, self.ended = stop.value, True
+        return self
+
+    def pin(self):
+        self.order.before_next(*(array[:8, :LANES].astype(F32) for array in self.sent))
         return self
 
     def end(self):
@@ -957,6 +967,14 @@
     return order.tie(value)
 
 
+def butterfly(order, value, axis, join):
+    for bit in bits_of(axis):
+        got = flipped(value, axis, bit)
+        yield (value,)
+        value = order.tie(join(value, got))
+    return value
+
+
 def bits_of(axis):
     size = lax.axis_size(axis)
     assert size & (size - 1) == 0
@@ -967,8 +985,9 @@
     return lax.ppermute(value, axis, [(i, i ^ bit) for i in range(lax.axis_size(axis))])
 
 
-def pack(state, decay):
-    return jnp.concatenate([state, jnp.broadcast_to(decay, decay.shape[:-2] + (8, decay.shape[-1]))], axis=-2)
+def joined(one, two):
+    state = lax.broadcasted_iota(I32, one.shape, 0) < STATE
+    return jnp.where(state, two[STATE : STATE + 1] * one + two, one * two)
 
 
 def carried(order, payload, axis, backward):
@@ -980,26 +999,21 @@
     got = flipped(give, axis, 1)
     yield (give,)
     is_first = odd if backward else jnp.logical_not(odd)
+    got = order.tie(got)
     one, two = jnp.where(is_first, own, got), jnp.where(is_first, got, own)
-    one_decay, two_decay = order.tie(one[STATE : STATE + 1]), order.tie(two[STATE : STATE + 1])
-    state = two_decay * one[:STATE] + two[:STATE]
-    decay = one_decay * two_decay
-    entering, through = jnp.zeros_like(state), jnp.ones_like(decay)
+    total = joined(one, two)
+    entering = jnp.broadcast_to((lax.iota(I32, total.shape[0]) >= STATE).astype(F32)[:, None], total.shape)
     for bit in steps[1:]:
         later = ((mine & bit) == 0) if backward else ((mine & bit) != 0)
         last = bit == steps[-1]
         pairs = [(i, i ^ bit) for i in range(size) if not last or bool(i & bit) == backward]
-        sent = pack(state, decay)
-        got = lax.ppermute(sent, axis, pairs)
-        yield (sent,)
-        got_state, got_decay = got[:STATE], order.tie(got[STATE : STATE + 1])
-        through = order.tie(through)
-        entering = jnp.where(later, through * got_state + entering, entering)
-        through = jnp.where(later, got_decay * through, through)
+        got = lax.ppermute(total, axis, pairs)
+        yield (total,)
+        got = order.tie(got)
+        entering = jnp.where(later, joined(got, entering), entering)
         if not last:
-            state = jnp.where(later, decay * got_state + state, got_decay * state + got_state)
-            decay = decay * got_decay
-    second = one_decay * entering + one[:STATE]
+            total = joined(jnp.where(later, got, total), jnp.where(later, total, got))
+    second = joined(entering, one)
     mine_now, other_now = jnp.where(is_first, entering, second), jnp.where(is_first, second, entering)
     back = flipped(other_now, axis, 1)
     yield (other_now,)
@@ -1012,16 +1026,8 @@
     return value
 
 
-def gathered(order, value, axis):
-    mine = lax.axis_index(axis)
-    for bit in bits_of(axis):
-        got = flipped(value, axis, bit)
-        yield (value,)
-        got = order.tie(got)
-        value = jnp.where(
-            (mine & bit) == 0, jnp.concatenate([value, got], axis=1), jnp.concatenate([got, value], axis=1)
-        )
-    return value
+def gathered(value, axis):
+    return lax.all_gather(value, axis, axis=1, tiled=True)
 
 
 def shifted(block, axis, distance):
@@ -1064,24 +1070,27 @@
     slot = lax.iota(jnp.int32, slots)[:, None]
 
     before = shifted(residual_in[:, slots - 8 :], "seq", 1)
-    pair_gather = run(gathered(order, input_state_pair_weight, "head"))
-    taps_gather = run(
-        gathered(order, jnp.pad(jnp.concatenate([bc_taps, bc_bias[None]], 0), ((0, 3), (0, 0))), "head")
-    )
+    pair_rows = gathered(
+        jnp.concatenate(
+            [input_state_pair_weight.astype(F32), bc_taps, bc_bias[None], jnp.zeros((3, own), F32)], axis=0
+        ),
+        "head",
+    )
+    pair_weight = pair_rows[:width].astype(BF16)
+    bc_taps_all, bc_bias_all = pair_rows[width : width + CONV], pair_rows[width + CONV : width + CONV + 1]
     step_weight = pad_lanes(step_size_weight, LANES)
-    out_weight_t = output_projection_weight.T
     bias = x_bias[None]
     gain_row = norm_gain[None]
 
-    normed, branch_grad, proj, bc_raw, xs, bcs, sc, grad_hidden = ([None] * GROUPS for _ in range(8))
+    normed, branch_grad, proj, bc_raw, xs, bcs, sc, grad_hidden, cot_peak = ([None] * GROUPS for _ in range(9))
     starts, partials, mixed, states, final, ends = ([None] * GROUPS for _ in range(6))
-    hidden, grad_gate, dy, grad_ins, gain_acc, gate_peak = ([None] * GROUPS for _ in range(6))
+    hidden, grad_gate, dy, grad_ins, gain_acc = ([None] * GROUPS for _ in range(5))
     branches, sums_of = {}, {}
 
     def project_of(g):
-        normed[g], branch_grad[g], proj[g], grad_hidden[g] = project(
+        normed[g], branch_grad[g], proj[g], grad_hidden[g], cot_peak[g] = project(
             order, meta, residual_in, cotangent, gain_row, gate_projection_weight, head_channels_weight, step_weight,
-            out_weight_t, g * count, count,
+            output_projection_weight, g * count, count,
         )
 
     def states_of(g):
@@ -1098,7 +1107,7 @@
         sums_of[g] = run(crossed(order, sums, "head", lambda a, b: a + b))
 
     def gate_of(g):
-        hidden[g], grad_gate[g], dy[g], grad_end, gain_acc[g], gate_peak[g] = gate_back(
+        hidden[g], grad_gate[g], dy[g], grad_end, gain_acc[g] = gate_back(
             order, meta, mixed[g], proj[g], grad_hidden[g], sums_of[g].end(), bcs[g], sc[g], chan
         )
         grad_ins[g] = run(carried(order, grad_end, "seq", True))
@@ -1116,37 +1125,36 @@
         own_rows, got = branches[s].end()
         return place(order, meta, own_rows[None], got[None], s, seqs, target)
 
-    gps, dbcs, tails, edges, accs, haccs = ({} for _ in range(6))
+    backs, gps, accs, haccs = [[] for _ in range(GROUPS)], {}, {}, {}
     parts, gbcs, baccs, gain_accs = {}, {}, [], []
     dbc_sums, fixes = {}, {}
 
-    def peaks_of():
-        largest = functools.reduce(jnp.maximum, [jnp.max(peak) for peak in gate_peak])
-        return run(crossed(order, jnp.full((8, LANES), largest, F32), "head", jnp.maximum))
+    def scale_of():
+        largest = jnp.max(functools.reduce(jnp.maximum, cot_peak))
+        return run(butterfly(order, jnp.full((8, LANES), largest, F32), "seq", jnp.maximum))
 
     def back_of(s):
         g, i = divmod(s, count)
-        gps[s], dbcs[s], tails[s], edges[s], accs[s], haccs[s] = state_back(
+        *backs[g], accs[s], haccs[s] = state_back(
             order, meta, i, g * count, proj[g], halo_x, bcs[g], sc[g], dy[g], mixed[g], states[g], final[g],
-            grad_ins[g].end(), grad_gate[g], x_taps, bias, head, chan, expand,
+            grad_ins[g].end(), grad_gate[g], x_taps, bias, head, chan, expand, backs[g] or None,
         )
 
     def edges_of(g):
-        mine = [g * count + i for i in range(count)]
-        edge = jnp.concatenate([edges[s] for s in mine])
-        fixes[g] = (shifted(edge, "seq", -1), jnp.concatenate([tails[s][:, -1] for s in mine]))
+        gps[g], _, tail, edge = backs[g]
+        fixes[g] = (shifted(edge, "seq", -1), tail[:, -1])
         order.before_next(edge)
-        dbc_sums[g] = run(line_sum(order, jnp.concatenate([dbcs[s] for s in mine]), "head", lambda total: total))
+
+    def pair_sum_of(g):
+        dbc_sums[g] = run(line_sum(order, order.tie(backs[g][1]), "head", lambda total: total))
 
     def fix_of(g):
         got, tail = fixes[g]
         fixed = order.tie(tail + edge_terms(got, x_taps)).astype(BF16)
-        for i in range(count):
-            s = g * count + i
-            gps[s] = lax.dynamic_update_slice(gps[s][0], fixed[i], (slots - 8, channels))
+        gps[g] = lax.dynamic_update_slice(gps[g], fixed, (0, slots - 8, channels))
 
     def part_of(s):
-        part = (dot("gl,ol->go", gps[s], weight) * scale[0]).astype(F16)
+        part = (dot("gl,ol->go", gps[s // count][s % count], weight) * scale[0]).astype(F16)
         parts[s] = run(line_sum(order, part, "head", lambda total: total.astype(F16)))
 
     def pair_of(g):
@@ -1174,26 +1182,27 @@
     add = lambda terms: functools.reduce(lambda a, b: a + b, terms)
     tied_dots = lambda spec, pairs: order.tie(add([dot(spec, a, b) for a, b in pairs]))
     project_of(0)
-    pair_gather.advance()
-    taps_gather.advance()
     project_of(1)
-    pair_weight = pair_gather.end()
-    bc_taps_all, bc_bias_all = taps_gather.end()[:CONV], taps_gather.end()[CONV : CONV + 1]
     halo_x, halo_bc = edge_halos(order, meta, before, gain_row, head_channels_weight, pair_weight)
     states_of(0)
+    peak = scale_of()
     order.fence()
     weight = jnp.concatenate([gate_projection_weight, head_channels_weight, order.tie(step_weight)], axis=1)
     order.before_next(weight)
     starts[0].advance()
     states_of(1)
+    peak.advance()
     starts[0].advance()
     order.fence()
     starts[1].advance()
     order.fence()
     starts[0].advance()
     starts[1].advance()
+    peak.advance()
     mix_of(0)
     starts[1].advance()
+    peak = jnp.maximum(peak.end()[0, 0], 1e-30)
+    scale = 0.0625 / peak, 16.0 * peak
     mix_of(1)
     gate_of(0)
     branch_of(0)
@@ -1210,70 +1219,82 @@
     order.fence()
     grad_ins[0].advance()
     grad_ins[1].advance()
+    branches[0].advance().pin()
     branch_of(2)
-    peak = peaks_of()
     back_of(0)
+    branches[1].advance().pin()
+    gate_grad = tied_dots("wji,wjr->ir", [(normed[g], grad_gate[g]) for g in groups])
+    order.before_next(gate_grad)
+    order.fence()
     grad_ins[1].advance()
-    branches[0].advance()
+    early = lax.psum((out_grad, order.tie(gate_grad)), "seq")
+    branch_of(3)
+    branches[3].pin()
     back_of(1)
     edges_of(0)
-    branch_of(3)
-    gate_grad = tied_dots("wji,wjr->ir", [(normed[g], grad_gate[g]) for g in groups])
-    early = lax.psum((out_grad, gate_grad, order.tie(jnp.zeros((8, LANES), F32))), "seq")
-    branches[1].advance()
     branches[0].advance()
-    back_of(2)
-    peak = jnp.maximum(peak.end()[0, 0], 1e-30)
-    scale = 0.5 / peak, 2.0 * peak
+    branches[2].advance().pin()
+    order.fence()
     fix_of(0)
     part_of(0)
-    branches[2].advance()
+    parts[0].pin()
+    back_of(2)
     branches[1].advance()
+    branches[3].advance().pin()
+    result = result_of(0, None)
+    pair_sum_of(0)
     back_of(3)
     edges_of(1)
+    part_of(1)
+    parts[1].pin()
+    order.fence()
+    parts[0].advance().pin()
+    branches[2].advance()
+    fix_of(1)
     dbc_sums[0].advance()
-    result = result_of(0, None)
+    result = result_of(1, result)
+    pair_sum_of(1)
+    part_of(2)
+    parts[2].pin()
+    order.fence()
     branches[3].advance()
-    branches[2].advance()
-    part_of(1)
+    result = result_of(2, result)
+    part_of(3)
+    parts[3].pin()
+    order.fence()
+    parts[1].advance().pin()
     dbc_sums[0].advance()
-    fix_of(1)
-    part_of(2)
-    result = result_of(1, result)
-    branches[3].advance()
+    grad_x_weight = tied_dots("wji,wjr->ir", [(normed[g], gps[g][..., channels : 2 * channels]) for g in groups])
+    grad_step_weight = tied_dots("wji,wjr->ir", [(normed[g], gps[g][..., 2 * channels :]) for g in groups])
+    order.before_next(grad_x_weight, grad_step_weight)
+    order.fence()
+    dbc_sums[1].advance()
     parts[0].advance()
+    result = result_of(3, result)
+    out_result, gate_result = order.tie(early[0]), order.tie(early[1])
+    order.before_next(out_result, gate_result)
+    zero = jnp.clip(out_result[0, 0] + gate_result[0, 0], -1.0, 1.0) * 0.0
+    late = lax.psum((grad_x_weight, grad_step_weight + zero), "seq")
+    order.fence()
+    parts[2].advance().pin()
+    order.fence()
+    parts[1].advance()
     pair_of(0)
     pair_fix(0)
-    result = result_of(2, result)
-    part_of(3)
-    order.fence()
-    grad_x_weight = tied_dots(
-        "ji,jr->ir", [(normed[s // count][s % count], gps[s][..., channels : 2 * channels]) for s in range(seqs)]
-    )
-    grad_step_weight = tied_dots(
-        "ji,jr->ir", [(normed[s // count][s % count], gps[s][..., 2 * channels :]) for s in range(seqs)]
-    )
-    order.before_next(grad_x_weight, grad_step_weight)
-    order.fence()
+    grad_input = finish_of(0, None)
+    parts[3].advance().pin()
     dbc_sums[1].advance()
-    parts[1].advance()
-    parts[0].advance()
-    result = result_of(3, result)
-    zero = order.tie(jnp.zeros((8, LANES), F32)) + jnp.clip(early[0][0, 0] + early[1][0, 0], -1.0, 1.0) * 0.0
-    late = lax.psum((grad_x_weight, grad_step_weight, zero), "seq")
+    order.fence()
     parts[2].advance()
-    parts[1].advance()
-    dbc_sums[1].advance()
-    grad_input = finish_of(0, None)
-    parts[3].advance()
-    parts[2].advance()
+    grad_input = finish_of(1, grad_input)
     pair_of(1)
     pair_fix(1)
+    parts[3].advance()
     grad_pair = add(dot("wji,wjr->ir", normed[g], gbcs[g]) for g in groups)
     grad_own = lax.dynamic_slice(grad_pair, (0, head_at * own), (width, own))
-    grad_input = finish_of(1, grad_input)
-    parts[3].advance()
     grad_input = finish_of(2, grad_input)
+    x_result, step_result = order.tie(late[0]), late[1]
+    order.before_next(x_result)
     grad_input = finish_of(3, grad_input)
     acc = jnp.sum(add(accs.values()).reshape(6, 8, channels), axis=1)
     acc = jnp.concatenate([acc, jnp.sum(add(gain_acc), axis=0)[None]], axis=0)
@@ -1291,10 +1312,10 @@
         result,
         grad_input,
         gain,
-        early[1],
-        late[0],
+        gate_result,
+        x_result,
         grad_own,
-        late[1][:, :heads],
+        step_result[:, :heads],
         acc[:CONV],
         bacc[:CONV],
         acc[CONV],
@@ -1303,7 +1324,7 @@
         hacc[1, :heads],
         jnp.sum(acc[5].reshape(heads, HEAD_DIM), axis=1),
         acc[6],
-        early[0],
+        out_result,
     )
 
 

time: 912 us -> 799 us (0.88)
  waiting for transfers between devices: 151 us -> 58 us
  other arithmetic: 178 us -> 160 us
  local copies, waits for them, and re-layouts: 84.2 us -> 68.9 us
  starting transfers between devices: 124 us -> 138 us
    ppermute x18 -> x17, waiting for transfers between devices: 52.3 us -> 6.68 us  [flipped(): lax.ppermute(value, axis, [(i, i ^ bit) for i in range(lax.axis_size(axis...]
    ppermute x30, waiting for transfers between devices: 81.7 us -> 43.9 us  [line_sum(): send = lambda value, pairs: lax.ppermute(value, axis, pairs)]
    unnamed x196 -> x213, local copies, waits for them, and re-layouts: 28.4 us -> 8.91 us
    convert_element_type x8 -> x6, other arithmetic: 33.8 us -> 18.3 us  [line_sum(): part = plus(part, got).astype(part.dtype)]
    convert_element_type x1 -> x16, other arithmetic: 1.34 us -> 14.9 us  [the longest x13 13.3 us: pin(): array[:8, :LANES].astype(F32)]
    ppermute x8, waiting for transfers between devices: 16.6 us -> 6.78 us  [carried(): got = lax.ppermute(total, axis, pairs)]
    ppermute x18 -> x17, starting transfers between devices: 9.74 us -> 18.7 us  [flipped(): lax.ppermute(value, axis, [(i, i ^ bit) for i in range(lax.axis_size(axis...]
    convert_element_type x4 -> x3, other arithmetic: 20.5 us -> 16.1 us  [branch_of(): done = lambda total: jnp.where(slot < limit[s], u.astype(F32) + total * (...]
  transfers between devices with their start and end apart: 71 -> 69, of which waited for: 16 -> 11; matrix products, arithmetic and copies ran while one was open for 37% -> 39% of each run, Pallas kernels for 25% -> 31%
where the time goes in v2:
time: 799 us; the launch traced here: 783 us
  Pallas kernels  246 us (31%)
  other arithmetic  160 us (20%)
  starting transfers between devices  138 us (17%)
  matrix products  86.1 us (11%)
  local copies, waits for them, and re-layouts  68.9 us (9%)
  waiting for transfers between devices  58 us (7%)
  between operations  25.8 us (3%)
    pallas_call x23, Pallas kernels, call(): pl.pallas_call(body, grid_spec=pltpu.PrefetchScalarGridSpec(num_scalar_pr...  235 us
    ppermute x30, starting transfers between devices, line_sum(): send = lambda value, pairs: lax.ppermute(value, axis, pairs)  88.4 us
    dot_general x18, matrix products, per_device(): dot = lambda spec, a, b: jnp.einsum(spec, a, b, preferred_element_type=F32)  86.1 us
    ppermute x30, waiting for transfers between devices, line_sum(): send = lambda value, pairs: lax.ppermute(value, axis, pairs)  43.9 us
    add x18, other arithmetic, tie(): return value + zeros.reshape((1,) * (value.ndim - 1) + (value.shape[-1],))  38.2 us
    slice x43, local copies, waits for them, and re-layouts, tie(): lax.slice(self.now, (0, 0), (1, value.shape[-1])).astype(value.dtype)  34.7 us
    ppermute x17, starting transfers between devices, flipped(): lax.ppermute(value, axis, [(i, i ^ bit) for i in range(lax.axis_size(axis...  18.7 us
    convert_element_type x6, other arithmetic, line_sum(): part = plus(part, got).astype(part.dtype)  18.3 us
  transfers between devices with their start and end apart: 69, of which 11 were waited for; matrix products, arithmetic and copies ran while one was open for 39% of the time, Pallas kernels for 31%

profile of v2, /device:TPU:0, one launch (start us, length us, event | category | flops | bytes accessed | tf_op | source)
XLA Modules:
  0.0 783.4 jit_solution(10476488314016099525)
XLA Ops:
  19.9 16.3 %project.2 = (bf16[2,512,1536]{2,1,0:T(8,128)(2,1)}, bf16[2,512,1536]{2,1,0:T(8,128)(2,1)}, f32[2,512,1664]{2,1,0:T(8,128)}, f32[2,512,768]{2,1,0:T(8,128)}, f32[8,1536]{1,0:T(8,128)}, /*index=5*/f32[8,2048]{1,0:T(8,128)}) custom-call(s32[9]{0:T(128)} %get-tuple-element.126.meta_ref, bf16[4,512,1536]{2,1,0:T(8,128)(2,1)} %refs_1_.11, ...), custom_call_target="tpu_custom_call" | custom-call | flops 7650410496 | bytes 19398656 | tf_op jit(solution)/shard_map/project/pallas_call | solution.py:174
  36.3 16.4 %project.3 = (bf16[2,512,1536]{2,1,0:T(8,128)(2,1)}, bf16[2,512,1536]{2,1,0:T(8,128)(2,1)}, f32[2,512,1664]{2,1,0:T(8,128)}, f32[2,512,768]{2,1,0:T(8,128)}, f32[8,1536]{1,0:T(8,128)}, /*index=5*/f32[8,2048]{1,0:T(8,128)}) custom-call(s32[9]{0:T(128)} %get-tuple-element.126.meta_ref, bf16[4,512,1536]{2,1,0:T(8,128)(2,1)} %refs_1_.11, ...), custom_call_target="tpu_custom_call" | custom-call | flops 7650410496 | bytes 19398656 | tf_op jit(solution)/shard_map/project/pallas_call | solution.py:174
  81.3 12.9 %local_states.2 = (f32[2,512,768]{2,1,0:T(8,128)}, f32[2,512,256]{2,1,0:T(8,128)}, f32[2,512,256]{2,1,0:T(8,128)}, f32[2,512,128]{2,1,0:T(8,128)}, f32[2,136,768]{2,1,0:T(8,128)}, /*index=5*/f32[8,2048]{1,0:T(8,128)}) custom-call(s32[9]{0:T(128)} %get-tuple-element.126.meta_ref, f32[2,512,1664]{2,1,0:T(8,128)} %get-tuple-element.134.refs_0_.refs_5_.refs_4_.refs_1_, ...), custom_call_target="tpu_custom_call" | custom-call | flops 8000000000 | bytes 6291456 | tf_op jit(solution)/shard_map/local_states/pallas_call | solution.py:174
  105.0 13.0 %local_states.3 = (f32[2,512,768]{2,1,0:T(8,128)}, f32[2,512,256]{2,1,0:T(8,128)}, f32[2,512,256]{2,1,0:T(8,128)}, f32[2,512,128]{2,1,0:T(8,128)}, f32[2,136,768]{2,1,0:T(8,128)}, /*index=5*/f32[8,2048]{1,0:T(8,128)}) custom-call(s32[9]{0:T(128)} %get-tuple-element.126.meta_ref, f32[2,512,1664]{2,1,0:T(8,128)} %get-tuple-element.128.refs_0_.refs_5_.refs_4_.refs_1_, ...), custom_call_target="tpu_custom_call" | custom-call | flops 8000000000 | bytes 6291456 | tf_op jit(solution)/shard_map/local_states/pallas_call | solution.py:174
  149.4 13.1 %mix.2 = (f32[2,512,768]{2,1,0:T(8,128)}, f32[2,8,512]{2,1,0:T(8,128)}, f32[2,4,128,768]{3,2,1,0:T(8,128)}, f32[2,128,768]{2,1,0:T(8,128)}, f32[8,2048]{1,0:T(8,128)}) custom-call(s32[9]{0:T(128)} %get-tuple-element.126.meta_ref, f32[2,512,768]{2,1,0:T(8,128)} %get-tuple-element.146.refs_0_, f32[2,512,256]{2,1,0:T(8,128)} %get-tuple-element.147.refs_1_.refs_4_.refs_3_, ...), custom_call_target="tpu_custom_call" | custom-call | flops 12000000000 | bytes 15728640 | tf_op jit(solution)/shard_map/mix/pallas_call | solution.py:174
  173.1 13.2 %mix.3 = (f32[2,512,768]{2,1,0:T(8,128)}, f32[2,8,512]{2,1,0:T(8,128)}, f32[2,4,128,768]{3,2,1,0:T(8,128)}, f32[2,128,768]{2,1,0:T(8,128)}, f32[8,2048]{1,0:T(8,128)}) custom-call(s32[9]{0:T(128)} %get-tuple-element.126.meta_ref, f32[2,512,768]{2,1,0:T(8,128)} %get-tuple-element.141.refs_0_, f32[2,512,256]{2,1,0:T(8,128)} %get-tuple-element.142.refs_1_.refs_4_.refs_3_, ...), custom_call_target="tpu_custom_call" | custom-call | flops 12000000000 | bytes 15728640 | tf_op jit(solution)/shard_map/mix/pallas_call | solution.py:174
  191.5 10.6 %gate_back.2 = (bf16[2,512,768]{2,1,0:T(8,128)(2,1)}, bf16[2,512,768]{2,1,0:T(8,128)(2,1)}, f32[2,512,768]{2,1,0:T(8,128)}, f32[2,136,768]{2,1,0:T(8,128)}, f32[8,768]{1,0:T(8,128)}, /*index=5*/f32[8,2048]{1,0:T(8,128)}) custom-call(s32[9]{0:T(128)} %get-tuple-element.126.meta_ref, f32[2,512,768]{2,1,0:T(8,128)} %get-tuple-element.156.refs_0_.refs_7_, ...), custom_call_target="tpu_custom_call" | custom-call | flops 8000000000 | bytes 15728640 | tf_op jit(solution)/shard_map/gate_back/pallas_call | solution.py:174
  229.6 10.5 %gate_back.3 = (bf16[2,512,768]{2,1,0:T(8,128)(2,1)}, bf16[2,512,768]{2,1,0:T(8,128)(2,1)}, f32[2,512,768]{2,1,0:T(8,128)}, f32[2,136,768]{2,1,0:T(8,128)}, f32[8,768]{1,0:T(8,128)}, /*index=5*/f32[8,2048]{1,0:T(8,128)}) custom-call(s32[9]{0:T(128)} %get-tuple-element.126.meta_ref, f32[2,512,768]{2,1,0:T(8,128)} %get-tuple-element.154.refs_0_.refs_7_, ...), custom_call_target="tpu_custom_call" | custom-call | flops 8000000000 | bytes 15728640 | tf_op jit(solution)/shard_map/gate_back/pallas_call | solution.py:174
  263.4 6.5 fusion.2.refs_0_
  285.1 18.8 %state_back.4 = (bf16[2,512,1664]{2,1,0:T(8,128)(2,1)}, f32[2,512,256]{2,1,0:T(8,128)}, f32[2,2,8,768]{3,2,1,0:T(8,128)}, f32[2,8,768]{2,1,0:T(8,128)}, f32[48,7...) custom-call(s32[9]{0:T(128)} %get-tuple-element.126.meta_ref, ...), custom_call_target="tpu_custom_call" | custom-call | flops 12000000000 | bytes 9437184 | tf_op jit(solution)/shard_map/state_back/pallas_call | solution.py:174
  311.1 6.0 fusion.1.refs_1_
  326.1 18.9 %state_back.5 = (bf16[2,512,1664]{2,1,0:T(8,128)(2,1)}, f32[2,512,256]{2,1,0:T(8,128)}, f32[2,2,8,768]{3,2,1,0:T(8,128)}, f32[2,8,768]{2,1,0:T(8,128)}, f32[48,7...) custom-call(s32[9]{0:T(128)} %get-tuple-element.126.meta_ref, ...), custom_call_target="tpu_custom_call", output_to_operand_aliasing={{0}: (18, {}), {1}: (19, {}), {2}: (20, {}), {3}: (21, {})} | custom-call | flops 12000000000 | bytes 9437184 | tf_op jit(solution)/shard_map/state_back/pallas_call | solution.py:174
  350.6 6.0 add_convert_fusion.9
  361.3 7.2 fusion.15
  369.8 6.9 collective-permute-start.36
  378.7 19.6 %state_back.6 = (bf16[2,512,1664]{2,1,0:T(8,128)(2,1)}, f32[2,512,256]{2,1,0:T(8,128)}, f32[2,2,8,768]{3,2,1,0:T(8,128)}, f32[2,8,768]{2,1,0:T(8,128)}, f32[48,7...) custom-call(s32[9]{0:T(128)} %get-tuple-element.126.meta_ref, ...), custom_call_target="tpu_custom_call" | custom-call | flops 12000000000 | bytes 9437184 | tf_op jit(solution)/shard_map/state_back/pallas_call | solution.py:174
  399.1 7.3 fusion.16
  433.4 19.0 %state_back.7 = (bf16[2,512,1664]{2,1,0:T(8,128)(2,1)}, f32[2,512,256]{2,1,0:T(8,128)}, f32[2,2,8,768]{3,2,1,0:T(8,128)}, f32[2,8,768]{2,1,0:T(8,128)}, f32[48,7...) custom-call(s32[9]{0:T(128)} %get-tuple-element.126.meta_ref, ...), custom_call_target="tpu_custom_call", output_to_operand_aliasing={{0}: (18, {}), {1}: (19, {}), {2}: (20, {}), {3}: (21, {})} | custom-call | flops 12000000000 | bytes 9437184 | tf_op jit(solution)/shard_map/state_back/pallas_call | solution.py:174
  457.4 6.7 collective-permute-start.38
  464.1 6.0 fusion.4
  477.1 7.3 fusion.18
  497.4 8.5 %collective-permute-start.49 = (f16[512,1536]{1,0:T(8,128)(2,1)}, f16[512,1536]{1,0:T(8,128)(2,1)}, u32[]{:S(2)}, u32[]{:S(2)}) collective-permute-start(f16[512,1536]{1,0:T(8,128)(2,1)} %fusion.17), channel_id=1, source_target_pairs={{0,1},{3,2},{4,5},{7,6},{8,9},{11,10},{12,13},{15,14},{16,17},{19,... | collective-permute-start | bytes 4718600 | tf_op jit(solution)/shard_map/ppermute | solution.py:940
  525.9 8.7 %fusion.refs_2_ = f32[1536,768]{1,0:T(8,128)} fusion(f32[1536,768,1]{1,0,2:T(8,128)} %fusion.22, bf16[2,512,1536]{2,1,0:T(8,128)(2,1)} %get-tuple-element.131.refs_2_, f32[768]{0:T(1024)S(1)} %slice_reduce_fusion.18, bf16[2,512,1664]{2,1,0:T(8,128)(2,1)} %fusion.58), kind=kOutput, calls=%fused_computation.2 | convolution fusion | flops 2418278400 | bytes 14158848 | tf_op jit(solution)/shard_map/wji,wjr->ir/dot_general | solution.py:1063
  543.5 18.1 %collective-permute-start.45 = (f16[512,1536]{1,0:T(8,128)(2,1)}, f16[512,1536]{1,0:T(8,128)(2,1)}, u32[]{:S(2)}, u32[]{:S(2)}) collective-permute-start(f16[512,1536]{1,0:T(8,128)(2,1)} %fusion.18), channel_id=1, source_target_pairs={{0,1},{3,2},{4,5},{7,6},{8,9},{11,10},{12,13},{15,14},{16,17},{19,... | collective-permute-start | bytes 4718600 | tf_op jit(solution)/shard_map/ppermute | solution.py:940
  621.6 11.9 %collective-permute-done.47 = f16[512,1536]{1,0:T(8,128)(2,1)} collective-permute-done((f16[512,1536]{1,0:T(8,128)(2,1)}, f16[512,1536]{1,0:T(8,128)(2,1)}, u32[]{:S(2)}, u32[]{:S(2)}) %collective-permute-start.47) | collective-permute-done | bytes 1572896 | tf_op jit(solution)/shard_map/ppermute | solution.py:940
  637.4 6.3 finish.4
  661.2 6.0 collective-permute-done.55
  670.8 6.1 finish.5
  677.6 12.1 %collective-permute-done.53 = f32[2,512,256]{2,1,0:T(8,128)} collective-permute-done((f32[2,512,256]{2,1,0:T(8,128)}, f32[2,512,256]{2,1,0:T(8,128)}, u32[]{:S(2)}, u32[]{:S(2)}) %collective-permute-start.53) | collective-permute-done | bytes 1048608 | tf_op jit(solution)/shard_map/ppermute | solution.py:940
  729.0 6.1 finish.6
  742.2 13.0 %collective-permute-done.56 = f16[512,1536]{1,0:T(8,128)(2,1)S(1)} collective-permute-done((f16[512,1536]{1,0:T(8,128)(2,1)}, f16[512,1536]{1,0:T(8,128)(2,1)S(1)}, u32[]{:S(2)}, u32[]{:S(2)}) %collective-permute-start.56) | collective-permute-done | bytes 1572896 | tf_op jit(solution)/shard_map/ppermute | solution.py:940
  757.4 6.2 finish.7
  (591 shorter events, 412.5 us)
Async XLA Ops:
  7.2 63.3 %all-gather.2.cloned.1.call-start = ((), (), s32[]{:S(2)}) async-start(), calls=%async_computation | async-start | bytes 2129920 | tf_op jit(solution)/shard_map/all_gather | solution.py:1030
  10.5 571.3 %all-reduce.12.cloned.1.call-start = ((), (), s32[]{:S(2)}) async-start(), calls=%async_computation.2 | async-start | bytes 18874368 | tf_op jit(solution)/shard_map/psum | solution.py:1230
  11.5 65.2 %collective-permute-start = (bf16[4,8,1536]{2,1,0:T(8,128)(2,1)S(1)}, bf16[4,8,1536]{2,1,0:T(8,128)(2,1)S(1)}, u32[]{:S(2)}, u32[]{:S(2)}) collective-permute-start(bf16[4,8,1536]{2,1,0:T(8,128)(2,1)S(1)} %slice.499), channel_id=1, source_target_pairs={{0,4},{4,8},{8,12},{12,16},{16,20},{20,24},{24,28},{1,5},{5,9},{9,... | collective-permute-start | bytes 294920 | tf_op jit(solution)/shard_map/ppermute | solution.py:1036
  54.8 65.3 %collective-permute-start.3 = (f32[8,128]{1,0:T(8,128)S(1)}, f32[8,128]{1,0:T(8,128)S(1)}, u32[]{:S(2)}, u32[]{:S(2)}) collective-permute-start(f32[8,128]{1,0:T(8,128)S(1)} %broadcast_in_dim.146.refs_1_), channel_id=1, source_target_pairs={{0,4},{4,0},{8,12},{12,8},{16,20},{20,16},{24,28},{28,24},{1,5},{5... | collective-permute-start | bytes 12296 | tf_op jit(solution)/shard_map/ppermute | solution.py:985
  187.0 40.7 %collective-permute-start.12 = (f32[2,8,512]{2,1,0:T(8,128)}, f32[2,8,512]{2,1,0:T(8,128)S(1)}, u32[]{:S(2)}, u32[]{:S(2)}) collective-permute-start(f32[2,8,512]{2,1,0:T(8,128)} %get-tuple-element.155.refs_7_), channel_id=1, source_target_pairs={{0,2},{1,3},{2,0},{3,1},{4,6},{5,7},{6,4},{7,5},{8,10},{9,11},{10,... | collective-permute-start | bytes 98312 | tf_op jit(solution)/shard_map/ppermute | solution.py:963
  212.4 64.3 %collective-permute-start.26 = (f16[512,1536]{1,0:T(8,128)(2,1)}, f16[512,1536]{1,0:T(8,128)(2,1)}, u32[]{:S(2)}, u32[]{:S(2)}) collective-permute-start(f16[512,1536]{1,0:T(8,128)(2,1)} %fusion.13), channel_id=1, source_target_pairs={{0,1},{3,2},{4,5},{7,6},{8,9},{11,10},{12,13},{15,14},{16,17},{19,... | collective-permute-start | bytes 4718600 | tf_op jit(solution)/shard_map/ppermute | solution.py:940
  225.3 80.8 %collective-permute-start.23 = (f16[512,1536]{1,0:T(8,128)(2,1)}, f16[512,1536]{1,0:T(8,128)(2,1)}, u32[]{:S(2)}, u32[]{:S(2)}) collective-permute-start(f16[512,1536]{1,0:T(8,128)(2,1)} %fusion.12), channel_id=1, source_target_pairs={{0,1},{3,2},{4,5},{7,6},{8,9},{11,10},{12,13},{15,14},{16,17},{19,... | collective-permute-start | bytes 4718600 | tf_op jit(solution)/shard_map/ppermute | solution.py:940
  246.1 167.4 %collective-permute-start.18 = (f16[512,1536]{1,0:T(8,128)(2,1)}, f16[512,1536]{1,0:T(8,128)(2,1)}, u32[]{:S(2)}, u32[]{:S(2)}) collective-permute-start(f16[512,1536]{1,0:T(8,128)(2,1)} %fusion.11), channel_id=1, source_target_pairs={{0,1},{3,2},{4,5},{7,6},{8,9},{11,10},{12,13},{15,14},{16,17},{19,... | collective-permute-start | bytes 4718600 | tf_op jit(solution)/shard_map/ppermute | solution.py:940
  272.9 77.7 %collective-permute-start.30 = (f16[512,1536]{1,0:T(8,128)(2,1)}, f16[512,1536]{1,0:T(8,128)(2,1)}, u32[]{:S(2)}, u32[]{:S(2)}) collective-permute-start(f16[512,1536]{1,0:T(8,128)(2,1)} %fusion.14), channel_id=1, source_target_pairs={{0,1},{3,2},{4,5},{7,6},{8,9},{11,10},{12,13},{15,14},{16,17},{19,... | collective-permute-start | bytes 4718600 | tf_op jit(solution)/shard_map/ppermute | solution.py:940
  277.3 46.0 %collective-permute-start.22 = (f32[136,768]{1,0:T(8,128)}, f32[136,768]{1,0:T(8,128)}, u32[]{:S(2)}, u32[]{:S(2)}) collective-permute-start(f32[136,768]{1,0:T(8,128)} %get-tuple-element.355.refs_18_), channel_id=1, source_target_pairs={{16,0},{20,4},{24,8},{28,12},{17,1},{21,5},{25,9},{29,13},{18,2},{... | collective-permute-start | bytes 1253384 | tf_op jit(solution)/shard_map/ppermute | solution.py:1010
  281.6 68.9 %collective-permute-start.29 = (f16[512,1536]{1,0:T(8,128)(2,1)S(1)}, f16[512,1536]{1,0:T(8,128)(2,1)}, u32[]{:S(2)}, u32[]{:S(2)}) collective-permute-start(f16[512,1536]{1,0:T(8,128)(2,1)S(1)} %add_convert_fusion.11), channel_id=1, source_target_pairs={{1,2},{2,1},{5,6},{6,5},{9,10},{10,9},{13,14},{14,13},{17,18},{18,... | collective-permute-start | bytes 4718600 | tf_op jit(solution)/shard_map/ppermute | solution.py:940
  309.3 107.0 %collective-permute-start.34 = (f16[512,1536]{1,0:T(8,128)(2,1)S(1)}, f16[512,1536]{1,0:T(8,128)(2,1)}, u32[]{:S(2)}, u32[]{:S(2)}) collective-permute-start(f16[512,1536]{1,0:T(8,128)(2,1)S(1)} %add_convert_fusion.10), channel_id=1, source_target_pairs={{1,2},{2,1},{5,6},{6,5},{9,10},{10,9},{13,14},{14,13},{17,18},{18,... | collective-permute-start | bytes 4718600 | tf_op jit(solution)/shard_map/ppermute | solution.py:940
  325.9 390.1 %all-reduce.10.cloned.1.call-start = ((), (), s32[]{:S(2)}) async-start(), calls=%async_computation.1 | async-start | bytes 11010048 | tf_op jit(solution)/shard_map/psum | solution.py:1277
  357.9 67.1 %collective-permute-start.33 = (bf16[512,1536]{1,0:T(8,128)(2,1)S(1)}, bf16[512,1536]{1,0:T(8,128)(2,1)}, u32[]{:S(2)}, u32[]{:S(2)}) collective-permute-start(bf16[512,1536]{1,0:T(8,128)(2,1)S(1)} %get-tuple-element.353.refs_1_), channel_id=1, source_target_pairs={{1,0},{2,3},{5,4},{6,7},{9,8},{10,11},{13,12},{14,15},{17,16},{18,... | collective-permute-start | bytes 4718600 | tf_op jit(solution)/shard_map/ppermute | solution.py:940
  369.8 86.2 %collective-permute-start.36 = (f16[512,1536]{1,0:T(8,128)(2,1)}, f16[512,1536]{1,0:T(8,128)(2,1)}, u32[]{:S(2)}, u32[]{:S(2)}) collective-permute-start(f16[512,1536]{1,0:T(8,128)(2,1)} %fusion.15), channel_id=1, source_target_pairs={{0,1},{3,2},{4,5},{7,6},{8,9},{11,10},{12,13},{15,14},{16,17},{19,... | collective-permute-start | bytes 4718600 | tf_op jit(solution)/shard_map/ppermute | solution.py:940
  376.7 80.7 %collective-permute-start.37 = (f16[512,1536]{1,0:T(8,128)(2,1)}, f16[512,1536]{1,0:T(8,128)(2,1)}, u32[]{:S(2)}, u32[]{:S(2)}) collective-permute-start(f16[512,1536]{1,0:T(8,128)(2,1)} %get-tuple-element.352), channel_id=1, source_target_pairs={{1,2},{2,1},{5,6},{6,5},{9,10},{10,9},{13,14},{14,13},{17,18},{18,... | collective-permute-start | bytes 4718600 | tf_op jit(solution)/shard_map/ppermute | solution.py:940
  413.4 121.2 %collective-permute-start.43 = (f16[512,1536]{1,0:T(8,128)(2,1)}, f16[512,1536]{1,0:T(8,128)(2,1)}, u32[]{:S(2)}, u32[]{:S(2)}) collective-permute-start(f16[512,1536]{1,0:T(8,128)(2,1)} %fusion.16), channel_id=1, source_target_pairs={{0,1},{3,2},{4,5},{7,6},{8,9},{11,10},{12,13},{15,14},{16,17},{19,... | collective-permute-start | bytes 4718600 | tf_op jit(solution)/shard_map/ppermute | solution.py:940
  421.9 90.8 %collective-permute-start.32 = (f16[512,1536]{1,0:T(8,128)(2,1)}, f16[512,1536]{1,0:T(8,128)(2,1)}, u32[]{:S(2)}, u32[]{:S(2)}) collective-permute-start(f16[512,1536]{1,0:T(8,128)(2,1)} %get-tuple-element.351), channel_id=1, source_target_pairs={{1,2},{2,1},{5,6},{6,5},{9,10},{10,9},{13,14},{14,13},{17,18},{18,... | collective-permute-start | bytes 4718600 | tf_op jit(solution)/shard_map/ppermute | solution.py:940
  425.0 72.4 %collective-permute-start.35 = (bf16[512,1536]{1,0:T(8,128)(2,1)S(1)}, bf16[512,1536]{1,0:T(8,128)(2,1)}, u32[]{:S(2)}, u32[]{:S(2)}) collective-permute-start(bf16[512,1536]{1,0:T(8,128)(2,1)S(1)} %get-tuple-element.350.refs_2_), channel_id=1, source_target_pairs={{1,0},{2,3},{5,4},{6,7},{9,8},{10,11},{13,12},{14,15},{17,16},{18,... | collective-permute-start | bytes 4718600 | tf_op jit(solution)/shard_map/ppermute | solution.py:940
  474.1 44.8 %collective-permute-start.41 = (bf16[512,1536]{1,0:T(8,128)(2,1)S(1)}, bf16[512,1536]{1,0:T(8,128)(2,1)}, u32[]{:S(2)}, u32[]{:S(2)}) collective-permute-start(bf16[512,1536]{1,0:T(8,128)(2,1)S(1)} %get-tuple-element.348.refs_4_), channel_id=1, source_target_pairs={{1,0},{2,3},{5,4},{6,7},{9,8},{10,11},{13,12},{14,15},{17,16},{18,... | collective-permute-start | bytes 4718600 | tf_op jit(solution)/shard_map/ppermute | solution.py:940
  493.2 76.8 %collective-permute-start.46 = (f16[512,1536]{1,0:T(8,128)(2,1)}, f16[512,1536]{1,0:T(8,128)(2,1)}, u32[]{:S(2)}, u32[]{:S(2)}) collective-permute-start(f16[512,1536]{1,0:T(8,128)(2,1)} %get-tuple-element.349), channel_id=1, source_target_pairs={{1,2},{2,1},{5,6},{6,5},{9,10},{10,9},{13,14},{14,13},{17,18},{18,... | collective-permute-start | bytes 4718600 | tf_op jit(solution)/shard_map/ppermute | solution.py:940
  497.4 93.7 %collective-permute-start.49 = (f16[512,1536]{1,0:T(8,128)(2,1)}, f16[512,1536]{1,0:T(8,128)(2,1)}, u32[]{:S(2)}, u32[]{:S(2)}) collective-permute-start(f16[512,1536]{1,0:T(8,128)(2,1)} %fusion.17), channel_id=1, source_target_pairs={{0,1},{3,2},{4,5},{7,6},{8,9},{11,10},{12,13},{15,14},{16,17},{19,... | collective-permute-start | bytes 4718600 | tf_op jit(solution)/shard_map/ppermute | solution.py:940
  518.9 47.6 %collective-permute-start.42 = (f32[2,512,256]{2,1,0:T(8,128)}, f32[2,512,256]{2,1,0:T(8,128)S(1)}, u32[]{:S(2)}, u32[]{:S(2)}) collective-permute-start(f32[2,512,256]{2,1,0:T(8,128)} %broadcast_add_fusion.4.refs_0_), channel_id=1, source_target_pairs={{0,1},{3,2},{4,5},{7,6},{8,9},{11,10},{12,13},{15,14},{16,17},{19,... | collective-permute-start | bytes 3145736 | tf_op jit(solution)/shard_map/ppermute | solution.py:940
  543.5 105.8 %collective-permute-start.45 = (f16[512,1536]{1,0:T(8,128)(2,1)}, f16[512,1536]{1,0:T(8,128)(2,1)}, u32[]{:S(2)}, u32[]{:S(2)}) collective-permute-start(f16[512,1536]{1,0:T(8,128)(2,1)} %fusion.18), channel_id=1, source_target_pairs={{0,1},{3,2},{4,5},{7,6},{8,9},{11,10},{12,13},{15,14},{16,17},{19,... | collective-permute-start | bytes 4718600 | tf_op jit(solution)/shard_map/ppermute | solution.py:940
  566.5 46.9 %collective-permute-start.54 = (f16[512,1536]{1,0:T(8,128)(2,1)}, f16[512,1536]{1,0:T(8,128)(2,1)}, u32[]{:S(2)}, u32[]{:S(2)}) collective-permute-start(f16[512,1536]{1,0:T(8,128)(2,1)} %copy-done.21), channel_id=1, source_target_pairs={{1,2},{2,1},{5,6},{6,5},{9,10},{10,9},{13,14},{14,13},{17,18},{18,... | collective-permute-start | bytes 4718600 | tf_op jit(solution)/shard_map/ppermute | solution.py:940
  575.2 69.3 %collective-permute-start.52 = (f32[2,512,256]{2,1,0:T(8,128)S(1)}, f32[2,512,256]{2,1,0:T(8,128)}, u32[]{:S(2)}, u32[]{:S(2)}) collective-permute-start(f32[2,512,256]{2,1,0:T(8,128)S(1)} %add_add_fusion.2.refs_3_), channel_id=1, source_target_pairs={{1,2},{2,1},{5,6},{6,5},{9,10},{10,9},{13,14},{14,13},{17,18},{18,... | collective-permute-start | bytes 3145736 | tf_op jit(solution)/shard_map/ppermute | solution.py:940
  591.1 42.4 %collective-permute-start.47 = (f16[512,1536]{1,0:T(8,128)(2,1)}, f16[512,1536]{1,0:T(8,128)(2,1)}, u32[]{:S(2)}, u32[]{:S(2)}) collective-permute-start(f16[512,1536]{1,0:T(8,128)(2,1)} %add_convert_fusion.5), channel_id=1, source_target_pairs={{1,0},{2,3},{5,4},{6,7},{9,8},{10,11},{13,12},{14,15},{17,16},{18,... | collective-permute-start | bytes 4718600 | tf_op jit(solution)/shard_map/ppermute | solution.py:940
  602.4 54.1 %collective-permute-start.57 = (f16[512,1536]{1,0:T(8,128)(2,1)}, f16[512,1536]{1,0:T(8,128)(2,1)}, u32[]{:S(2)}, u32[]{:S(2)}) collective-permute-start(f16[512,1536]{1,0:T(8,128)(2,1)} %copy-done.23), channel_id=1, source_target_pairs={{1,2},{2,1},{5,6},{6,5},{9,10},{10,9},{13,14},{14,13},{17,18},{18,... | collective-permute-start | bytes 4718600 | tf_op jit(solution)/shard_map/ppermute | solution.py:940
  618.0 49.2 %collective-permute-start.55 = (f16[512,1536]{1,0:T(8,128)(2,1)}, f16[512,1536]{1,0:T(8,128)(2,1)}, u32[]{:S(2)}, u32[]{:S(2)}) collective-permute-start(f16[512,1536]{1,0:T(8,128)(2,1)} %add_convert_fusion.2), channel_id=1, source_target_pairs={{1,0},{2,3},{5,4},{6,7},{9,8},{10,11},{13,12},{14,15},{17,16},{18,... | collective-permute-start | bytes 4718600 | tf_op jit(solution)/shard_map/ppermute | solution.py:940
  647.1 42.6 %collective-permute-start.53 = (f32[2,512,256]{2,1,0:T(8,128)}, f32[2,512,256]{2,1,0:T(8,128)}, u32[]{:S(2)}, u32[]{:S(2)}) collective-permute-start(f32[2,512,256]{2,1,0:T(8,128)} %add_add_fusion.refs_1_), channel_id=1, source_target_pairs={{1,0},{2,3},{5,4},{6,7},{9,8},{10,11},{13,12},{14,15},{17,16},{18,... | collective-permute-start | bytes 3145736 | tf_op jit(solution)/shard_map/ppermute | solution.py:940
  651.8 59.7 %collective-permute-start.51 = (f16[512,1536]{1,0:T(8,128)(2,1)S(1)}, f16[512,1536]{1,0:T(8,128)(2,1)}, u32[]{:S(2)}, u32[]{:S(2)}) collective-permute-start(f16[512,1536]{1,0:T(8,128)(2,1)S(1)} %add_convert_fusion.3), channel_id=1, source_target_pairs={{1,2},{2,1},{5,6},{6,5},{9,10},{10,9},{13,14},{14,13},{17,18},{18,... | collective-permute-start | bytes 4718600 | tf_op jit(solution)/shard_map/ppermute | solution.py:940
  659.6 65.8 %collective-permute-start.58 = (f16[512,1536]{1,0:T(8,128)(2,1)}, f16[512,1536]{1,0:T(8,128)(2,1)}, u32[]{:S(2)}, u32[]{:S(2)}) collective-permute-start(f16[512,1536]{1,0:T(8,128)(2,1)} %add_convert_fusion), channel_id=1, source_target_pairs={{1,0},{2,3},{5,4},{6,7},{9,8},{10,11},{13,12},{14,15},{17,16},{18,... | collective-permute-start | bytes 4718600 | tf_op jit(solution)/shard_map/ppermute | solution.py:940
  (141 other events, 1613.7 us)
Sparse Core Ops, SparseCore 0:
  10.7 41.9 all-gather.1
  326.0 140.8 all-reduce.11
  601.7 102.7 all-reduce.9

commit v3 on v2

--- a/solution.py
+++ b/solution.py
@@ -227,7 +227,7 @@
 
 def project_kernel(
     meta_ref, u_ref, cot_ref, gain_ref, gate_ref, x_ref, step_ref, out_ref, normed_ref, branch_ref, proj_ref, gh_ref,
-    peak_ref, *, first
+    peak_ref, input_ref, *, first
 ):
     @pl.when((pl.program_id(1) == 0) & (pl.program_id(0) == 0))
     def _():
@@ -238,6 +238,7 @@
     normed_ref[...] = normed
     at = pl.program_id(1) * rows + lax.broadcasted_iota(jnp.int32, cot_ref.shape, 0)
     live = at < meta_ref[4 + first + pl.program_id(0)]
+    input_ref[...] = jnp.where(live, u_ref[...].astype(F32), 0.0).astype(BF16)
     branch = jnp.where(live, cot_ref[...].astype(F32), 0.0)
     peak_ref[...] = jnp.maximum(peak_ref[...], peak8(branch))
     branch = branch.astype(BF16)
@@ -372,9 +373,11 @@
 
 def gate_back_kernel(
     meta_ref, mixed_ref, gate_ref, gh_ref, row_ref, bcs_ref, sc_ref, chan_ref,
-    hidden_ref, ggate_ref, dy_ref, gend_ref, acc_ref, grad, total,
+    hidden_ref, ggate_ref, dy_ref, gend_ref, acc_ref, grad, total, *, first
 ):
     c, rows = pl.program_id(1), mixed_ref.shape[0]
+    start = (pl.num_programs(1) - 1 - c) * rows
+    limit = meta_ref[4 + first + pl.program_id(0)]
     channels = mixed_ref.shape[1]
 
     @pl.when(c == 0)
@@ -393,6 +396,7 @@
         ct2 = halves(bcs_ref[here, STATE:].T)
         keep = spread(rows8(jnp.exp(cum[CHUNK - 1 : CHUNK, :])), channels)
         grown = jnp.exp(cum)
+        live = start + at + lax.broadcasted_iota(I32, (CHUNK, LANES), 0) < limit
         squares, dots = as_column(row_ref[0:1, here]), as_column(row_ref[1:2, here])
         r = lax.rsqrt(squares * (1.0 / INNER) + EPSILON)
         pull = r * r * r * dots * (1.0 / INNER)
@@ -404,7 +408,7 @@
             silu = gate * sig
             gated = mixed * silu
             normal = gated * r
-            hidden_ref[here, lanes] = (normal * out_gain).astype(BF16)
+            hidden_ref[here, lanes] = jnp.where(live, normal * out_gain, 0.0).astype(BF16)
             acc_ref[:, lanes] += fold8(gh * normal)
             grad_gated = r * (gh * out_gain) - gated * pull
             dy = grad_gated * silu
@@ -461,7 +465,7 @@
     upper = triangle(CHUNK, False)
     left = left_half(CHUNK)
     zero = jnp.zeros((CHUNK, LANES), BF16)
-    turn = lambda value: pltpu.roll(value.astype(F32), HEAD_DIM, 1).astype(BF16)
+    right_lanes = jnp.logical_not(left)
     for at in reversed(range(0, rows, CHUNK)):
         here = slice(at, at + CHUNK)
         sc = sc_ref[here, :]
@@ -485,21 +489,18 @@
             wh, wl = halves(weighted)
             dy = dy_ref[here, lanes]
             dh, dl = halves(dy)
-            turned_wh, turned_wl, turned_dh = turn(wh), turn(wl), turn(dh)
-            w_rows = (
-                jnp.concatenate([jnp.where(left, wh, turned_wl), jnp.where(left, wh, zero)], axis=1),
-                jnp.concatenate([jnp.where(left, turned_wh, wl), jnp.where(left, zero, wh)], axis=1),
-            )
-            d_rows = (
-                jnp.concatenate([jnp.where(left, dh, turned_dh), dl], axis=1),
-                jnp.concatenate([jnp.where(left, turned_dh, dh), dl], axis=1),
-            )
+            mine = [
+                (jnp.where(keep_lane, wh, zero), jnp.where(keep_lane, wl, zero)) for keep_lane in (left, right_lanes)
+            ]
+            wide_rows = jnp.concatenate([jnp.concatenate(pieces, axis=1) for pieces in mine], axis=0)
+            high_rows = jnp.concatenate([pieces[0] for pieces in mine], axis=0)
+            products = mm(wide_rows, jnp.concatenate([dh, dh], axis=1), 1, 1) + mm(high_rows, dl, 1, 1)
             stacked, columns = [], []
             for side, h in enumerate((HALF + 2 * pair, HALF + 2 * pair + 1)):
                 column = jnp.broadcast_to(sc[:, h : h + 1], (CHUNK, LANES))
                 columns.append(column)
                 kern = jnp.where(upper, jnp.exp(sc_t[h : h + 1, :] - column), 0.0)
-                dscores_t = dscores_t + kern * mm(w_rows[side], d_rows[side], 1, 1)
+                dscores_t = dscores_t + kern * products[side * CHUNK : (side + 1) * CHUNK]
                 stacked.append(jnp.concatenate(halves(kern * scores_t), axis=1))
             right = jnp.concatenate(
                 [jnp.concatenate([dh, dl], axis=1), jnp.concatenate([dh, zero], axis=1)], axis=0
@@ -654,10 +655,11 @@
         meta=meta,
         grid=(count, slots // rows),
         in_specs=[placed, placed] + [whole(a.shape) for a in (gain, gate, x, step, out)],
-        out_specs=[plain(width), plain(width), plain(wide), plain(channels), whole((8, width))],
+        out_specs=[plain(width), plain(width), plain(wide), plain(channels), whole((8, width)), plain(width)],
         out_shape=[
             SHAPE((count, slots, width), BF16), SHAPE((count, slots, width), BF16),
             SHAPE((count, slots, wide), F32), SHAPE((count, slots, channels), F32), SHAPE((8, width), F32),
+            SHAPE((count, slots, width), BF16),
         ],
         flops=2 * count * slots * width * (wide + channels),
         moved=count * slots * (width * 8 + wide * 4),
@@ -745,14 +747,14 @@
     )
 
 
-def gate_back(order, meta, mixed, proj, grad_hidden, rows, bcs, sc, chan):
+def gate_back(order, meta, first, mixed, proj, grad_hidden, rows, bcs, sc, chan):
     count, slots, channels = mixed.shape
     chunks = slots // ROWS
     row = lambda width, column: pl.BlockSpec(
         (None, ROWS, width), lambda s, c, meta: (s, chunks - 1 - c, column)
     )
     return order.call(
-        gate_back_kernel,
+        functools.partial(gate_back_kernel, first=first),
         (mixed, proj, grad_hidden, rows, bcs, sc, chan),
         meta=meta,
         grid=(count, chunks),
@@ -1066,8 +1068,6 @@
     run = lambda steps: Running(order, steps)
 
     meta, head, chan, expand = constants(lengths, step_bias, decay_log, skip_gain, out_gain, slots)
-    places, limit = meta[:seqs], meta[seqs : 2 * seqs]
-    slot = lax.iota(jnp.int32, slots)[:, None]
 
     before = shifted(residual_in[:, slots - 8 :], "seq", 1)
     pair_rows = gathered(
@@ -1082,13 +1082,13 @@
     bias = x_bias[None]
     gain_row = norm_gain[None]
 
-    normed, branch_grad, proj, bc_raw, xs, bcs, sc, grad_hidden, cot_peak = ([None] * GROUPS for _ in range(9))
+    normed, branch_grad, proj, bc_raw, xs, bcs, sc, grad_hidden, cot_peak, inputs = ([None] * GROUPS for _ in range(10))
     starts, partials, mixed, states, final, ends = ([None] * GROUPS for _ in range(6))
     hidden, grad_gate, dy, grad_ins, gain_acc = ([None] * GROUPS for _ in range(5))
     branches, sums_of = {}, {}
 
     def project_of(g):
-        normed[g], branch_grad[g], proj[g], grad_hidden[g], cot_peak[g] = project(
+        normed[g], branch_grad[g], proj[g], grad_hidden[g], cot_peak[g], inputs[g] = project(
             order, meta, residual_in, cotangent, gain_row, gate_projection_weight, head_channels_weight, step_weight,
             output_projection_weight, g * count, count,
         )
@@ -1108,17 +1108,14 @@
 
     def gate_of(g):
         hidden[g], grad_gate[g], dy[g], grad_end, gain_acc[g] = gate_back(
-            order, meta, mixed[g], proj[g], grad_hidden[g], sums_of[g].end(), bcs[g], sc[g], chan
+            order, meta, g * count, mixed[g], proj[g], grad_hidden[g], sums_of[g].end(), bcs[g], sc[g], chan
         )
         grad_ins[g] = run(carried(order, grad_end, "seq", True))
 
     def branch_of(s):
         g, i = divmod(s, count)
         branch = (dot("mq,qh->mh", hidden[g][i], output_projection_weight) * BRANCH_SCALE).astype(F16)
-        u = lax.dynamic_index_in_dim(residual_in, places[s], 0, keepdims=False)
-        done = lambda total: jnp.where(
-            slot < limit[s], u.astype(F32) + total * (1.0 / BRANCH_SCALE), 0.0
-        ).astype(BF16)
+        done = lambda total: (inputs[g][i].astype(F32) + total * (1.0 / BRANCH_SCALE)).astype(BF16)
         branches[s] = run(line_sum(order, branch, "head", done, choose=False))
 
     def result_of(s, target):
@@ -1227,10 +1224,10 @@
     order.before_next(gate_grad)
     order.fence()
     grad_ins[1].advance()
-    early = lax.psum((out_grad, order.tie(gate_grad)), "seq")
     branch_of(3)
     branches[3].pin()
     back_of(1)
+    early = lax.psum((out_grad, gate_grad), "seq")
     edges_of(0)
     branches[0].advance()
     branches[2].advance().pin()
@@ -1259,8 +1256,6 @@
     order.fence()
     branches[3].advance()
     result = result_of(2, result)
-    part_of(3)
-    parts[3].pin()
     order.fence()
     parts[1].advance().pin()
     dbc_sums[0].advance()
@@ -1269,32 +1264,37 @@
     order.before_next(grad_x_weight, grad_step_weight)
     order.fence()
     dbc_sums[1].advance()
+    part_of(3)
+    parts[3].pin()
     parts[0].advance()
     result = result_of(3, result)
-    out_result, gate_result = order.tie(early[0]), order.tie(early[1])
-    order.before_next(out_result, gate_result)
-    zero = jnp.clip(out_result[0, 0] + gate_result[0, 0], -1.0, 1.0) * 0.0
+    zero = jnp.clip(early[0][0, 0] + early[1][0, 0], -1.0, 1.0) * 0.0
     late = lax.psum((grad_x_weight, grad_step_weight + zero), "seq")
     order.fence()
     parts[2].advance().pin()
     order.fence()
-    parts[1].advance()
+    parts[3].advance().pin()
+    parts[1].advance().pin()
+    order.fence()
+    dbc_sums[1].advance()
     pair_of(0)
     pair_fix(0)
     grad_input = finish_of(0, None)
+    parts[2].advance().pin()
+    out_result, gate_result = order.tie(early[0]), order.tie(early[1])
+    order.before_next(out_result, gate_result)
+    order.fence()
+    grad_input = finish_of(1, grad_input)
     parts[3].advance().pin()
-    dbc_sums[1].advance()
-    order.fence()
-    parts[2].advance()
-    grad_input = finish_of(1, grad_input)
+    order.fence()
     pair_of(1)
     pair_fix(1)
-    parts[3].advance()
     grad_pair = add(dot("wji,wjr->ir", normed[g], gbcs[g]) for g in groups)
     grad_own = lax.dynamic_slice(grad_pair, (0, head_at * own), (width, own))
+    x_result, step_result = order.tie(late[0]), order.tie(late[1])
+    order.before_next(x_result)
+    order.fence()
     grad_input = finish_of(2, grad_input)
-    x_result, step_result = order.tie(late[0]), late[1]
-    order.before_next(x_result)
     grad_input = finish_of(3, grad_input)
     acc = jnp.sum(add(accs.values()).reshape(6, 8, channels), axis=1)
     acc = jnp.concatenate([acc, jnp.sum(add(gain_acc), axis=0)[None]], axis=0)

time: 799 us -> 794 us (level)
  starting transfers between devices: 138 us -> 128 us
  waiting for transfers between devices: 58 us -> 68 us
    ppermute x30, waiting for transfers between devices: 43.9 us -> 52 us  [line_sum(): send = lambda value, pairs: lax.ppermute(value, axis, pairs)]
    add x18 -> x17, other arithmetic: 38.2 us -> 32.7 us  [tie(): return value + zeros.reshape((1,) * (value.ndim - 1) + (value.shape[-1],))]
    slice x43 -> x40, local copies, waits for them, and re-layouts: 34.7 us -> 32.2 us  [tie(): lax.slice(self.now, (0, 0), (1, value.shape[-1])).astype(value.dtype)]
    convert_element_type x5 -> x3, other arithmetic: 17.8 us -> 15.3 us  [branch_of(): (inputs[g][i].astype(F32) + total * (1.0 / BRANCH_SCALE)).astype(BF16)]
    convert_element_type x6 -> x5, other arithmetic: 18.3 us -> 17 us  [line_sum(): part = plus(part, got).astype(part.dtype)]
where the time goes in v3:
time: 794 us; the launch traced here: 779 us
  Pallas kernels  247 us (31%)
  other arithmetic  158 us (20%)
  starting transfers between devices  128 us (16%)
  matrix products  88.5 us (11%)
  local copies, waits for them, and re-layouts  71.2 us (9%)
  waiting for transfers between devices  68 us (9%)
  between operations  17.9 us (2%)
    pallas_call x23, Pallas kernels, call(): pl.pallas_call(body, grid_spec=pltpu.PrefetchScalarGridSpec(num_scalar_pr...  233 us
    dot_general x18, matrix products, per_device(): dot = lambda spec, a, b: jnp.einsum(spec, a, b, preferred_element_type=F32)  88.5 us
    ppermute x30, starting transfers between devices, line_sum(): send = lambda value, pairs: lax.ppermute(value, axis, pairs)  81.5 us
    ppermute x30, waiting for transfers between devices, line_sum(): send = lambda value, pairs: lax.ppermute(value, axis, pairs)  52 us
    add x17, other arithmetic, tie(): return value + zeros.reshape((1,) * (value.ndim - 1) + (value.shape[-1],))  32.7 us
    slice x40, local copies, waits for them, and re-layouts, tie(): lax.slice(self.now, (0, 0), (1, value.shape[-1])).astype(value.dtype)  32.2 us
    convert_element_type x5, other arithmetic, line_sum(): part = plus(part, got).astype(part.dtype)  17 us
    ppermute x17, starting transfers between devices, flipped(): lax.ppermute(value, axis, [(i, i ^ bit) for i in range(lax.axis_size(axis...  16.4 us
  transfers between devices with their start and end apart: 69, of which 11 were waited for; matrix products, arithmetic and copies ran while one was open for 39% of the time, Pallas kernels for 31%

profile of v3, /device:TPU:0, one launch (start us, length us, event | category | flops | bytes accessed | tf_op | source)
XLA Modules:
  0.0 778.6 jit_solution(7121613797852272650)
XLA Ops:
  19.9 16.6 %project.2 = (bf16[2,512,1536]{2,1,0:T(8,128)(2,1)}, bf16[2,512,1536]{2,1,0:T(8,128)(2,1)}, f32[2,512,1664]{2,1,0:T(8,128)}, f32[2,512,768]{2,1,0:T(8,128)}, f32...) custom-call(s32[9]{0:T(128)} %get-tuple-element.128.meta_ref, bf16[4,512,1536]{2,1,0:T(8,128)(2,1)} %refs_1_.11, ...), custom_call_target="tpu_custom_call" | custom-call | flops 7650410496 | bytes 19398656 | tf_op jit(solution)/shard_map/project/pallas_call | solution.py:174
  36.5 16.7 %project.3 = (bf16[2,512,1536]{2,1,0:T(8,128)(2,1)}, bf16[2,512,1536]{2,1,0:T(8,128)(2,1)}, f32[2,512,1664]{2,1,0:T(8,128)}, f32[2,512,768]{2,1,0:T(8,128)}, f32...) custom-call(s32[9]{0:T(128)} %get-tuple-element.128.meta_ref, bf16[4,512,1536]{2,1,0:T(8,128)(2,1)} %refs_1_.11, ...), custom_call_target="tpu_custom_call" | custom-call | flops 7650410496 | bytes 19398656 | tf_op jit(solution)/shard_map/project/pallas_call | solution.py:174
  69.2 12.9 %local_states.2 = (f32[2,512,768]{2,1,0:T(8,128)}, f32[2,512,256]{2,1,0:T(8,128)}, f32[2,512,256]{2,1,0:T(8,128)}, f32[2,512,128]{2,1,0:T(8,128)}, f32[2,136,768]{2,1,0:T(8,128)}, /*index=5*/f32[8,2048]{1,0:T(8,128)}) custom-call(s32[9]{0:T(128)} %get-tuple-element.128.meta_ref, f32[2,512,1664]{2,1,0:T(8,128)} %get-tuple-element.137.refs_0_.refs_5_.refs_4_.refs_1_, ...), custom_call_target="tpu_custom_call" | custom-call | flops 8000000000 | bytes 6291456 | tf_op jit(solution)/shard_map/local_states/pallas_call | solution.py:174
  92.9 12.9 %local_states.3 = (f32[2,512,768]{2,1,0:T(8,128)}, f32[2,512,256]{2,1,0:T(8,128)}, f32[2,512,256]{2,1,0:T(8,128)}, f32[2,512,128]{2,1,0:T(8,128)}, f32[2,136,768]{2,1,0:T(8,128)}, /*index=5*/f32[8,2048]{1,0:T(8,128)}) custom-call(s32[9]{0:T(128)} %get-tuple-element.128.meta_ref, f32[2,512,1664]{2,1,0:T(8,128)} %get-tuple-element.131.refs_0_.refs_5_.refs_4_.refs_1_, ...), custom_call_target="tpu_custom_call" | custom-call | flops 8000000000 | bytes 6291456 | tf_op jit(solution)/shard_map/local_states/pallas_call | solution.py:174
  137.1 13.1 %mix.2 = (f32[2,512,768]{2,1,0:T(8,128)}, f32[2,8,512]{2,1,0:T(8,128)}, f32[2,4,128,768]{3,2,1,0:T(8,128)}, f32[2,128,768]{2,1,0:T(8,128)}, f32[8,2048]{1,0:T(8,128)}) custom-call(s32[9]{0:T(128)} %get-tuple-element.128.meta_ref, f32[2,512,768]{2,1,0:T(8,128)} %get-tuple-element.149.refs_0_, f32[2,512,256]{2,1,0:T(8,128)} %get-tuple-element.150.refs_1_.refs_4_.refs_3_, ...), custom_call_target="tpu_custom_call" | custom-call | flops 12000000000 | bytes 15728640 | tf_op jit(solution)/shard_map/mix/pallas_call | solution.py:174
  160.7 13.2 %mix.3 = (f32[2,512,768]{2,1,0:T(8,128)}, f32[2,8,512]{2,1,0:T(8,128)}, f32[2,4,128,768]{3,2,1,0:T(8,128)}, f32[2,128,768]{2,1,0:T(8,128)}, f32[8,2048]{1,0:T(8,128)}) custom-call(s32[9]{0:T(128)} %get-tuple-element.128.meta_ref, f32[2,512,768]{2,1,0:T(8,128)} %get-tuple-element.144.refs_0_, f32[2,512,256]{2,1,0:T(8,128)} %get-tuple-element.145.refs_1_.refs_4_.refs_3_, ...), custom_call_target="tpu_custom_call" | custom-call | flops 12000000000 | bytes 15728640 | tf_op jit(solution)/shard_map/mix/pallas_call | solution.py:174
  179.1 10.5 %gate_back.2 = (bf16[2,512,768]{2,1,0:T(8,128)(2,1)}, bf16[2,512,768]{2,1,0:T(8,128)(2,1)}, f32[2,512,768]{2,1,0:T(8,128)}, f32[2,136,768]{2,1,0:T(8,128)}, f32[8,768]{1,0:T(8,128)}, /*index=5*/f32[8,2048]{1,0:T(8,128)}) custom-call(s32[9]{0:T(128)} %get-tuple-element.128.meta_ref, f32[2,512,768]{2,1,0:T(8,128)} %get-tuple-element.159.refs_0_.refs_7_, ...), custom_call_target="tpu_custom_call" | custom-call | flops 8000000000 | bytes 15728640 | tf_op jit(solution)/shard_map/gate_back/pallas_call | solution.py:174
  217.3 10.6 %gate_back.3 = (bf16[2,512,768]{2,1,0:T(8,128)(2,1)}, bf16[2,512,768]{2,1,0:T(8,128)(2,1)}, f32[2,512,768]{2,1,0:T(8,128)}, f32[2,136,768]{2,1,0:T(8,128)}, f32[8,768]{1,0:T(8,128)}, /*index=5*/f32[8,2048]{1,0:T(8,128)}) custom-call(s32[9]{0:T(128)} %get-tuple-element.128.meta_ref, f32[2,512,768]{2,1,0:T(8,128)} %get-tuple-element.157.refs_0_.refs_7_, ...), custom_call_target="tpu_custom_call" | custom-call | flops 8000000000 | bytes 15728640 | tf_op jit(solution)/shard_map/gate_back/pallas_call | solution.py:174
  251.2 6.5 fusion.2.refs_0_
  274.9 18.4 %state_back.4 = (bf16[2,512,1664]{2,1,0:T(8,128)(2,1)}, f32[2,512,256]{2,1,0:T(8,128)}, f32[2,2,8,768]{3,2,1,0:T(8,128)}, f32[2,8,768]{2,1,0:T(8,128)}, f32[48,7...) custom-call(s32[9]{0:T(128)} %get-tuple-element.128.meta_ref, ...), custom_call_target="tpu_custom_call" | custom-call | flops 12000000000 | bytes 9437184 | tf_op jit(solution)/shard_map/state_back/pallas_call | solution.py:174
  299.9 6.0 fusion.1.refs_1_
  311.2 18.5 %state_back.5 = (bf16[2,512,1664]{2,1,0:T(8,128)(2,1)}, f32[2,512,256]{2,1,0:T(8,128)}, f32[2,2,8,768]{3,2,1,0:T(8,128)}, f32[2,8,768]{2,1,0:T(8,128)}, f32[48,7...) custom-call(s32[9]{0:T(128)} %get-tuple-element.128.meta_ref, ...), custom_call_target="tpu_custom_call", output_to_operand_aliasing={{0}: (18, {}), {1}: (19, {}), {2}: (20, {}), {3}: (21, {})} | custom-call | flops 12000000000 | bytes 9437184 | tf_op jit(solution)/shard_map/state_back/pallas_call | solution.py:174
  348.7 7.2 fusion.11
  357.3 6.9 collective-permute-start.36
  366.1 19.1 %state_back.6 = (bf16[2,512,1664]{2,1,0:T(8,128)(2,1)}, f32[2,512,256]{2,1,0:T(8,128)}, f32[2,2,8,768]{3,2,1,0:T(8,128)}, f32[2,8,768]{2,1,0:T(8,128)}, f32[48,7...) custom-call(s32[9]{0:T(128)} %get-tuple-element.128.meta_ref, ...), custom_call_target="tpu_custom_call" | custom-call | flops 12000000000 | bytes 9437184 | tf_op jit(solution)/shard_map/state_back/pallas_call | solution.py:174
  386.0 7.2 fusion.12
  420.7 18.5 %state_back.7 = (bf16[2,512,1664]{2,1,0:T(8,128)(2,1)}, f32[2,512,256]{2,1,0:T(8,128)}, f32[2,2,8,768]{3,2,1,0:T(8,128)}, f32[2,8,768]{2,1,0:T(8,128)}, f32[48,7...) custom-call(s32[9]{0:T(128)} %get-tuple-element.128.meta_ref, ...), custom_call_target="tpu_custom_call", output_to_operand_aliasing={{0}: (18, {}), {1}: (19, {}), {2}: (20, {}), {3}: (21, {})} | custom-call | flops 12000000000 | bytes 9437184 | tf_op jit(solution)/shard_map/state_back/pallas_call | solution.py:174
  444.0 6.7 collective-permute-start.38
  463.6 7.3 fusion.14
  483.8 8.0 %collective-permute-start.46 = (f16[512,1536]{1,0:T(8,128)(2,1)}, f16[512,1536]{1,0:T(8,128)(2,1)}, u32[]{:S(2)}, u32[]{:S(2)}) collective-permute-start(f16[512,1536]{1,0:T(8,128)(2,1)} %fusion.13), channel_id=1, source_target_pairs={{0,1},{3,2},{4,5},{7,6},{8,9},{11,10},{12,13},{15,14},{16,17},{19,... | collective-permute-start | bytes 4718600 | tf_op jit(solution)/shard_map/ppermute | solution.py:942
  511.6 8.7 %fusion.refs_2_ = f32[1536,768]{1,0:T(8,128)} fusion(f32[1536,768,1]{1,0,2:T(8,128)} %fusion.18, bf16[2,512,1536]{2,1,0:T(8,128)(2,1)} %get-tuple-element.134.refs_2_, f32[768]{0:T(1024)S(1)} %slice_reduce_fusion.16, bf16[2,512,1664]{2,1,0:T(8,128)(2,1)} %fusion.54), kind=kOutput, calls=%fused_computation.2 | convolution fusion | flops 2418278400 | bytes 14158848 | tf_op jit(solution)/shard_map/wji,wjr->ir/dot_general | solution.py:1065
  535.8 12.1 %collective-permute-start.45 = (f16[512,1536]{1,0:T(8,128)(2,1)}, f16[512,1536]{1,0:T(8,128)(2,1)}, u32[]{:S(2)}, u32[]{:S(2)}) collective-permute-start(f16[512,1536]{1,0:T(8,128)(2,1)} %fusion.14), channel_id=1, source_target_pairs={{0,1},{3,2},{4,5},{7,6},{8,9},{11,10},{12,13},{15,14},{16,17},{19,... | collective-permute-start | bytes 4718600 | tf_op jit(solution)/shard_map/ppermute | solution.py:942
  574.2 7.0 collective-permute-done.45
  609.7 7.1 collective-permute-done.52
  620.4 6.1 finish.4
  642.0 18.0 %collective-permute-done.49 = f16[512,1536]{1,0:T(8,128)(2,1)} collective-permute-done((f16[512,1536]{1,0:T(8,128)(2,1)}, f16[512,1536]{1,0:T(8,128)(2,1)}, u32[]{:S(2)}, u32[]{:S(2)}) %collective-permute-start.49) | collective-permute-done | bytes 1572896 | tf_op jit(solution)/shard_map/ppermute | solution.py:942
  663.6 6.1 finish.5
  676.4 6.0 collective-permute-done.58
  718.0 6.3 collective-permute-done.64
  731.2 6.1 finish.6
  739.8 10.1 %collective-permute-done.56 = f16[512,1536]{1,0:T(8,128)(2,1)} collective-permute-done((f16[512,1536]{1,0:T(8,128)(2,1)S(1)}, f16[512,1536]{1,0:T(8,128)(2,1)}, u32[]{:S(2)}, u32[]{:S(2)}) %collective-permute-start.56) | collective-permute-done | bytes 1572896 | tf_op jit(solution)/shard_map/ppermute | solution.py:942
  753.4 6.2 finish.7
  (574 shorter events, 424.4 us)
Async XLA Ops:
  7.2 51.3 %all-gather.2.cloned.1.call-start = ((), (), s32[]{:S(2)}) async-start(), calls=%async_computation | async-start | bytes 2129920 | tf_op jit(solution)/shard_map/all_gather | solution.py:1032
  11.4 53.2 %collective-permute-start = (bf16[4,8,1536]{2,1,0:T(8,128)(2,1)S(1)}, bf16[4,8,1536]{2,1,0:T(8,128)(2,1)S(1)}, u32[]{:S(2)}, u32[]{:S(2)}) collective-permute-start(bf16[4,8,1536]{2,1,0:T(8,128)(2,1)S(1)} %slice.487), channel_id=1, source_target_pairs={{0,4},{4,8},{8,12},{12,16},{16,20},{20,24},{24,28},{1,5},{5,9},{9,... | collective-permute-start | bytes 294920 | tf_op jit(solution)/shard_map/ppermute | solution.py:1038
  55.3 52.7 %collective-permute-start.3 = (f32[8,128]{1,0:T(8,128)S(1)}, f32[8,128]{1,0:T(8,128)S(1)}, u32[]{:S(2)}, u32[]{:S(2)}) collective-permute-start(f32[8,128]{1,0:T(8,128)S(1)} %broadcast_in_dim.114.refs_1_), channel_id=1, source_target_pairs={{0,4},{4,0},{8,12},{12,8},{16,20},{20,16},{24,28},{28,24},{1,5},{5... | collective-permute-start | bytes 12296 | tf_op jit(solution)/shard_map/ppermute | solution.py:987
  174.6 40.8 %collective-permute-start.12 = (f32[2,8,512]{2,1,0:T(8,128)}, f32[2,8,512]{2,1,0:T(8,128)S(1)}, u32[]{:S(2)}, u32[]{:S(2)}) collective-permute-start(f32[2,8,512]{2,1,0:T(8,128)} %get-tuple-element.158.refs_7_), channel_id=1, source_target_pairs={{0,2},{1,3},{2,0},{3,1},{4,6},{5,7},{6,4},{7,5},{8,10},{9,11},{10,... | collective-permute-start | bytes 98312 | tf_op jit(solution)/shard_map/ppermute | solution.py:965
  199.9 66.6 %collective-permute-start.26 = (f16[512,1536]{1,0:T(8,128)(2,1)}, f16[512,1536]{1,0:T(8,128)(2,1)}, u32[]{:S(2)}, u32[]{:S(2)}) collective-permute-start(f16[512,1536]{1,0:T(8,128)(2,1)} %fusion.9), channel_id=1, source_target_pairs={{0,1},{3,2},{4,5},{7,6},{8,9},{11,10},{12,13},{15,14},{16,17},{19,... | collective-permute-start | bytes 4718600 | tf_op jit(solution)/shard_map/ppermute | solution.py:942
  213.0 82.6 %collective-permute-start.23 = (f16[512,1536]{1,0:T(8,128)(2,1)}, f16[512,1536]{1,0:T(8,128)(2,1)}, u32[]{:S(2)}, u32[]{:S(2)}) collective-permute-start(f16[512,1536]{1,0:T(8,128)(2,1)} %fusion.8), channel_id=1, source_target_pairs={{0,1},{3,2},{4,5},{7,6},{8,9},{11,10},{12,13},{15,14},{16,17},{19,... | collective-permute-start | bytes 4718600 | tf_op jit(solution)/shard_map/ppermute | solution.py:942
  233.8 166.6 %collective-permute-start.18 = (f16[512,1536]{1,0:T(8,128)(2,1)}, f16[512,1536]{1,0:T(8,128)(2,1)}, u32[]{:S(2)}, u32[]{:S(2)}) collective-permute-start(f16[512,1536]{1,0:T(8,128)(2,1)} %fusion.7), channel_id=1, source_target_pairs={{0,1},{3,2},{4,5},{7,6},{8,9},{11,10},{12,13},{15,14},{16,17},{19,... | collective-permute-start | bytes 4718600 | tf_op jit(solution)/shard_map/ppermute | solution.py:942
  260.6 77.5 %collective-permute-start.30 = (f16[512,1536]{1,0:T(8,128)(2,1)}, f16[512,1536]{1,0:T(8,128)(2,1)}, u32[]{:S(2)}, u32[]{:S(2)}) collective-permute-start(f16[512,1536]{1,0:T(8,128)(2,1)} %fusion.10), channel_id=1, source_target_pairs={{0,1},{3,2},{4,5},{7,6},{8,9},{11,10},{12,13},{15,14},{16,17},{19,... | collective-permute-start | bytes 4718600 | tf_op jit(solution)/shard_map/ppermute | solution.py:942
  267.1 41.5 %collective-permute-start.22 = (f32[136,768]{1,0:T(8,128)}, f32[136,768]{1,0:T(8,128)}, u32[]{:S(2)}, u32[]{:S(2)}) collective-permute-start(f32[136,768]{1,0:T(8,128)} %get-tuple-element.361.refs_18_), channel_id=1, source_target_pairs={{16,0},{20,4},{24,8},{28,12},{17,1},{21,5},{25,9},{29,13},{18,2},{... | collective-permute-start | bytes 1253384 | tf_op jit(solution)/shard_map/ppermute | solution.py:1012
  271.5 66.6 %collective-permute-start.29 = (f16[512,1536]{1,0:T(8,128)(2,1)S(1)}, f16[512,1536]{1,0:T(8,128)(2,1)}, u32[]{:S(2)}, u32[]{:S(2)}) collective-permute-start(f16[512,1536]{1,0:T(8,128)(2,1)S(1)} %add_convert_fusion.11), channel_id=1, source_target_pairs={{1,2},{2,1},{5,6},{6,5},{9,10},{10,9},{13,14},{14,13},{17,18},{18,... | collective-permute-start | bytes 4718600 | tf_op jit(solution)/shard_map/ppermute | solution.py:942
  298.0 106.1 %collective-permute-start.34 = (f16[512,1536]{1,0:T(8,128)(2,1)S(1)}, f16[512,1536]{1,0:T(8,128)(2,1)}, u32[]{:S(2)}, u32[]{:S(2)}) collective-permute-start(f16[512,1536]{1,0:T(8,128)(2,1)S(1)} %add_convert_fusion.10), channel_id=1, source_target_pairs={{1,2},{2,1},{5,6},{6,5},{9,10},{10,9},{13,14},{14,13},{17,18},{18,... | collective-permute-start | bytes 4718600 | tf_op jit(solution)/shard_map/ppermute | solution.py:942
  307.1 220.9 %all-reduce.12.cloned.1.call-start = ((), (), s32[]{:S(2)}) async-start(), calls=%async_computation.2 | async-start | bytes 18874368 | tf_op jit(solution)/shard_map/psum | solution.py:1230
  345.4 67.0 %collective-permute-start.33 = (bf16[512,1536]{1,0:T(8,128)(2,1)S(1)}, bf16[512,1536]{1,0:T(8,128)(2,1)}, u32[]{:S(2)}, u32[]{:S(2)}) collective-permute-start(bf16[512,1536]{1,0:T(8,128)(2,1)S(1)} %get-tuple-element.359.refs_1_), channel_id=1, source_target_pairs={{1,0},{2,3},{5,4},{6,7},{9,8},{10,11},{13,12},{14,15},{17,16},{18,... | collective-permute-start | bytes 4718600 | tf_op jit(solution)/shard_map/ppermute | solution.py:942
  357.3 85.4 %collective-permute-start.36 = (f16[512,1536]{1,0:T(8,128)(2,1)}, f16[512,1536]{1,0:T(8,128)(2,1)}, u32[]{:S(2)}, u32[]{:S(2)}) collective-permute-start(f16[512,1536]{1,0:T(8,128)(2,1)} %fusion.11), channel_id=1, source_target_pairs={{0,1},{3,2},{4,5},{7,6},{8,9},{11,10},{12,13},{15,14},{16,17},{19,... | collective-permute-start | bytes 4718600 | tf_op jit(solution)/shard_map/ppermute | solution.py:942
  364.2 79.8 %collective-permute-start.37 = (f16[512,1536]{1,0:T(8,128)(2,1)}, f16[512,1536]{1,0:T(8,128)(2,1)}, u32[]{:S(2)}, u32[]{:S(2)}) collective-permute-start(f16[512,1536]{1,0:T(8,128)(2,1)} %get-tuple-element.358), channel_id=1, source_target_pairs={{1,2},{2,1},{5,6},{6,5},{9,10},{10,9},{13,14},{14,13},{17,18},{18,... | collective-permute-start | bytes 4718600 | tf_op jit(solution)/shard_map/ppermute | solution.py:942
  400.4 119.9 %collective-permute-start.43 = (f16[512,1536]{1,0:T(8,128)(2,1)}, f16[512,1536]{1,0:T(8,128)(2,1)}, u32[]{:S(2)}, u32[]{:S(2)}) collective-permute-start(f16[512,1536]{1,0:T(8,128)(2,1)} %fusion.12), channel_id=1, source_target_pairs={{0,1},{3,2},{4,5},{7,6},{8,9},{11,10},{12,13},{15,14},{16,17},{19,... | collective-permute-start | bytes 4718600 | tf_op jit(solution)/shard_map/ppermute | solution.py:942
  409.3 89.2 %collective-permute-start.32 = (f16[512,1536]{1,0:T(8,128)(2,1)}, f16[512,1536]{1,0:T(8,128)(2,1)}, u32[]{:S(2)}, u32[]{:S(2)}) collective-permute-start(f16[512,1536]{1,0:T(8,128)(2,1)} %get-tuple-element.357), channel_id=1, source_target_pairs={{1,2},{2,1},{5,6},{6,5},{9,10},{10,9},{13,14},{14,13},{17,18},{18,... | collective-permute-start | bytes 4718600 | tf_op jit(solution)/shard_map/ppermute | solution.py:942
  412.4 71.4 %collective-permute-start.35 = (bf16[512,1536]{1,0:T(8,128)(2,1)S(1)}, bf16[512,1536]{1,0:T(8,128)(2,1)}, u32[]{:S(2)}, u32[]{:S(2)}) collective-permute-start(bf16[512,1536]{1,0:T(8,128)(2,1)S(1)} %get-tuple-element.356.refs_2_), channel_id=1, source_target_pairs={{1,0},{2,3},{5,4},{6,7},{9,8},{10,11},{13,12},{14,15},{17,16},{18,... | collective-permute-start | bytes 4718600 | tf_op jit(solution)/shard_map/ppermute | solution.py:942
  460.6 43.9 %collective-permute-start.41 = (bf16[512,1536]{1,0:T(8,128)(2,1)S(1)}, bf16[512,1536]{1,0:T(8,128)(2,1)}, u32[]{:S(2)}, u32[]{:S(2)}) collective-permute-start(bf16[512,1536]{1,0:T(8,128)(2,1)S(1)} %get-tuple-element.354.refs_4_), channel_id=1, source_target_pairs={{1,0},{2,3},{5,4},{6,7},{9,8},{10,11},{13,12},{14,15},{17,16},{18,... | collective-permute-start | bytes 4718600 | tf_op jit(solution)/shard_map/ppermute | solution.py:942
  479.5 76.7 %collective-permute-start.51 = (f16[512,1536]{1,0:T(8,128)(2,1)}, f16[512,1536]{1,0:T(8,128)(2,1)}, u32[]{:S(2)}, u32[]{:S(2)}) collective-permute-start(f16[512,1536]{1,0:T(8,128)(2,1)} %get-tuple-element.355), channel_id=1, source_target_pairs={{1,2},{2,1},{5,6},{6,5},{9,10},{10,9},{13,14},{14,13},{17,18},{18,... | collective-permute-start | bytes 4718600 | tf_op jit(solution)/shard_map/ppermute | solution.py:942
  483.8 83.3 %collective-permute-start.46 = (f16[512,1536]{1,0:T(8,128)(2,1)}, f16[512,1536]{1,0:T(8,128)(2,1)}, u32[]{:S(2)}, u32[]{:S(2)}) collective-permute-start(f16[512,1536]{1,0:T(8,128)(2,1)} %fusion.13), channel_id=1, source_target_pairs={{0,1},{3,2},{4,5},{7,6},{8,9},{11,10},{12,13},{15,14},{16,17},{19,... | collective-permute-start | bytes 4718600 | tf_op jit(solution)/shard_map/ppermute | solution.py:942
  504.5 48.3 %collective-permute-start.42 = (f32[2,512,256]{2,1,0:T(8,128)}, f32[2,512,256]{2,1,0:T(8,128)S(1)}, u32[]{:S(2)}, u32[]{:S(2)}) collective-permute-start(f32[2,512,256]{2,1,0:T(8,128)} %broadcast_add_fusion.3.refs_0_), channel_id=1, source_target_pairs={{0,1},{3,2},{4,5},{7,6},{8,9},{11,10},{12,13},{15,14},{16,17},{19,... | collective-permute-start | bytes 3145736 | tf_op jit(solution)/shard_map/ppermute | solution.py:942
  520.3 40.8 %collective-permute-start.40 = (bf16[512,1536]{1,0:T(8,128)(2,1)S(1)}, bf16[512,1536]{1,0:T(8,128)(2,1)}, u32[]{:S(2)}, u32[]{:S(2)}) collective-permute-start(bf16[512,1536]{1,0:T(8,128)(2,1)S(1)} %copy-done.3), channel_id=1, source_target_pairs={{1,0},{2,3},{5,4},{6,7},{9,8},{10,11},{13,12},{14,15},{17,16},{18,... | collective-permute-start | bytes 4718600 | tf_op jit(solution)/shard_map/ppermute | solution.py:942
  535.8 45.3 %collective-permute-start.45 = (f16[512,1536]{1,0:T(8,128)(2,1)}, f16[512,1536]{1,0:T(8,128)(2,1)}, u32[]{:S(2)}, u32[]{:S(2)}) collective-permute-start(f16[512,1536]{1,0:T(8,128)(2,1)} %fusion.14), channel_id=1, source_target_pairs={{0,1},{3,2},{4,5},{7,6},{8,9},{11,10},{12,13},{15,14},{16,17},{19,... | collective-permute-start | bytes 4718600 | tf_op jit(solution)/shard_map/ppermute | solution.py:942
  551.2 154.3 %all-reduce.10.cloned.1.call-start = ((), (), s32[]{:S(2)}) async-start(), calls=%async_computation.1 | async-start | bytes 11010048 | tf_op jit(solution)/shard_map/psum | solution.py:1272
  567.1 49.7 %collective-permute-start.52 = (f16[512,1536]{1,0:T(8,128)(2,1)}, f16[512,1536]{1,0:T(8,128)(2,1)}, u32[]{:S(2)}, u32[]{:S(2)}) collective-permute-start(f16[512,1536]{1,0:T(8,128)(2,1)} %add_convert_fusion.2), channel_id=1, source_target_pairs={{1,0},{2,3},{5,4},{6,7},{9,8},{10,11},{13,12},{14,15},{17,16},{18,... | collective-permute-start | bytes 4718600 | tf_op jit(solution)/shard_map/ppermute | solution.py:942
  581.1 55.5 %collective-permute-start.50 = (f16[512,1536]{1,0:T(8,128)(2,1)}, f16[512,1536]{1,0:T(8,128)(2,1)}, u32[]{:S(2)}, u32[]{:S(2)}) collective-permute-start(f16[512,1536]{1,0:T(8,128)(2,1)} %copy-done.22), channel_id=1, source_target_pairs={{1,2},{2,1},{5,6},{6,5},{9,10},{10,9},{13,14},{14,13},{17,18},{18,... | collective-permute-start | bytes 4718600 | tf_op jit(solution)/shard_map/ppermute | solution.py:942
  600.8 59.2 %collective-permute-start.49 = (f16[512,1536]{1,0:T(8,128)(2,1)}, f16[512,1536]{1,0:T(8,128)(2,1)}, u32[]{:S(2)}, u32[]{:S(2)}) collective-permute-start(f16[512,1536]{1,0:T(8,128)(2,1)} %copy-done.25), channel_id=1, source_target_pairs={{1,0},{2,3},{5,4},{6,7},{9,8},{10,11},{13,12},{14,15},{17,16},{18,... | collective-permute-start | bytes 4718600 | tf_op jit(solution)/shard_map/ppermute | solution.py:942
  602.1 68.4 %collective-permute-start.47 = (f16[512,1536]{1,0:T(8,128)(2,1)}, f16[512,1536]{1,0:T(8,128)(2,1)}, u32[]{:S(2)}, u32[]{:S(2)}) collective-permute-start(f16[512,1536]{1,0:T(8,128)(2,1)} %copy-done.24), channel_id=1, source_target_pairs={{1,2},{2,1},{5,6},{6,5},{9,10},{10,9},{13,14},{14,13},{17,18},{18,... | collective-permute-start | bytes 4718600 | tf_op jit(solution)/shard_map/ppermute | solution.py:942
  603.9 78.6 %collective-permute-start.58 = (f32[2,512,256]{2,1,0:T(8,128)}, f32[2,512,256]{2,1,0:T(8,128)}, u32[]{:S(2)}, u32[]{:S(2)}) collective-permute-start(f32[2,512,256]{2,1,0:T(8,128)} %get-tuple-element.364.refs_5_), channel_id=1, source_target_pairs={{1,0},{2,3},{5,4},{6,7},{9,8},{10,11},{13,12},{14,15},{17,16},{18,... | collective-permute-start | bytes 3145736 | tf_op jit(solution)/shard_map/ppermute | solution.py:942
  638.7 89.0 %collective-permute-start.57 = (f16[512,1536]{1,0:T(8,128)(2,1)S(1)}, f16[512,1536]{1,0:T(8,128)(2,1)}, u32[]{:S(2)}, u32[]{:S(2)}) collective-permute-start(f16[512,1536]{1,0:T(8,128)(2,1)S(1)} %add_convert_fusion.1), channel_id=1, source_target_pairs={{1,0},{2,3},{5,4},{6,7},{9,8},{10,11},{13,12},{14,15},{17,16},{18,... | collective-permute-start | bytes 4718600 | tf_op jit(solution)/shard_map/ppermute | solution.py:942
  672.9 76.9 %collective-permute-start.56 = (f16[512,1536]{1,0:T(8,128)(2,1)S(1)}, f16[512,1536]{1,0:T(8,128)(2,1)}, u32[]{:S(2)}, u32[]{:S(2)}) collective-permute-start(f16[512,1536]{1,0:T(8,128)(2,1)S(1)} %add_convert_fusion), channel_id=1, source_target_pairs={{1,0},{2,3},{5,4},{6,7},{9,8},{10,11},{13,12},{14,15},{17,16},{18,... | collective-permute-start | bytes 4718600 | tf_op jit(solution)/shard_map/ppermute | solution.py:942
  (135 other events, 1433.2 us)
Sparse Core Ops, SparseCore 0:
  10.7 41.9 all-gather.1
  312.2 141.7 all-reduce.11
  555.8 95.5 all-reduce.9
